TPU v7x, 32 devices: a whole 2x2x4 slice. The times are simulated.
32 devices in a mesh: gx: 4 (over z), gy: 8 (over y, x, core).
Axes of the slice: x: 2, y: 2, z: 4, core: 2. Of those that a mesh axis runs over, the one named last changes fastest.
Arguments:
- block_input: bfloat16 [4096, 2048], P('gx', 'gy'), may hold values from -6 to 6
- out_grad: bfloat16 [4096, 2048], P('gx', 'gy'), may hold values from -6 to 6
- routes: int32 [4096, 8], P('gx'), may hold values from 0 to 31, all different within a row; in each aligned block of 1024 rows (0 to 1023, 1024 to 2047, ...) at most 288 rows name the same one
- adapter_ids: int32 [4], P('gx'), may hold values from 0 to 7
- piece_starts: int32 [4, 2], P('gx'), may hold values from 0 to 768, as said below
- attn_gain: float32 [2048], replicated, may hold values from 0.1 to 1.9
- qk_gain: float32 [2, 2048], replicated, may hold values from 0.1 to 1.9
- mlp_gain: float32 [2048], replicated, may hold values from 0.1 to 1.9
- w_qkv: bfloat16 [2048, 16, 3, 128], P('gx', 'gy'), may hold values from -0.125 to 0.125
- w_out: bfloat16 [16, 128, 2048], P('gy', None, 'gx'), may hold values from -3 to 3
- a_qkv: bfloat16 [3, 2048, 128], P(None, 'gy'), may hold values from -0.125 to 0.125
- b_out: bfloat16 [128, 2048], P(None, 'gy'), may hold values from -1 to 1
- head_pack: bfloat16 [16, 4, 128, 128], P('gy'), may hold values from -1.5 to 1.5
- router: bfloat16 [2048, 32], replicated, may hold values from -0.0625 to 0.0625
- w_gate_up: bfloat16 [32, 2048, 2, 1024], P('gy', 'gx'), may hold values from -0.125 to 0.125
- w_down: bfloat16 [32, 2048, 1024], P('gy', 'gx'), may hold values from -1.5 to 1.5
- exp_wide: bfloat16 [32, 2048, 3, 128], P('gy', 'gx'), may hold values from -0.125 to 0.125
- exp_hidden: bfloat16 [32, 1024, 3, 128], P('gy', 'gx'), may hold values from -1.5 to 1.5
Outputs:
- layer_out: bfloat16 [4096, 2048], P('gx', 'gy')
- input_grad: float32 [4096, 2048], P('gx', 'gy')
- a_qkv_grad: float32 [3, 2048, 128], P(None, 'gy')
- b_out_grad: float32 [128, 2048], P(None, 'gy')
- head_pack_grad: float32 [16, 4, 128, 128], P('gy')
- exp_wide_grad: float32 [32, 2048, 3, 128], P('gy', 'gx')
- exp_hidden_grad: float32 [32, 1024, 3, 128], P('gy', 'gx')
Inputs may be any that keep to these rules, and one draw needn't show every extreme that they name: `routes`: in each aligned block of the rows that one index of gx holds, no expert is named by more than 288 rows, a bound that some block reaches. `piece_starts`: each sequence has two pieces of 256 positions; the first starts in the first half of the sequence and ends in it, the second lies in the second half.
All inputs are finite; a program needn't handle non-finite values.
Results may differ from a plain program's by a relative error of at most 0.02.
Values may be sent and summed in bfloat16 or wider, within the bound.
A program may use at most 320 MiB of HBM per device.

v0:
```python
import jax
import jax.numpy as jnp
from jax import lax
from jax.sharding import PartitionSpec as P

RANK = 16
SEQ = 1024
PIECE = 256
CAP = 288


norm_eps = 1e-05
rope_theta = 10000.0
rank_scale = 0.5
down_scale = 4.0
highest = lax.Precision.HIGHEST


def rope_tables(length, width):
    half_width = width // 2
    frequency = rope_theta ** (-2.0 * jnp.arange(half_width, dtype=jnp.float32) / width)
    angles = jnp.arange(length, dtype=jnp.float32)[:, None] * frequency[None, :]
    return (jnp.cos(angles), jnp.sin(angles))


def apply_rotary(values, cosine, sine):
    half_width = values.shape[-1] // 2
    first = values[..., :half_width]
    second = values[..., half_width:]
    return jnp.concatenate(
        [first * cosine - second * sine, second * cosine + first * sine], axis=-1
    )


def unrotate(grads, cosine, sine):
    half_width = grads.shape[-1] // 2
    first = grads[..., :half_width]
    second = grads[..., half_width:]
    return jnp.concatenate(
        [first * cosine + second * sine, second * cosine - first * sine], axis=-1
    )


def allowed_mask(piece_starts):
    places = jnp.arange(SEQ, dtype=jnp.int32)
    causal = places[None, :] <= places[:, None]
    inside = (places[None, None, :] >= piece_starts[:, :, None]) & (
        places[None, None, :] < piece_starts[:, :, None] + PIECE
    )
    same_piece = jnp.any(inside[:, :, :, None] & inside[:, :, None, :], axis=1)
    return causal[None] | same_piece


def fetch_experts(w_gate_up, w_down, exp_wide, exp_hidden):
    return (
        lax.all_gather(w_gate_up, "gx", axis=1, tiled=True),
        lax.all_gather(w_down, "gx", axis=1, tiled=True),
        lax.all_gather(exp_wide, "gx", axis=1, tiled=True),
        lax.all_gather(exp_hidden, "gx", axis=1, tiled=True),
    )


def shards(
    block_input,
    out_grad,
    routes,
    adapter_ids,
    piece_starts,
    attn_gain,
    qk_gain,
    mlp_gain,
    w_qkv,
    w_out,
    a_qkv,
    b_out,
    head_pack,
    router,
    w_gate_up,
    w_down,
    exp_wide,
    exp_hidden,
):
    groups = lax.axis_size("gy")
    column = lax.axis_index("gy")
    rows = block_input.shape[0]
    width_local = block_input.shape[1]
    width = width_local * groups
    heads_local = head_pack.shape[0]
    rank_cols = head_pack.shape[2]
    head_width = head_pack.shape[3]
    experts_local = w_gate_up.shape[0]
    nseq = adapter_ids.shape[0]
    inv_root = head_width ** (-0.5)
    full_rows, a_full, b_full = (
        lax.all_gather(block_input, "gy", axis=1, tiled=True),
        lax.all_gather(a_qkv, "gy", axis=1, tiled=True),
        lax.all_gather(b_out, "gy", axis=1, tiled=True),
    )
    qkv_weight, out_weight = (
        lax.all_gather(w_qkv, "gx", axis=0, tiled=True),
        lax.all_gather(w_out, "gx", axis=2, tiled=True),
    )
    token_adapter = jnp.repeat(adapter_ids, SEQ, total_repeat_length=rows)
    rank_mask = (
        token_adapter[:, None] == jnp.arange(rank_cols, dtype=jnp.int32)[None, :] // RANK
    ).astype(jnp.float32)
    col_start = column * width_local
    first_norm_gain = lax.dynamic_slice_in_dim(attn_gain, col_start, width_local)
    input_f = full_rows.astype(jnp.float32)
    scale_one = lax.rsqrt(jnp.mean(input_f * input_f, axis=-1, keepdims=True) + norm_eps)
    hat_one = input_f * scale_one
    normed_bf = (hat_one * attn_gain).astype(jnp.bfloat16)
    base = jnp.einsum("td,dhce->thce", normed_bf, qkv_weight, preferred_element_type=jnp.float32)
    rank_in = jnp.einsum("td,cdr->tcr", normed_bf, a_full, preferred_element_type=jnp.float32)
    rank_low = (rank_in * rank_mask[:, None, :]).astype(jnp.bfloat16)
    projected = base + rank_scale * jnp.einsum(
        "tcr,hcre->thce", rank_low, head_pack[:, :3], preferred_element_type=jnp.float32
    )
    query_pre = projected[:, :, 0]
    key_pre = projected[:, :, 1]
    value_bf = projected[:, :, 2].astype(jnp.bfloat16)
    square_sums = lax.psum(
        (jnp.sum(query_pre * query_pre, axis=(1, 2)), jnp.sum(key_pre * key_pre, axis=(1, 2))), "gy"
    )
    query_scale = lax.rsqrt(square_sums[0] / width + norm_eps)[:, None, None]
    key_scale = lax.rsqrt(square_sums[1] / width + norm_eps)[:, None, None]
    head_start = column * heads_local * head_width
    gains_local = lax.dynamic_slice_in_dim(
        qk_gain, head_start, heads_local * head_width, axis=1
    ).reshape(2, heads_local, head_width)
    query_hat = query_pre * query_scale
    key_hat = key_pre * key_scale
    cosine, sine = rope_tables(SEQ, head_width)
    cosine = cosine[None, :, None, :]
    sine = sine[None, :, None, :]
    query_bf = apply_rotary(
        (query_hat * gains_local[0]).reshape(nseq, SEQ, heads_local, head_width), cosine, sine
    ).astype(jnp.bfloat16)
    key_bf = apply_rotary(
        (key_hat * gains_local[1]).reshape(nseq, SEQ, heads_local, head_width), cosine, sine
    ).astype(jnp.bfloat16)
    values_seq = value_bf.reshape(nseq, SEQ, heads_local, head_width)
    allowed = allowed_mask(piece_starts)[:, None]
    scores = (
        jnp.einsum("nqhe,nkhe->nhqk", query_bf, key_bf, preferred_element_type=jnp.float32)
        * inv_root
    )
    scores = jnp.where(allowed, scores, -1e30)
    row_peak = jnp.max(scores, axis=-1, keepdims=True)
    raised = jnp.exp(scores - row_peak)
    row_total = jnp.sum(raised, axis=-1, keepdims=True)
    log_total = row_peak + jnp.log(row_total)
    weights = raised / row_total
    attended = jnp.einsum(
        "nhqk,nkhe->nqhe",
        weights.astype(jnp.bfloat16),
        values_seq,
        preferred_element_type=jnp.float32,
    )
    attn_bf = attended.reshape(rows, heads_local, head_width).astype(jnp.bfloat16)
    rank_out = jnp.einsum(
        "the,hre->thr", attn_bf, head_pack[:, 3], preferred_element_type=jnp.float32
    )
    rank_out_low = (rank_out * rank_mask[:, None, :]).astype(jnp.bfloat16)
    out_terms = jnp.einsum(
        "the,hed->td", attn_bf, out_weight, preferred_element_type=jnp.float32
    ) + rank_scale * jnp.einsum(
        "thr,rd->td", rank_out_low, b_full, preferred_element_type=jnp.float32
    )
    branch = lax.psum_scatter(out_terms, "gy", scatter_dimension=1, tiled=True)
    middle = block_input.astype(jnp.float32) + branch
    middle_rows = lax.all_gather(middle.astype(jnp.bfloat16), "gy", axis=1, tiled=True)
    middle_f = middle_rows.astype(jnp.float32)
    scale_two = lax.rsqrt(jnp.mean(middle_f * middle_f, axis=-1, keepdims=True) + norm_eps)
    hat_two = middle_f * scale_two
    expert_in = (hat_two * mlp_gain).astype(jnp.bfloat16)
    logits = jnp.dot(expert_in, router, preferred_element_type=jnp.float32)
    logit_peak = jnp.max(logits, axis=-1, keepdims=True)
    logit_raised = jnp.exp(logits - logit_peak)
    route_probs = logit_raised / jnp.sum(logit_raised, axis=-1, keepdims=True)
    first_expert = column * experts_local
    expert_ids = first_expert + jnp.arange(experts_local, dtype=jnp.int32)
    hits = jnp.any(routes[:, :, None] == expert_ids[None, None, :], axis=1)
    hit_int = hits.astype(jnp.int32)
    places = jnp.cumsum(hit_int, axis=0) - 1
    slot_at = jnp.where(hits, places, CAP)
    token_ids = jnp.broadcast_to(jnp.arange(rows, dtype=jnp.int32)[:, None], (rows, experts_local))
    slot_rows = (
        jnp.zeros((experts_local, CAP), jnp.int32)
        .at[jnp.arange(experts_local, dtype=jnp.int32)[None, :], slot_at]
        .set(token_ids, mode="drop")
    )
    valid = (jnp.arange(CAP, dtype=jnp.int32)[None, :] < jnp.sum(hit_int, axis=0)[:, None]).astype(
        jnp.float32
    )
    probs_local = lax.dynamic_slice_in_dim(route_probs, first_expert, experts_local, axis=1)
    gate_slot = jnp.take_along_axis(probs_local.T, slot_rows, axis=1) * valid
    mask_slot = rank_mask[slot_rows]
    expert_rows = expert_in[slot_rows]
    slot_flat = slot_rows.reshape(-1)
    gate_up_w, down_w, wide_w, hidden_w = fetch_experts(w_gate_up, w_down, exp_wide, exp_hidden)
    pre_gu = jnp.einsum(
        "esd,edcf->escf", expert_rows, gate_up_w, preferred_element_type=jnp.float32
    )
    rank_gu = jnp.einsum(
        "esd,edcr->escr", expert_rows, wide_w[:, :, :2], preferred_element_type=jnp.float32
    )
    rank_gu_low = (rank_gu * mask_slot[:, :, None, :]).astype(jnp.bfloat16)
    pre_gu = pre_gu + rank_scale * jnp.einsum(
        "escr,efcr->escf", rank_gu_low, hidden_w[:, :, :2], preferred_element_type=jnp.float32
    )
    gate_pre = pre_gu[:, :, 0]
    up_pre = pre_gu[:, :, 1]
    sigma = jax.nn.sigmoid(gate_pre)
    activated = gate_pre * sigma
    inner_bf = (activated * up_pre).astype(jnp.bfloat16)
    rank_down = jnp.einsum(
        "esf,efr->esr", inner_bf, hidden_w[:, :, 2], preferred_element_type=jnp.float32
    )
    rank_down_low = (rank_down * mask_slot).astype(jnp.bfloat16)
    expert_output = jnp.einsum(
        "esf,edf->esd", inner_bf, down_w, preferred_element_type=jnp.float32
    ) + down_scale * jnp.einsum(
        "esr,edr->esd", rank_down_low, wide_w[:, :, 2], preferred_element_type=jnp.float32
    )
    weighted = (gate_slot[:, :, None] * expert_output).reshape(-1, width)
    combined = jnp.zeros((rows, width), jnp.float32).at[slot_flat].add(weighted)
    moe_part = lax.psum_scatter(
        combined.astype(jnp.bfloat16), "gy", scatter_dimension=1, tiled=True
    ).astype(jnp.float32)
    layer_out = (middle + moe_part).astype(jnp.bfloat16)
    grad_rows = lax.all_gather(out_grad, "gy", axis=1, tiled=True)
    grad_slot = grad_rows[slot_rows].astype(jnp.float32)
    gate_grad = jnp.sum(grad_slot * expert_output, axis=-1) * valid
    out_grad_bf = (gate_slot[:, :, None] * grad_slot).astype(jnp.bfloat16)
    gate_up_w, down_w, wide_w, hidden_w = fetch_experts(w_gate_up, w_down, exp_wide, exp_hidden)
    inner_grad = jnp.einsum("esd,edf->esf", out_grad_bf, down_w, preferred_element_type=jnp.float32)
    rank_down_grad = (
        down_scale
        * jnp.einsum(
            "esd,edr->esr", out_grad_bf, wide_w[:, :, 2], preferred_element_type=jnp.float32
        )
        * mask_slot
    ).astype(jnp.bfloat16)
    wide_down_grad = down_scale * jnp.einsum(
        "esd,esr->edr", out_grad_bf, rank_down_low, preferred_element_type=jnp.float32
    )
    inner_grad = inner_grad + jnp.einsum(
        "esr,efr->esf", rank_down_grad, hidden_w[:, :, 2], preferred_element_type=jnp.float32
    )
    hidden_down_grad = jnp.einsum(
        "esf,esr->efr", inner_bf, rank_down_grad, preferred_element_type=jnp.float32
    )
    gate_pre_grad = inner_grad * up_pre * sigma * (1.0 + gate_pre * (1.0 - sigma))
    up_pre_grad = inner_grad * activated
    gu_grad = jnp.stack([gate_pre_grad, up_pre_grad], axis=2).astype(jnp.bfloat16)
    rows_grad = jnp.einsum("escf,edcf->esd", gu_grad, gate_up_w, preferred_element_type=jnp.float32)
    rank_gu_grad = (
        rank_scale
        * jnp.einsum(
            "escf,efcr->escr", gu_grad, hidden_w[:, :, :2], preferred_element_type=jnp.float32
        )
        * mask_slot[:, :, None, :]
    ).astype(jnp.bfloat16)
    hidden_gu_grad = rank_scale * jnp.einsum(
        "escf,escr->efcr", gu_grad, rank_gu_low, preferred_element_type=jnp.float32
    )
    rows_grad = rows_grad + jnp.einsum(
        "escr,edcr->esd", rank_gu_grad, wide_w[:, :, :2], preferred_element_type=jnp.float32
    )
    wide_gu_grad = jnp.einsum(
        "esd,escr->edcr", expert_rows, rank_gu_grad, preferred_element_type=jnp.float32
    )
    probs_grad_local = (
        jnp.zeros((experts_local, rows), jnp.float32)
        .at[jnp.arange(experts_local, dtype=jnp.int32)[:, None], slot_rows]
        .add(gate_grad)
        .T
    )
    mixed = jnp.sum(probs_local * probs_grad_local, axis=-1, keepdims=True)
    logit_grad = lax.dynamic_update_slice_in_dim(
        -route_probs * mixed, probs_local * (probs_grad_local - mixed), first_expert, axis=1
    )
    normed_two_grad = jnp.dot(logit_grad, router.astype(jnp.float32).T, precision=highest)
    normed_two_grad = normed_two_grad.at[slot_flat].add(rows_grad.reshape(-1, width))
    stat_two = jnp.sum(normed_two_grad * mlp_gain * hat_two, axis=-1, keepdims=True)
    part_two, stat_two_sum = (
        lax.psum_scatter(
            normed_two_grad.astype(jnp.bfloat16), "gy", scatter_dimension=1, tiled=True
        ).astype(jnp.float32),
        lax.psum_scatter(
            jnp.broadcast_to(stat_two, (rows, groups)).astype(jnp.bfloat16),
            "gy",
            scatter_dimension=1,
            tiled=True,
        ).astype(jnp.float32),
    )
    gain_two_local = lax.dynamic_slice_in_dim(mlp_gain, col_start, width_local)
    hat_two_local = lax.dynamic_slice_in_dim(hat_two, col_start, width_local, axis=1)
    middle_grad = out_grad.astype(jnp.float32) + scale_two * (
        part_two * gain_two_local - hat_two_local * stat_two_sum / width
    )
    branch_rows = lax.all_gather(middle_grad.astype(jnp.bfloat16), "gy", axis=1, tiled=True)
    attention_gradient = jnp.einsum(
        "td,hed->the", branch_rows, out_weight, preferred_element_type=jnp.float32
    )
    rank_out_grad = rank_scale * jnp.einsum(
        "td,rd->tr", branch_rows, b_full, preferred_element_type=jnp.float32
    )
    rank_out_bf = (rank_out_grad * rank_mask).astype(jnp.bfloat16)
    b_out_part = rank_scale * jnp.einsum(
        "thr,td->rd", rank_out_low, branch_rows, preferred_element_type=jnp.float32
    )
    pack_out_grad = jnp.einsum(
        "the,tr->hre", attn_bf, rank_out_bf, preferred_element_type=jnp.float32
    )
    attention_gradient = attention_gradient + jnp.einsum(
        "tr,hre->the", rank_out_bf, head_pack[:, 3], preferred_element_type=jnp.float32
    )
    attn_grad_bf = attention_gradient.reshape(nseq, SEQ, heads_local, head_width).astype(
        jnp.bfloat16
    )
    scores_again = (
        jnp.einsum("nqhe,nkhe->nhqk", query_bf, key_bf, preferred_element_type=jnp.float32)
        * inv_root
    )
    scores_again = jnp.where(allowed, scores_again, -1e30)
    weights_again = jnp.exp(scores_again - log_total)
    value_grad = jnp.einsum(
        "nhqk,nqhe->nkhe",
        weights_again.astype(jnp.bfloat16),
        attn_grad_bf,
        preferred_element_type=jnp.float32,
    )
    weight_grad = jnp.einsum(
        "nqhe,nkhe->nhqk", attn_grad_bf, values_seq, preferred_element_type=jnp.float32
    )
    row_dot = jnp.sum(weight_grad * weights_again, axis=-1, keepdims=True)
    score_grad = (weights_again * (weight_grad - row_dot)).astype(jnp.bfloat16)
    query_grad = (
        jnp.einsum("nhqk,nkhe->nqhe", score_grad, key_bf, preferred_element_type=jnp.float32)
        * inv_root
    )
    key_grad = (
        jnp.einsum("nhqk,nqhe->nkhe", score_grad, query_bf, preferred_element_type=jnp.float32)
        * inv_root
    )
    query_hat_grad = (
        unrotate(query_grad, cosine, sine).reshape(rows, heads_local, head_width) * gains_local[0]
    )
    key_hat_grad = (
        unrotate(key_grad, cosine, sine).reshape(rows, heads_local, head_width) * gains_local[1]
    )
    value_pre_grad = value_grad.reshape(rows, heads_local, head_width)
    b_heads_f = head_pack[:, :3].astype(jnp.float32)
    stat_query = jnp.sum(query_hat_grad * query_hat, axis=(1, 2))
    stat_key = jnp.sum(key_hat_grad * key_hat, axis=(1, 2))
    first_terms = jnp.einsum(
        "tche,hcre->tcr",
        jnp.stack([query_hat_grad, key_hat_grad, value_pre_grad], axis=1),
        b_heads_f,
        precision=highest,
    )
    second_terms = jnp.einsum(
        "tche,hcre->tcr",
        jnp.stack([query_hat, key_hat], axis=1),
        b_heads_f[:, :2],
        precision=highest,
    )
    stat_total, first_total, second_total = (
        lax.psum(jnp.stack([stat_query, stat_key], axis=1).astype(jnp.bfloat16), "gy").astype(
            jnp.float32
        ),
        lax.psum(first_terms.astype(jnp.bfloat16), "gy").astype(jnp.float32),
        lax.psum(second_terms.astype(jnp.bfloat16), "gy").astype(jnp.float32),
    )
    mean_qk = stat_total / width
    scales_qk = jnp.stack([query_scale[:, 0, 0], key_scale[:, 0, 0]], axis=1)
    rank_qk = scales_qk[:, :, None] * (first_total[:, :2] - second_total * mean_qk[:, :, None])
    rank_grad_full = rank_scale * jnp.concatenate([rank_qk, first_total[:, 2:]], axis=1)
    rank_grad_bf = (rank_grad_full * rank_mask[:, None, :]).astype(jnp.bfloat16)
    query_pre_grad = query_scale * (query_hat_grad - query_hat * mean_qk[:, 0][:, None, None])
    key_pre_grad = key_scale * (key_hat_grad - key_hat * mean_qk[:, 1][:, None, None])
    pre_grad = jnp.stack([query_pre_grad, key_pre_grad, value_pre_grad], axis=2)
    pack_b_grad = rank_scale * jnp.einsum(
        "tcr,thce->hcre", rank_low.astype(jnp.float32), pre_grad, precision=highest
    )
    normed_one_grad = jnp.einsum(
        "thce,dhce->td",
        pre_grad.astype(jnp.bfloat16),
        qkv_weight,
        preferred_element_type=jnp.float32,
    )
    adapter_input_gradient = jnp.einsum(
        "tcr,cdr->td", rank_grad_bf, a_qkv, preferred_element_type=jnp.float32
    )
    first_normalized_shard = lax.dynamic_slice_in_dim(hat_one, col_start, width_local, axis=1)
    normed_local_bf = lax.dynamic_slice_in_dim(normed_bf, col_start, width_local, axis=1)
    a_rows_grad = jnp.einsum(
        "td,tcr->cdr", normed_local_bf, rank_grad_bf, preferred_element_type=jnp.float32
    )
    stat_one = jnp.sum(normed_one_grad * attn_gain * hat_one, axis=-1, keepdims=True) + jnp.sum(
        adapter_input_gradient * first_norm_gain * first_normalized_shard, axis=-1, keepdims=True
    )
    first_portion, stat_one_sum, b_out_sum = (
        lax.psum_scatter(
            normed_one_grad.astype(jnp.bfloat16), "gy", scatter_dimension=1, tiled=True
        ).astype(jnp.float32),
        lax.psum_scatter(
            jnp.broadcast_to(stat_one, (rows, groups)).astype(jnp.bfloat16),
            "gy",
            scatter_dimension=1,
            tiled=True,
        ).astype(jnp.float32),
        lax.psum_scatter(
            b_out_part.astype(jnp.bfloat16), "gy", scatter_dimension=1, tiled=True
        ).astype(jnp.float32),
    )
    normalized_shard_rows = first_portion + adapter_input_gradient
    input_grad = middle_grad + scale_one * (
        normalized_shard_rows * first_norm_gain - first_normalized_shard * stat_one_sum / width
    )
    head_grad = jnp.concatenate([pack_b_grad, pack_out_grad[:, None]], axis=1)
    head_sum, a_sum, b_sum = (
        lax.psum(head_grad.astype(jnp.bfloat16), "gx").astype(jnp.float32),
        lax.psum(a_rows_grad.astype(jnp.bfloat16), "gx").astype(jnp.float32),
        lax.psum(b_out_sum.astype(jnp.bfloat16), "gx").astype(jnp.float32),
    )
    wide_grad = jnp.concatenate([wide_gu_grad, wide_down_grad[:, :, None, :]], axis=2)
    hidden_grad = jnp.concatenate([hidden_gu_grad, hidden_down_grad[:, :, None, :]], axis=2)
    wide_sum, hidden_sum = (
        lax.psum_scatter(
            wide_grad.astype(jnp.bfloat16), "gx", scatter_dimension=1, tiled=True
        ).astype(jnp.float32),
        lax.psum_scatter(
            hidden_grad.astype(jnp.bfloat16), "gx", scatter_dimension=1, tiled=True
        ).astype(jnp.float32),
    )
    return (layer_out, input_grad, a_sum, b_sum, head_sum, wide_sum, hidden_sum)


def solution(mesh):
    return jax.shard_map(
        shards,
        mesh=mesh,
        in_specs=(
            P("gx", "gy"),
            P("gx", "gy"),
            P("gx", None),
            P("gx"),
            P("gx", None),
            P(),
            P(),
            P(),
            P("gx", "gy", None, None),
            P("gy", None, "gx"),
            P(None, "gy", None),
            P(None, "gy"),
            P("gy", None, None, None),
            P(),
            P("gy", "gx", None, None),
            P("gy", "gx", None),
            P("gy", "gx", None, None),
            P("gy", "gx", None, None),
        ),
        out_specs=(
            P("gx", "gy"),
            P("gx", "gy"),
            P(None, "gy", None),
            P(None, "gy"),
            P("gy", None, None, None),
            P("gy", "gx", None, None),
            P("gy", "gx", None, None),
        ),
        check_vma=False,
    )
```

profile of v0, /device:TPU:0, one launch (start us, length us, event | category | flops | bytes accessed | tf_op | source)
XLA Modules:
  0.0 2028.4 jit_solution(17170038854522961511)
XLA Ops:
  20.8 15.2 all_gather.44
  36.8 14.6 all-gather.12.cloned.1.call-done
  58.3 58.8 %all-gather.14.cloned.1.call-done = bf16[2048,2,3,128]{0,3,2,1:T(8,128)(2,1)} async-done(((bf16[512,2,3,128]{0,3,2,1:T(8,128)(2,1)}), bf16[2048,2,3,128]{0,3,2,1:T(8,128)(2,1)}) %all-gather.14.cloned.1.call-update) | async-done | bytes 3145744 | tf_op jit(solution)/shard_map/all_gather | solution.py:100
  125.4 18.1 all-gather.16.cloned.1.call-done
  149.7 14.6 all-reduce.2
  182.2 71.2 %reduce-scatter.8.cloned.1.call-done = f32[1024,256]{1,0:T(8,128)} async-done(((f32[1024,2048]{1,0:T(8,128)}), f32[1024,256]{1,0:T(8,128)}) %reduce-scatter.8.cloned.1.call-update) | async-done | bytes 1048592 | tf_op jit(solution)/shard_map/reduce_scatter | solution.py:170
  270.2 24.1 %scatter_custom_fusion.2 = s32[1152]{0:T(1024)S(1)} fusion(s32[4096]{0:T(1024)S(1)} %reshape.742, s32[4096]{0:T(1024)S(1)} %reshape.744, s32[]{:T(128)} %constant.200.clone.1), kind=kCustom, calls=%fused_computation.263 | custom fusion | bytes 4612
  312.3 20.6 %all-gather.20.cloned.1.call-done = bf16[1024,2048]{1,0:T(8,128)(2,1)} async-done(((bf16[1024,256]{1,0:T(8,128)(2,1)}), bf16[1024,2048]{1,0:T(8,128)(2,1)}) %all-gather.20.cloned.1.call-update) | async-done | bytes 4194320 | tf_op jit(solution)/shard_map/all_gather | solution.py:172
  349.4 100.4 %all-gather.24.cloned.1.call-done = bf16[4,2048,3,128]{3,1,2,0:T(8,128)(2,1)} async-done(((bf16[4,512,3,128]{3,1,2,0:T(8,128)(2,1)}), bf16[4,2048,3,128]{3,1,2,0:T(8,128)(2,1)}) %all-gather.24.cloned.1.call-update) | async-done | bytes 6291472 | tf_op jit(solution)/shard_map/all_gather | solution.py:58
  473.5 263.0 %all-gather.28.cloned.1.call-done = bf16[4,2048,1024]{2,1,0:T(8,128)(2,1)} async-done(((bf16[4,512,1024]{2,1,0:T(8,128)(2,1)}), bf16[4,2048,1024]{2,1,0:T(8,128)(2,1)}) %all-gather.28.cloned.1.call-update) | async-done | bytes 16777232 | tf_op jit(solution)/shard_map/all_gather | solution.py:57
  750.4 547.2 %all-gather.22.cloned.1.call-done = bf16[4,2048,2,1024]{3,1,2,0:T(8,128)(2,1)} async-done(((bf16[4,512,2,1024]{3,1,2,0:T(8,128)(2,1)}), bf16[4,2048,2,1024]{3,1,2,0:T(8,128)(2,1)}) %all-gather.22.cloned.1.call-update) | async-done | bytes 33554448 | tf_op jit(solution)/shard_map/all_gather | solution.py:56
  1297.6 20.1 fusion.203
  1317.7 43.3 %all-gather.26.cloned.1.call-done = bf16[4,1024,3,128]{3,1,2,0:T(8,128)(2,1)} async-done(((bf16[4,256,3,128]{3,1,2,0:T(8,128)(2,1)}), bf16[4,1024,3,128]{3,1,2,0:T(8,128)(2,1)}) %all-gather.26.cloned.1.call-update) | async-done | bytes 3145744 | tf_op jit(solution)/shard_map/all_gather | solution.py:59
  1420.1 20.7 %bitcast_add_fusion = f32[4,288,2048]{2,1,0:T(8,128)} fusion(f32[4,288,2048,1]{2,1,3,0:T(8,128)} %fusion.28, bf16[4,2048,2,1024]{3,1,2,0:T(8,128)(2,1)} %all-gather.22.cloned.1.call-done, bf16[4,288,1,1024]{3,1,0,2:T(8,128)(2,1)} %get-tuple-element.71, bf16[4,288,1,1024]{3,1,0,2:T(8,128)(2,1)S(1)} %copy-done.95), kind=kOutput, calls=%fused_computation.18 | convolution fusion | flops 9668395008 | bytes 57147392 | tf_op jit(solution)/shard_map/escf,edcf->esd/dot_general | solution.py:257
  1440.8 27.8 %scatter_fusion = f32[1024,2048]{1,0:T(8,128)} fusion(f32[1024,2048]{1,0:T(8,128)} %fusion.205, s32[1152]{0:T(1024)S(1)} %fusion.179, f32[1152,2048]{1,0:T(8,128)} %bitcast.351), kind=kCustom, calls=%fused_computation.5 | custom fusion | flops 2359296 | bytes 28316160 | tf_op jit(solution)/shard_map/scatter-add | solution.py:285
  1482.4 24.3 %all-reduce = bf16[1024,8]{0,1:T(8,128)(2,1)S(1)} all-reduce(bf16[1024,8]{0,1:T(8,128)(2,1)S(1)} %broadcast_in_dim.63), channel_id=5, replica_groups=mesh['gx'=4,'gy'=8] {'gy'}, use_global_device_ids=true, to_apply=%region_26.27.clone | all-reduce | flops 8192 | bytes 32768
  1507.3 24.5 %reduce-scatter.12.cloned.1.call-done = bf16[1024,256]{1,0:T(8,128)(2,1)} async-done(((bf16[1024,2048]{1,0:T(8,128)(2,1)}), bf16[1024,256]{1,0:T(8,128)(2,1)}) %reduce-scatter.12.cloned.1.call-update) | async-done | bytes 524304 | tf_op jit(solution)/shard_map/reduce_scatter | solution.py:288
  1537.6 34.5 %all-gather.32.cloned.1.call-done = bf16[1024,2048]{1,0:T(8,128)(2,1)} async-done(((bf16[1024,256]{1,0:T(8,128)(2,1)}), bf16[1024,2048]{1,0:T(8,128)(2,1)}) %all-gather.32.cloned.1.call-update) | async-done | bytes 4194320 | tf_op jit(solution)/shard_map/all_gather | solution.py:303
  1608.0 25.2 %scatter_custom_fusion = f32[1024,2048]{1,0:T(8,128)} fusion(s32[1152]{0:T(1024)S(1)} %fusion.179, f32[1152,2048]{1,0:T(8,128)} %bitcast.352, f32[]{:T(128)} %constant.195.clone.1), kind=kCustom, calls=%fused_computation.58 | custom fusion | flops 2359296 | bytes 8389120 | tf_op jit(solution)/shard_map/scatter-add | solution.py:227
  1701.6 51.8 %reduce-scatter.20.cloned.1.call-done = bf16[4,256,3,128]{1,3,2,0:T(8,128)(2,1)} async-done(((bf16[4,1024,3,128]{1,3,2,0:T(8,128)(2,1)}), bf16[4,256,3,128]{1,3,2,0:T(8,128)(2,1)}) %reduce-scatter.20.cloned.1.call-update) | async-done | bytes 786448 | tf_op jit(solution)/shard_map/reduce_scatter | solution.py:435
  1755.9 52.0 %reduce-scatter.10.cloned.1.call-done = bf16[1024,256]{1,0:T(8,128)(2,1)} async-done(((bf16[1024,2048]{1,0:T(8,128)(2,1)}), bf16[1024,256]{1,0:T(8,128)(2,1)}) %reduce-scatter.10.cloned.1.call-update) | async-done | bytes 524304 | tf_op jit(solution)/shard_map/reduce_scatter | solution.py:228
  1809.9 111.0 %reduce-scatter.18.cloned.1.call-done = bf16[4,512,3,128]{3,1,2,0:T(8,128)(2,1)} async-done(((bf16[4,2048,3,128]{3,1,2,0:T(8,128)(2,1)}), bf16[4,512,3,128]{3,1,2,0:T(8,128)(2,1)}) %reduce-scatter.18.cloned.1.call-update) | async-done | bytes 1572880 | tf_op jit(solution)/shard_map/reduce_scatter | solution.py:432
  1932.9 24.5 %all-reduce.1 = bf16[1024,8]{0,1:T(8,128)(2,1)S(1)} all-reduce(bf16[1024,8]{0,1:T(8,128)(2,1)S(1)} %broadcast_in_dim.64), channel_id=7, replica_groups=mesh['gx'=4,'gy'=8] {'gy'}, use_global_device_ids=true, to_apply=%region_36.37.clone | all-reduce | flops 8192 | bytes 32768
  1969.0 49.3 %reduce-scatter.14.cloned.1.call-done = bf16[1024,256]{1,0:T(8,128)(2,1)} async-done(((bf16[1024,2048]{1,0:T(8,128)(2,1)}), bf16[1024,256]{1,0:T(8,128)(2,1)}) %reduce-scatter.14.cloned.1.call-update) | async-done | bytes 524304 | tf_op jit(solution)/shard_map/reduce_scatter | solution.py:406
  (407 shorter events, 354.9 us)
Async XLA Ops:
  7.2 330.1 %copy-start = (bf16[2048,32]{0,1:T(8,128)(2,1)S(1)}, bf16[2048,32]{0,1:T(8,128)(2,1)}, u32[]{:S(2)}) copy-start(bf16[2048,32]{0,1:T(8,128)(2,1)} %param.35) | copy-start | bytes 393220
  7.2 44.3 %all-gather.12.cloned.1.call-start = ((), (), s32[]{:S(2)}) async-start(), calls=%async_computation.7 | async-start | bytes 4718592 | tf_op jit(solution)/shard_map/all_gather | solution.py:95
  7.9 109.2 %all-gather.14.cloned.1.call-start = ((), (), s32[]{:S(2)}) async-start(), calls=%async_computation.8 | async-start | bytes 3932160 | tf_op jit(solution)/shard_map/all_gather | solution.py:100
  11.0 132.4 %all-gather.16.cloned.1.call-start = ((), (), s32[]{:S(2)}) async-start(), calls=%async_computation.9 | async-start | bytes 1769472 | tf_op jit(solution)/shard_map/all_gather | solution.py:96
  11.8 162.4 %all-gather.18.cloned.1.call-start = ((), (), s32[]{:S(2)}) async-start(), calls=%async_computation.10 | async-start | bytes 1310720 | tf_op jit(solution)/shard_map/all_gather | solution.py:101
  12.4 241.0 %reduce-scatter.8.cloned.1.call-start = ((), (), s32[]{:S(2)}) async-start(), calls=%async_computation.11 | async-start | bytes 9437184 | tf_op jit(solution)/shard_map/reduce_scatter | solution.py:170
  181.6 117.3 %all-gather.30.cloned.1.call-start = ((), (), s32[]{:S(2)}) async-start(), calls=%async_computation.18 | async-start | bytes 4718592 | tf_op jit(solution)/shard_map/all_gather | solution.py:232
  182.1 150.7 %all-gather.20.cloned.1.call-start = ((), (), s32[]{:S(2)}) async-start(), calls=%async_computation.12 | async-start | bytes 4718592 | tf_op jit(solution)/shard_map/all_gather | solution.py:172
  255.5 194.3 %all-gather.24.cloned.1.call-start = ((), (), s32[]{:S(2)}) async-start(), calls=%async_computation.14 | async-start | bytes 7864320 | tf_op jit(solution)/shard_map/all_gather | solution.py:58
  256.3 480.2 %all-gather.28.cloned.1.call-start = ((), (), s32[]{:S(2)}) async-start(), calls=%async_computation.16 | async-start | bytes 20971520 | tf_op jit(solution)/shard_map/all_gather | solution.py:57
  257.0 1040.6 %all-gather.22.cloned.1.call-start = ((), (), s32[]{:S(2)}) async-start(), calls=%async_computation.13 | async-start | bytes 41943040 | tf_op jit(solution)/shard_map/all_gather | solution.py:56
  266.4 1094.5 %all-gather.26.cloned.1.call-start = ((), (), s32[]{:S(2)}) async-start(), calls=%async_computation.15 | async-start | bytes 3932160 | tf_op jit(solution)/shard_map/all_gather | solution.py:59
  267.2 1264.6 %reduce-scatter.12.cloned.1.call-start = ((), (), s32[]{:S(2)}) async-start(), calls=%async_computation.19 | async-start | bytes 4718592 | tf_op jit(solution)/shard_map/reduce_scatter | solution.py:288
  349.4 1035.5 %copy-start.82 = (f32[4,288]{1,0:T(4,128)}, f32[4,288]{1,0:T(4,128)S(1)}, u32[]{:S(2)}) copy-start(f32[4,288]{1,0:T(4,128)S(1)} %select_select_fusion) | copy-start | bytes 13828
  454.3 912.5 %copy-start.57 = (bf16[4,288,128]{2,1,0:T(8,128)(2,1)}, bf16[4,288,128]{2,1,0:T(8,128)(2,1)S(1)}, u32[]{:S(2)}) copy-start(bf16[4,288,128]{2,1,0:T(8,128)(2,1)S(1)} %fusion.121) | copy-start | bytes 884740
  473.5 887.5 %copy-start.56 = (bf16[4,288,2,128]{3,1,2,0:T(8,128)(2,1)}, bf16[4,288,2,128]{3,1,2,0:T(8,128)(2,1)S(1)}, u32[]{:S(2)}) copy-start(bf16[4,288,2,128]{3,1,2,0:T(8,128)(2,1)S(1)} %fusion.85) | copy-start | bytes 1769476
  1481.6 90.5 %all-gather.32.cloned.1.call-start = ((), (), s32[]{:S(2)}) async-start(), calls=%async_computation.20 | async-start | bytes 4718592 | tf_op jit(solution)/shard_map/all_gather | solution.py:303
  1534.5 140.5 %all-reduce.8.cloned.1.call-start = ((), (), s32[]{:S(2)}) async-start(), calls=%async_computation.25 | async-start | bytes 2621440 | tf_op jit(solution)/shard_map/psum | solution.py:374
  1595.8 94.6 %reduce-scatter.16.cloned.1.call-start = ((), (), s32[]{:S(2)}) async-start(), calls=%async_computation.22 | async-start | bytes 589824 | tf_op jit(solution)/shard_map/reduce_scatter | solution.py:415
  1599.6 153.7 %reduce-scatter.20.cloned.1.call-start = ((), (), s32[]{:S(2)}) async-start(), calls=%async_computation.24 | async-start | bytes 3932160 | tf_op jit(solution)/shard_map/reduce_scatter | solution.py:435
  1607.9 200.0 %reduce-scatter.10.cloned.1.call-start = ((), (), s32[]{:S(2)}) async-start(), calls=%async_computation.17 | async-start | bytes 4718592 | tf_op jit(solution)/shard_map/reduce_scatter | solution.py:228
  1639.3 281.6 %reduce-scatter.18.cloned.1.call-start = ((), (), s32[]{:S(2)}) async-start(), calls=%async_computation.23 | async-start | bytes 7864320 | tf_op jit(solution)/shard_map/reduce_scatter | solution.py:432
  1653.1 310.7 %all-reduce.10.cloned.1.call-start = ((), (), s32[]{:S(2)}) async-start(), calls=%async_computation.26 | async-start | bytes 1048576 | tf_op jit(solution)/shard_map/psum | solution.py:426
  1690.4 327.9 %reduce-scatter.14.cloned.1.call-start = ((), (), s32[]{:S(2)}) async-start(), calls=%async_computation.21 | async-start | bytes 4718592 | tf_op jit(solution)/shard_map/reduce_scatter | solution.py:406
  (100 other events, 2420.1 us)
Sparse Core Ops, SparseCore 0:
  9.9 41.5 all-gather.11
  53.6 63.4 all-gather.13
  119.0 24.3 all-gather.15
  144.9 27.9 all-gather.17
  181.7 71.6 reduce-scatter.7
  255.3 37.4 all-gather.29
  295.3 37.4 all-gather.19
  334.5 115.3 all-gather.23
  451.5 284.9 all-gather.27
  738.0 559.5 all-gather.21
  1299.3 61.6 all-gather.25
  1481.8 49.9 reduce-scatter.11
  1534.7 37.4 all-gather.31
  1595.9 57.8 all-reduce.7
  1657.0 33.2 reduce-scatter.15
  1693.1 60.2 reduce-scatter.19
  1756.6 51.3 reduce-scatter.9
  1810.2 110.7 reduce-scatter.17
  1924.3 39.4 all-reduce.9
  1967.3 50.8 reduce-scatter.13
where the time goes:
time: 2040 us; the launch traced here: 2030 us
  waiting for transfers between devices  1480 us (73%)
  matrix products  196 us (10%)
  other arithmetic  142 us (7%)
  local copies, waits for them, and re-layouts  101 us (5%)
  blocking collectives  91.8 us (4%)
    all_gather x1, waiting for transfers between devices, fetch_experts(): lax.all_gather(w_gate_up, 'gx', axis=1, tiled=True)  547 us
    all_gather x1, waiting for transfers between devices, fetch_experts(): lax.all_gather(w_down, 'gx', axis=1, tiled=True)  263 us
    reduce_scatter x1, waiting for transfers between devices, shards(): lax.psum_scatter(wide_grad.astype(jnp.bfloat16), 'gx', scatter_dimension=...  111 us
    all_gather x1, waiting for transfers between devices, fetch_experts(): lax.all_gather(exp_wide, 'gx', axis=1, tiled=True)  100 us
    reduce_scatter x1, waiting for transfers between devices, shards(): branch = lax.psum_scatter(out_terms, 'gy', scatter_dimension=1, tiled=True)  71.2 us
    all_gather x1, waiting for transfers between devices, shards(): lax.all_gather(w_qkv, 'gx', axis=0, tiled=True)  58.8 us
    unnamed x219, local copies, waits for them, and re-layouts  55.5 us
    reduce_scatter x1, waiting for transfers between devices, shards(): lax.psum_scatter(combined.astype(jnp.bfloat16), 'gy', scatter_dimension=1...  52 us
  transfers between devices with their start and end apart: 20, of which 17 were waited for; matrix products, arithmetic and copies ran while one was open for 14% of the time, Pallas kernels for 0%

commit v1 on v0

v1 whole, which is shorter than its diff:
```python
import jax
import jax.numpy as jnp
from jax import lax
from jax.sharding import PartitionSpec as P

RANK = 16
SEQ = 1024
PIECE = 256
CAP = 288


norm_eps = 1e-05
rope_theta = 10000.0
rank_scale = 0.5
down_scale = 4.0
bf16 = jnp.bfloat16
f32 = jnp.float32


def rope_tables(length, width):
    half_width = width // 2
    frequency = rope_theta ** (-2.0 * jnp.arange(half_width, dtype=f32) / width)
    angles = jnp.arange(length, dtype=f32)[:, None] * frequency[None, :]
    return (jnp.cos(angles), jnp.sin(angles))


def apply_rotary(values, cosine, sine):
    half_width = values.shape[-1] // 2
    first = values[..., :half_width]
    second = values[..., half_width:]
    return jnp.concatenate(
        [first * cosine - second * sine, second * cosine + first * sine], axis=-1
    )


def unrotate(grads, cosine, sine):
    half_width = grads.shape[-1] // 2
    first = grads[..., :half_width]
    second = grads[..., half_width:]
    return jnp.concatenate(
        [first * cosine + second * sine, second * cosine - first * sine], axis=-1
    )


def allowed_mask(piece_starts):
    places = jnp.arange(SEQ, dtype=jnp.int32)
    causal = places[None, :] <= places[:, None]
    inside = (places[None, None, :] >= piece_starts[:, :, None]) & (
        places[None, None, :] < piece_starts[:, :, None] + PIECE
    )
    same_piece = jnp.any(inside[:, :, :, None] & inside[:, :, None, :], axis=1)
    return causal[None] | same_piece


def dot(spec, left, right):
    return jnp.einsum(spec, left, right, preferred_element_type=f32)


def after(first, *later):
    return lax.optimization_barrier((first,) + later)[1:]


def shards(
    block_input,
    out_grad,
    routes,
    adapter_ids,
    piece_starts,
    attn_gain,
    qk_gain,
    mlp_gain,
    w_qkv,
    w_out,
    a_qkv,
    b_out,
    head_pack,
    router,
    w_gate_up,
    w_down,
    exp_wide,
    exp_hidden,
):
    planes = lax.axis_size("gx")
    groups = lax.axis_size("gy")
    plane = lax.axis_index("gx")
    column = lax.axis_index("gy")
    rows, width_local = block_input.shape
    width = width_local * groups
    heads_local = head_pack.shape[0]
    rank_cols = head_pack.shape[2]
    head_width = head_pack.shape[3]
    experts_local = w_gate_up.shape[0]
    hidden_width = w_gate_up.shape[3]
    nseq = adapter_ids.shape[0]
    inv_root = head_width ** (-0.5)
    repeats = planes // experts_local
    sets = None
    if repeats > 1:
        sets = [[r * experts_local + k for k in range(experts_local)] for r in range(repeats)]
    own = lax.rem(plane, experts_local)

    def over_planes(x):
        return lax.all_gather(x, "gx", axis=0, tiled=False, axis_index_groups=sets)

    def sum_planes(x):
        parts = lax.all_to_all(x, "gx", 0, 0, tiled=True, axis_index_groups=sets)
        return jnp.sum(parts.astype(f32), axis=0)

    def own_expert(x):
        if repeats > 1:
            x = jnp.tile(x, (repeats, 1, 1))
        x = lax.all_to_all(x, "gx", 0, 0, tiled=True)
        return x.reshape((x.shape[0] * x.shape[1], x.shape[2]))

    def spread_grad(x):
        parts = lax.all_to_all(
            x.reshape(planes, x.shape[0] // planes, x.shape[1]), "gx", 0, 0, tiled=True
        )
        parts = parts.reshape((repeats, experts_local) + parts.shape[1:])
        return jnp.sum(parts.astype(f32), axis=0)

    compact = nseq * RANK

    def pick(x, axis):
        return jnp.concatenate(
            [
                lax.dynamic_slice_in_dim(x, adapter_ids[n] * RANK, RANK, axis=axis)
                for n in range(nseq)
            ],
            axis=axis,
        )

    token_seq = jnp.arange(rows, dtype=jnp.int32) // SEQ
    col_seq = jnp.arange(compact, dtype=jnp.int32) // RANK
    compact_mask = (token_seq[:, None] == col_seq[None, :]).astype(f32)
    a_pick = pick(a_qkv, 2)
    b_pick = pick(b_out, 0)
    pack_pick = pick(head_pack, 2)

    gathered = lax.all_gather(
        jnp.concatenate(
            [block_input, a_pick.transpose(0, 2, 1).reshape(3 * compact, width_local), b_pick],
            axis=0,
        ),
        "gy",
        axis=1,
        tiled=True,
    )
    full_rows = gathered[:rows]
    a_full = gathered[rows : rows + 3 * compact]
    b_full = gathered[rows + 3 * compact :]
    qkv_weight = lax.all_gather(w_qkv, "gx", axis=0, tiled=True)
    (w_out_later,) = after(qkv_weight, w_out)
    out_weight = lax.all_gather(w_out_later, "gx", axis=2, tiled=True)
    routes_all = over_planes(routes)
    adapters_all = lax.all_gather(adapter_ids, "gx", axis=0, tiled=False)

    out_grad_later, gate_up_later, wide_later, down_later, hidden_later = after(
        out_weight, out_grad, w_gate_up, exp_wide, w_down, exp_hidden
    )
    grad_planes = over_planes(out_grad_later)
    dl = w_gate_up.shape[1]
    wide_flat = exp_wide.reshape(experts_local, dl, 3 * rank_cols)
    first_shard = jnp.concatenate(
        [w_gate_up.reshape(experts_local, dl, 2 * hidden_width), wide_flat[:, :, : 2 * rank_cols]],
        axis=2,
    )
    second_shard = jnp.concatenate([w_down, wide_flat[:, :, 2 * rank_cols :]], axis=2)
    hidden_shard = exp_hidden.reshape(experts_local, exp_hidden.shape[1], 3 * rank_cols)
    (first_shard,) = after(grad_planes, first_shard)
    first_weight = own_expert(first_shard)
    second_shard, hidden_shard = after(first_weight, second_shard, hidden_shard)
    hidden_weight = own_expert(hidden_shard)
    second_weight = own_expert(second_shard)

    expert_ids = own + experts_local * jnp.arange(groups, dtype=jnp.int32)
    hits = jnp.any(routes_all[:, :, :, None] == expert_ids, axis=2)
    order = jnp.arange(rows, dtype=jnp.int32)
    earlier = (order[None, :] < order[:, None]).astype(bf16)
    places = dot("ts,gsc->gct", earlier, hits.astype(bf16))
    slot_key = jnp.where(hits.transpose(0, 2, 1), places.astype(jnp.int32), -1)
    slots = jnp.arange(CAP, dtype=jnp.int32)
    slot_pick = (slot_key[:, :, None, :] == slots[None, None, :, None]).astype(bf16)
    own_key = lax.dynamic_index_in_dim(slot_key, column, 1, keepdims=False)
    own_pick = (own_key[:, None, :] == slots[None, :, None]).astype(bf16)
    set_start = (plane // experts_local) * experts_local
    set_adapters = lax.dynamic_slice_in_dim(adapters_all, set_start, experts_local, axis=0)
    token_adapter = jnp.repeat(set_adapters, SEQ, axis=1, total_repeat_length=rows)
    rank_mask = (
        token_adapter[:, :, None] == jnp.arange(rank_cols, dtype=jnp.int32)[None, None, :] // RANK
    ).astype(bf16)
    slot_total = experts_local * CAP
    mask_slot = dot("gst,gtr->gsr", own_pick, rank_mask).reshape(slot_total, rank_cols)
    valid = jnp.max(mask_slot, axis=1)

    def to_experts(x):
        picked = dot("gcst,gtd->cgsd", slot_pick, x).astype(bf16)
        sent = lax.all_to_all(
            picked.reshape(groups, slot_total, width_local), "gy", 0, 0, tiled=True
        )
        return sent.transpose(1, 0, 2).reshape(slot_total, width)

    def from_experts(x):
        sent = x.astype(bf16).reshape(slot_total, groups, width_local).transpose(1, 0, 2)
        sent = lax.all_to_all(sent, "gy", 0, 0, tiled=True)
        placed = dot(
            "gcst,cgsd->gtd", slot_pick, sent.reshape(groups, experts_local, CAP, width_local)
        )
        return sum_planes(placed.astype(bf16))

    grad_slot = to_experts(grad_planes)

    col_start = column * width_local
    first_norm_gain = lax.dynamic_slice_in_dim(attn_gain, col_start, width_local)
    input_f = full_rows.astype(f32)
    scale_one = lax.rsqrt(jnp.mean(input_f * input_f, axis=-1, keepdims=True) + norm_eps)
    hat_one = input_f * scale_one
    normed_bf = (hat_one * attn_gain).astype(bf16)
    base = dot("td,dhce->thce", normed_bf, qkv_weight)
    rank_in = dot("td,kd->tk", normed_bf, a_full).reshape(rows, 3, compact)
    rank_low = (rank_in * compact_mask[:, None, :]).astype(bf16)
    projected = base + rank_scale * dot("tcr,hcre->thce", rank_low, pack_pick[:, :3])
    query_pre = projected[:, :, 0]
    key_pre = projected[:, :, 1]
    value_bf = projected[:, :, 2].astype(bf16)
    square_sums = lax.psum(
        jnp.stack(
            [
                jnp.sum(query_pre * query_pre, axis=(1, 2)),
                jnp.sum(key_pre * key_pre, axis=(1, 2)),
            ]
        ),
        "gy",
    )
    query_scale = lax.rsqrt(square_sums[0] / width + norm_eps)[:, None, None]
    key_scale = lax.rsqrt(square_sums[1] / width + norm_eps)[:, None, None]
    head_start = column * heads_local * head_width
    gains_local = lax.dynamic_slice_in_dim(
        qk_gain, head_start, heads_local * head_width, axis=1
    ).reshape(2, heads_local, head_width)
    query_hat = query_pre * query_scale
    key_hat = key_pre * key_scale
    cosine, sine = rope_tables(SEQ, head_width)
    cosine = cosine[None, :, None, :]
    sine = sine[None, :, None, :]
    query_bf = apply_rotary(
        (query_hat * gains_local[0]).reshape(nseq, SEQ, heads_local, head_width), cosine, sine
    ).astype(bf16)
    key_bf = apply_rotary(
        (key_hat * gains_local[1]).reshape(nseq, SEQ, heads_local, head_width), cosine, sine
    ).astype(bf16)
    values_seq = value_bf.reshape(nseq, SEQ, heads_local, head_width)
    allowed = allowed_mask(piece_starts)[:, None]
    scores = dot("nqhe,nkhe->nhqk", query_bf, key_bf) * inv_root
    scores = jnp.where(allowed, scores, -1e30)
    row_peak = jnp.max(scores, axis=-1, keepdims=True)
    raised = jnp.exp(scores - row_peak)
    row_total = jnp.sum(raised, axis=-1, keepdims=True)
    log_total = row_peak + jnp.log(row_total)
    weights = raised / row_total
    attended = dot("nhqk,nkhe->nqhe", weights.astype(bf16), values_seq)
    attn_bf = attended.reshape(rows, heads_local, head_width).astype(bf16)
    rank_out = dot("the,hre->thr", attn_bf, pack_pick[:, 3])
    rank_out_low = (rank_out * compact_mask[:, None, :]).astype(bf16)
    out_terms = dot("the,hed->td", attn_bf, out_weight) + rank_scale * dot(
        "thr,rd->td", rank_out_low, b_full
    )
    branch = lax.psum_scatter(out_terms.astype(bf16), "gy", scatter_dimension=1, tiled=True)
    middle = block_input.astype(f32) + branch.astype(f32)
    middle_low = middle.astype(bf16)

    middle_slot = to_experts(over_planes(middle_low)).astype(f32)
    slot_scale = lax.rsqrt(jnp.mean(middle_slot * middle_slot, axis=-1, keepdims=True) + norm_eps)
    expert_in = (middle_slot * slot_scale * mlp_gain).astype(bf16)
    logits = jnp.dot(expert_in, router, preferred_element_type=f32)
    logit_raised = jnp.exp(logits - jnp.max(logits, axis=-1, keepdims=True))
    route_probs = logit_raised / jnp.sum(logit_raised, axis=-1, keepdims=True)
    own_id = column * experts_local + own
    is_own = (jnp.arange(router.shape[1], dtype=jnp.int32) == own_id).astype(f32)[None, :]
    gate = jnp.sum(route_probs * is_own, axis=1, keepdims=True) * valid[:, None]
    two_masks = jnp.concatenate([mask_slot, mask_slot], axis=1)
    pre_wide = jnp.dot(expert_in, first_weight, preferred_element_type=f32)
    rank_gu_low = (pre_wide[:, 2 * hidden_width :] * two_masks).astype(bf16)
    hidden_gate = hidden_weight[:, :rank_cols]
    hidden_up = hidden_weight[:, rank_cols : 2 * rank_cols]
    hidden_down = hidden_weight[:, 2 * rank_cols :]
    gate_pre = pre_wide[:, :hidden_width] + rank_scale * dot(
        "sr,fr->sf", rank_gu_low[:, :rank_cols], hidden_gate
    )
    up_pre = pre_wide[:, hidden_width : 2 * hidden_width] + rank_scale * dot(
        "sr,fr->sf", rank_gu_low[:, rank_cols:], hidden_up
    )
    sigma = jax.nn.sigmoid(gate_pre)
    activated = gate_pre * sigma
    inner_bf = (activated * up_pre).astype(bf16)
    rank_down = dot("sf,fr->sr", inner_bf, hidden_down)
    rank_down_low = (rank_down * mask_slot).astype(bf16)
    inner_wide = jnp.concatenate([inner_bf, (down_scale * rank_down_low).astype(bf16)], axis=1)
    expert_output = dot("sf,df->sd", inner_wide, second_weight)
    moe_part = from_experts(gate * expert_output)
    layer_out = (middle + moe_part).astype(bf16)

    grad_slot_f = grad_slot.astype(f32)
    gate_grad = jnp.sum(grad_slot_f * expert_output, axis=-1, keepdims=True)
    out_grad_bf = (gate * grad_slot_f).astype(bf16)
    inner_wide_grad = dot("sd,df->sf", out_grad_bf, second_weight)
    rank_down_grad = (down_scale * inner_wide_grad[:, hidden_width:] * mask_slot).astype(bf16)
    inner_grad = inner_wide_grad[:, :hidden_width] + dot("sr,fr->sf", rank_down_grad, hidden_down)
    gate_pre_grad = (inner_grad * up_pre * sigma * (1.0 + gate_pre * (1.0 - sigma))).astype(bf16)
    up_pre_grad = (inner_grad * activated).astype(bf16)
    rank_gu_grad = (
        rank_scale
        * jnp.concatenate(
            [
                dot("sf,fr->sr", gate_pre_grad, hidden_gate),
                dot("sf,fr->sr", up_pre_grad, hidden_up),
            ],
            axis=1,
        )
        * two_masks
    ).astype(bf16)
    logit_grad = (is_own - route_probs) * (gate * gate_grad)
    logit_high = logit_grad.astype(bf16)
    logit_rest = (logit_grad - logit_high.astype(f32)).astype(bf16)
    pre_wide_grad = jnp.concatenate([gate_pre_grad, up_pre_grad, rank_gu_grad], axis=1)
    rows_grad = dot("sf,df->sd", pre_wide_grad, first_weight) + dot(
        "se,de->sd",
        jnp.concatenate([logit_high, logit_rest], axis=1),
        jnp.concatenate([router, router], axis=1),
    )
    normed_two_part = from_experts(rows_grad)

    wide_grad = jnp.concatenate(
        [
            dot("sd,sr->dr", expert_in, rank_gu_grad),
            down_scale * dot("sd,sr->dr", out_grad_bf, rank_down_low),
        ],
        axis=1,
    )
    hidden_grad = jnp.concatenate(
        [
            rank_scale * dot("sf,sr->fr", gate_pre_grad, rank_gu_low[:, :rank_cols]),
            rank_scale * dot("sf,sr->fr", up_pre_grad, rank_gu_low[:, rank_cols:]),
            dot("sf,sr->fr", inner_bf, rank_down_grad),
        ],
        axis=1,
    )
    wide_sum = spread_grad(wide_grad.astype(bf16)).reshape(exp_wide.shape)
    hidden_sum = spread_grad(hidden_grad.astype(bf16)).reshape(exp_hidden.shape)

    middle_rows = lax.all_gather(middle_low, "gy", axis=1, tiled=True).astype(f32)
    grad_rows = lax.all_gather(out_grad, "gy", axis=1, tiled=True).astype(f32)
    scale_two = lax.rsqrt(jnp.mean(middle_rows * middle_rows, axis=-1, keepdims=True) + norm_eps)
    normed_two_grad = lax.all_gather(
        normed_two_part.astype(bf16), "gy", axis=1, tiled=True
    ).astype(f32)
    hat_two = middle_rows * scale_two
    scaled_two = normed_two_grad * mlp_gain
    stat_two = jnp.mean(scaled_two * hat_two, axis=-1, keepdims=True)
    branch_rows = (grad_rows + scale_two * (scaled_two - hat_two * stat_two)).astype(bf16)
    gain_two_local = lax.dynamic_slice_in_dim(mlp_gain, col_start, width_local)
    middle_grad = out_grad.astype(f32) + scale_two * (
        normed_two_part * gain_two_local - middle_low.astype(f32) * scale_two * stat_two
    )
    rank_out_grad = rank_scale * dot("td,rd->tr", branch_rows, b_full)
    rank_out_bf = (rank_out_grad * compact_mask).astype(bf16)
    b_out_part = rank_scale * dot("thr,td->rd", rank_out_low, branch_rows)
    pack_out_grad = dot("the,tr->hre", attn_bf, rank_out_bf)
    attention_gradient = dot("td,hed->the", branch_rows, out_weight) + dot(
        "tr,hre->the", rank_out_bf, pack_pick[:, 3]
    )
    attn_grad_bf = attention_gradient.reshape(nseq, SEQ, heads_local, head_width).astype(bf16)
    scores_again = dot("nqhe,nkhe->nhqk", query_bf, key_bf) * inv_root
    scores_again = jnp.where(allowed, scores_again, -1e30)
    weights_again = jnp.exp(scores_again - log_total)
    value_grad = dot("nhqk,nqhe->nkhe", weights_again.astype(bf16), attn_grad_bf)
    weight_grad = dot("nqhe,nkhe->nhqk", attn_grad_bf, values_seq)
    row_dot = jnp.sum(weight_grad * weights_again, axis=-1, keepdims=True)
    score_grad = (weights_again * (weight_grad - row_dot)).astype(bf16)
    query_grad = dot("nhqk,nkhe->nqhe", score_grad, key_bf) * inv_root
    key_grad = dot("nhqk,nqhe->nkhe", score_grad, query_bf) * inv_root
    query_hat_grad = (
        unrotate(query_grad, cosine, sine).reshape(rows, heads_local, head_width) * gains_local[0]
    )
    key_hat_grad = (
        unrotate(key_grad, cosine, sine).reshape(rows, heads_local, head_width) * gains_local[1]
    )
    value_pre_grad = value_grad.reshape(rows, heads_local, head_width)
    stat_query = jnp.sum(query_hat_grad * query_hat, axis=(1, 2))
    stat_key = jnp.sum(key_hat_grad * key_hat, axis=(1, 2))

    def rank_terms(values, which):
        return dot("the,hre->rt", values.astype(bf16), pack_pick[:, which])

    sums = jnp.concatenate(
        [
            rank_terms(query_hat_grad, 0),
            rank_terms(key_hat_grad, 1),
            rank_terms(value_pre_grad, 2),
            rank_terms(query_hat, 0),
            rank_terms(key_hat, 1),
            jnp.stack([stat_query, stat_key]),
        ],
        axis=0,
    )
    sums = lax.psum(sums, "gy")
    first_total = sums[: 3 * compact].reshape(3, compact, rows)
    second_total = sums[3 * compact : 5 * compact].reshape(2, compact, rows)
    mean_qk = sums[5 * compact :] / width
    scales_qk = jnp.stack([query_scale[:, 0, 0], key_scale[:, 0, 0]])
    rank_qk = scales_qk[:, None, :] * (first_total[:2] - second_total * mean_qk[:, None, :])
    rank_grad_full = rank_scale * jnp.concatenate([rank_qk, first_total[2:]], axis=0)
    rank_grad_bf = (rank_grad_full * compact_mask.T[None]).astype(bf16)
    query_pre_grad = query_scale * (query_hat_grad - query_hat * mean_qk[0][:, None, None])
    key_pre_grad = key_scale * (key_hat_grad - key_hat * mean_qk[1][:, None, None])
    pre_grad = jnp.stack([query_pre_grad, key_pre_grad, value_pre_grad], axis=2).astype(bf16)
    pack_b_grad = rank_scale * dot("tcr,thce->rhce", rank_low, pre_grad)
    normed_one_grad = dot("thce,dhce->td", pre_grad, qkv_weight)
    adapter_input_gradient = dot("crt,cdr->td", rank_grad_bf, a_pick)
    first_normalized_shard = lax.dynamic_slice_in_dim(hat_one, col_start, width_local, axis=1)
    normed_local_bf = lax.dynamic_slice_in_dim(normed_bf, col_start, width_local, axis=1)
    a_rows_grad = dot("td,crt->rcd", normed_local_bf, rank_grad_bf)
    stat_one = jnp.sum(normed_one_grad * attn_gain * hat_one, axis=-1) + jnp.sum(
        adapter_input_gradient * first_norm_gain * first_normalized_shard, axis=-1
    )
    stat_rows = stat_one.reshape(rows // width_local, width_local)
    stat_high = stat_rows.astype(bf16)
    stat_low = (stat_rows - stat_high.astype(f32)).astype(bf16)
    summed = lax.psum_scatter(
        jnp.concatenate(
            [
                normed_one_grad.astype(bf16),
                b_out_part.astype(bf16),
                jnp.tile(jnp.concatenate([stat_high, stat_low]), (1, groups)),
            ],
            axis=0,
        ),
        "gy",
        scatter_dimension=1,
        tiled=True,
    ).astype(f32)
    first_portion = summed[:rows]
    b_out_sum = summed[rows : rows + compact]
    stat_sum = summed[rows + compact :].reshape(2, rows)
    stat_one_sum = (stat_sum[0] + stat_sum[1])[:, None]
    normalized_shard_rows = first_portion + adapter_input_gradient
    input_grad = middle_grad + scale_one * (
        normalized_shard_rows * first_norm_gain - first_normalized_shard * stat_one_sum / width
    )

    pack_grad = jnp.concatenate(
        [
            pack_b_grad.transpose(1, 2, 0, 3),
            pack_out_grad[:, None],
        ],
        axis=1,
    )
    small = jnp.concatenate(
        [
            a_rows_grad.reshape(compact, 3 * width_local),
            b_out_sum,
            pack_grad.transpose(2, 0, 1, 3).reshape(compact, heads_local * 4 * head_width),
        ],
        axis=1,
    )
    small_all = lax.all_gather(small, "gx", axis=0, tiled=True)
    row_at = (
        adapters_all[:, :, None] * RANK + jnp.arange(RANK, dtype=jnp.int32)[None, None, :]
    ).reshape(-1)
    put = (jnp.arange(rank_cols, dtype=jnp.int32)[:, None] == row_at[None, :]).astype(f32)
    small_sum = jnp.dot(put, small_all, precision=lax.Precision.HIGHEST)
    a_end = 3 * width_local
    b_end = a_end + width_local
    a_sum = small_sum[:, :a_end].reshape(rank_cols, 3, width_local).transpose(1, 2, 0)
    b_sum = small_sum[:, a_end:b_end]
    head_sum = small_sum[:, b_end:].reshape(rank_cols, heads_local, 4, head_width)
    head_sum = head_sum.transpose(1, 2, 0, 3)
    return (layer_out, input_grad, a_sum, b_sum, head_sum, wide_sum, hidden_sum)


def solution(mesh):
    return jax.shard_map(
        shards,
        mesh=mesh,
        in_specs=(
            P("gx", "gy"),
            P("gx", "gy"),
            P("gx", None),
            P("gx"),
            P("gx", None),
            P(),
            P(),
            P(),
            P("gx", "gy", None, None),
            P("gy", None, "gx"),
            P(None, "gy", None),
            P(None, "gy"),
            P("gy", None, None, None),
            P(),
            P("gy", "gx", None, None),
            P("gy", "gx", None),
            P("gy", "gx", None, None),
            P("gy", "gx", None, None),
        ),
        out_specs=(
            P("gx", "gy"),
            P("gx", "gy"),
            P(None, "gy", None),
            P(None, "gy"),
            P("gy", None, None, None),
            P("gy", "gx", None, None),
            P("gy", "gx", None, None),
        ),
        check_vma=False,
    )
```

time: 2040 us -> 1170 us (0.57)
  waiting for transfers between devices: 1480 us -> 441 us
  blocking collectives: 91.8 us -> 253 us
  starting transfers between devices: 1.19 us -> 47.2 us
  other arithmetic: 142 us -> 107 us
    all_gather x11 -> x8, waiting for transfers between devices: 1100 us -> 113 us  [the longest x1 66.3 us: shards(): qkv_weight = lax.all_gather(w_qkv, 'gx', axis=0, tiled=True)]
    reduce_scatter x7 -> x2, waiting for transfers between devices: 369 us -> 0.04 us  [the longest x1 0.02 us: shards(): lax.psum_scatter(jnp.concatenate([normed_one_grad.astype(bf16), b_out_par...]
    all_to_all x0 -> x10, waiting for transfers between devices: none -> 260 us  [the longest x2 83 us: to_experts(): lax.all_to_all(picked.reshape(groups, slot_total, width_local), 'gy', 0,...]
    all_gather x1 -> x2, blocking collectives: 15.2 us -> 185 us  [the longest x1 169 us: over_planes(): return lax.all_gather(x, 'gx', axis=0, tiled=False, axis_index_groups=sets)]
    psum x2 -> x1, waiting for transfers between devices: 5.71 us -> 66.2 us  [shards(): sums = lax.psum(sums, 'gy')]
    scatter-add x2 -> x0, other arithmetic: 53 us -> none  [the longest x1 27.8 us: shards(): normed_two_grad.at[slot_flat].add(rows_grad.reshape(-1, width))]
    all_to_all x0 -> x1, blocking collectives: none -> 48.4 us  [sum_planes(): parts = lax.all_to_all(x, 'gx', 0, 0, tiled=True, axis_index_groups=sets)]
    all_to_all x0 -> x10, starting transfers between devices: none -> 46.8 us  [the longest x3 14.9 us: own_expert(): x = lax.all_to_all(x, 'gx', 0, 0, tiled=True)]
  transfers between devices with their start and end apart: 20 -> 21, of which waited for: 17 -> 11; matrix products, arithmetic and copies ran while one was open for 14% -> 27% of each run, Pallas kernels for 0% -> 0%
where the time goes in v1:
time: 1170 us; the launch traced here: 1160 us
  waiting for transfers between devices  441 us (38%)
  blocking collectives  253 us (22%)
  matrix products  182 us (16%)
  local copies, waits for them, and re-layouts  115 us (10%)
  other arithmetic  107 us (9%)
  starting transfers between devices  47.2 us (4%)
  between operations  16.7 us (1%)
    all_gather x1, blocking collectives, over_planes(): return lax.all_gather(x, 'gx', axis=0, tiled=False, axis_index_groups=sets)  169 us
    dot_general x46, matrix products, dot(): return jnp.einsum(spec, left, right, preferred_element_type=f32)  162 us
    all_to_all x2, waiting for transfers between devices, to_experts(): lax.all_to_all(picked.reshape(groups, slot_total, width_local), 'gy', 0,...  83 us
    all_to_all x2, waiting for transfers between devices, from_experts(): sent = lax.all_to_all(sent, 'gy', 0, 0, tiled=True)  70.9 us
    all_gather x1, waiting for transfers between devices, shards(): qkv_weight = lax.all_gather(w_qkv, 'gx', axis=0, tiled=True)  66.3 us
    psum x1, waiting for transfers between devices, shards(): sums = lax.psum(sums, 'gy')  66.2 us
    all_to_all x1, blocking collectives, sum_planes(): parts = lax.all_to_all(x, 'gx', 0, 0, tiled=True, axis_index_groups=sets)  48.4 us
    all_to_all x3, waiting for transfers between devices, own_expert(): x = lax.all_to_all(x, 'gx', 0, 0, tiled=True)  46 us
  transfers between devices with their start and end apart: 21, of which 11 were waited for; matrix products, arithmetic and copies ran while one was open for 27% of the time, Pallas kernels for 0%

profile of v1, /device:TPU:0, one launch (start us, length us, event | category | flops | bytes accessed | tf_op | source)
XLA Modules:
  0.0 1161.7 jit_solution(7328363067287841274)
XLA Ops:
  10.5 66.3 %all-gather.15.cloned.1.call-done = bf16[2048,2,3,128]{0,3,2,1:T(8,128)(2,1)} async-done(((bf16[512,2,3,128]{0,3,2,1:T(8,128)(2,1)}), bf16[2048,2,3,128]{0,3,2,1:T(8,128)(2,1)}) %all-gather.15.cloned.1.call-update) | async-done | bytes 3145744 | tf_op jit(solution)/shard_map/all_gather | solution.py:152
  84.6 14.5 %reshape.852 = bf16[4,512,2048]{2,1,0:T(8,128)(2,1)} reshape(bf16[4,512,2,1024]{3,2,1,0:T(2,128)(2,1)} %param.36) | data formatting | bytes 16777216 | tf_op jit(solution)/shard_map/reshape | solution.py:165
  99.1 8.8 pad_maximum_fusion
  121.8 23.7 %all-gather.13.cloned.1.call-done = bf16[1088,2048]{1,0:T(8,128)(2,1)} async-done(((bf16[1088,256]{1,0:T(8,128)(2,1)}), bf16[1088,2048]{1,0:T(8,128)(2,1)}) %all-gather.13.cloned.1.call-update) | async-done | bytes 4456464 | tf_op jit(solution)/shard_map/all_gather | solution.py:140
  162.3 14.3 %psum.14 = f32[2,1024]{1,0:T(2,128)S(1)} all-reduce(f32[2,1024]{1,0:T(2,128)S(1)} %pad_maximum_fusion.17), channel_id=1, replica_groups=mesh['gx'=4,'gy'=8] {'gy'}, use_global_device_ids=true, to_apply=%region_4.5 | all-reduce | flops 2048 | bytes 16384 | tf_op jit(solution)/shard_map/psum | solution.py:226
  190.6 168.9 %all-gather = s32[4096,8]{0,1:T(8,128)S(1)} all-gather(s32[1024,8]{0,1:T(8,128)S(1)} %copy-done.80), channel_id=2, replica_groups=mesh['gx'=4,'gy'=8] {'gx'}, dimensions={0}, use_global_device_ids=true | all-gather | bytes 163840 | tf_op jit(solution)/shard_map/all_gather | solution.py:103
  360.3 8.3 convert_bitcast_fusion.2
  385.3 45.2 %all-to-all-done.6 = bf16[8,1152,256]{2,1,0:T(8,128)(2,1)} async-done(((bf16[8,1152,256]{2,1,0:T(8,128)(2,1)}), bf16[8,1152,256]{2,1,0:T(8,128)(2,1)}, u32[]{:S(2)}, u32[]{:S(2)}) %all-to-all-start.6) | async-done | bytes 4718624 | tf_op jit(solution)/shard_map/all_to_all | solution.py:198
  473.4 37.8 %all-to-all-done = bf16[8,1152,256]{2,1,0:T(8,128)(2,1)} async-done(((bf16[8,1152,256]{2,1,0:T(8,128)(2,1)}), bf16[8,1152,256]{2,1,0:T(8,128)(2,1)}, u32[]{:S(2)}, u32[]{:S(2)}) %all-to-all-start) | async-done | bytes 4718624 | tf_op jit(solution)/shard_map/all_to_all | solution.py:198
  532.3 9.7 copy.258
  557.5 14.0 %fusion.215 = f32[1152,2304]{1,0:T(8,128)S(1)} fusion(bf16[1152,2048]{0,1:T(8,128)(2,1)S(1)} %bitcast.373, bf16[2048,2304]{1,0:T(8,128)(2,1)} %bitcast.47), kind=kOutput, calls=%fused_computation.356 | convolution fusion | flops 10871635968 | bytes 24772608 | tf_op jit(solution)/shard_map/dot_general | solution.py:282
  579.0 39.5 %all-to-all-done.3 = bf16[4,512,1152]{2,1,0:T(8,128)(2,1)} async-done(((bf16[4,512,1152]{2,1,0:T(8,128)(2,1)}), bf16[4,512,1152]{2,1,0:T(8,128)(2,1)}, u32[]{:S(2)}, u32[]{:S(2)}) %all-to-all-start.3) | async-done | bytes 4718624 | tf_op jit(solution)/shard_map/all_to_all | solution.py:112
  618.5 12.8 %multiply_reduce_fusion = (f32[1152]{0:T(1024)S(1)}, f32[1152,2048]{1,0:T(8,128)}) fusion(f32[1152,2048]{1,0:T(8,128)} %bitcast.358, bf16[2048,1152]{1,0:T(8,128)(2,1)} %bitcast.51, bf16[1152,128]{1,0:T(8,128)(2,1)S(1)} %get-tuple-element.120, bf16[1152,1024]{1,0:T(8,128)(2,1)} %copy-done.26), kind=kOutput, calls=%fused_computation.30 | convolution fusion | flops 5445843968 | bytes 26251776 | tf_op jit(solution)/shard_map/sf,df->sd/dot_general | solution.py:56
  643.3 10.3 fusion.216
  661.8 15.5 %fusion.29 = f32[1152,2048]{1,0:T(8,128)S(1)} fusion(bf16[2048,2304]{1,0:T(8,128)(2,1)} %bitcast.47, bf16[1152,256]{1,0:T(8,128)(2,1)S(1)} %fusion.86, bf16[1152,1024]{1,0:T(8,128)(2,1)} %copy-done.14, bf16[1152,1024]{1,0:T(8,128)(2,1)} %copy-done.15), kind=kOutput, calls=%fused_computation.57 | convolution fusion | flops 10887561216 | bytes 24182784 | tf_op jit(solution)/shard_map/sf,df->sd/dot_general | solution.py:56
  686.9 70.9 %all-to-all-done.7 = bf16[8,1152,256]{2,1,0:T(8,128)(2,1)} async-done(((bf16[8,1152,256]{2,1,0:T(8,128)(2,1)}), bf16[8,1152,256]{2,1,0:T(8,128)(2,1)}, u32[]{:S(2)}, u32[]{:S(2)}) %all-to-all-start.7) | async-done | bytes 4718624 | tf_op jit(solution)/shard_map/all_to_all | solution.py:205
  757.7 12.9 %bitcast_convert_fusion.1 = bf16[4,1024,256]{2,1,0:T(8,128)(2,1)S(1)} fusion(bf16[8,4,288,256]{3,2,1,0:T(8,128)(2,1)} %bitcast.64, s32[4,8,1024]{2,1,0:T(8,128)S(1)} %fusion.91), kind=kOutput, calls=%fused_computation.90 | convolution fusion | flops 4842323968 | bytes 6946816 | tf_op jit(solution)/shard_map/gcst,cgsd->gtd/dot_general | solution.py:56
  770.8 48.4 %all_to_all.55 = bf16[4,1024,256]{2,1,0:T(8,128)(2,1)S(1)} all-to-all(bf16[4,1024,256]{2,1,0:T(8,128)(2,1)S(1)} %bitcast_convert_fusion.1), channel_id=1, replica_groups=mesh['gx'=4,'gy'=8] {'gx'}, dimensions={0} | all-to-all | bytes 4194304 | tf_op jit(solution)/shard_map/all_to_all | solution.py:106
  875.6 23.2 %all-gather.23.cloned.1.call-done = bf16[1024,2048]{1,0:T(8,128)(2,1)} async-done(((bf16[1024,256]{1,0:T(8,128)(2,1)}), bf16[1024,2048]{1,0:T(8,128)(2,1)}) %all-gather.23.cloned.1.call-update) | async-done | bytes 4194320 | tf_op jit(solution)/shard_map/all_gather | solution.py:352
  941.4 66.2 %all-reduce.3.cloned.1.call-done = f32[82,1024]{1,0:T(8,128)} async-done(((f32[82,1024]{1,0:T(8,128)}), f32[82,1024]{1,0:T(8,128)}) %all-reduce.3.cloned.1.call-update) | async-done | bytes 335888 | tf_op jit(solution)/shard_map/psum | solution.py:406
  1033.0 13.5 %bitcast_convert_fusion.2 = bf16[4,1024,256]{2,1,0:T(8,128)(2,1)} fusion(bf16[8,4,288,256]{3,2,1,0:T(8,128)(2,1)} %bitcast.53, s32[4,8,1024]{2,1,0:T(8,128)S(1)} %copy-done.95), kind=kOutput, calls=%fused_computation.91 | convolution fusion | flops 4842323968 | bytes 6946816 | tf_op jit(solution)/shard_map/gcst,cgsd->gtd/dot_general | solution.py:56
  1046.6 19.2 %all-to-all-done.9 = bf16[4,512,384]{1,2,0:T(8,128)(2,1)S(1)} async-done(((bf16[4,512,384]{1,2,0:T(8,128)(2,1)}), bf16[4,512,384]{1,2,0:T(8,128)(2,1)S(1)}, u32[]{:S(2)}, u32[]{:S(2)}) %all-to-all-start.9) | async-done | bytes 1572896 | tf_op jit(solution)/shard_map/all_to_all | solution.py:116
  1077.7 40.5 %all-to-all-done.5 = bf16[4,1024,256]{2,1,0:T(8,128)(2,1)S(1)} async-done(((bf16[4,1024,256]{2,1,0:T(8,128)(2,1)}), bf16[4,1024,256]{2,1,0:T(8,128)(2,1)S(1)}, u32[]{:S(2)}, u32[]{:S(2)}) %all-to-all-start.5) | async-done | bytes 2097184 | tf_op jit(solution)/shard_map/all_to_all | solution.py:106
  1125.5 15.8 %all_gather.59 = f32[64,2048]{1,0:T(8,128)S(1)} all-gather(f32[16,2048]{1,0:T(8,128)S(1)} %pad_maximum_fusion.16), channel_id=1, replica_groups=mesh['gx'=4,'gy'=8] {'gx'}, dimensions={0}, use_global_device_ids=true | all-gather | bytes 655360 | tf_op jit(solution)/shard_map/all_gather | solution.py:466
  (420 shorter events, 344.9 us)
Async XLA Ops:
  7.2 154.2 %copy-start = (bf16[2,4,128,128]{3,2,1,0:T(8,128)(2,1)S(1)}, bf16[2,4,128,128]{3,2,1,0:T(8,128)(2,1)}, u32[]{:S(2)}) copy-start(bf16[2,4,128,128]{3,2,1,0:T(8,128)(2,1)} %param.34) | copy-start | bytes 786436
  7.2 74.1 %copy-start.32 = (bf16[4,512,3,128]{3,1,2,0:T(8,128)(2,1)S(1)}, bf16[4,512,3,128]{3,1,2,0:T(8,128)(2,1)}, u32[]{:S(2)}) copy-start(bf16[4,512,3,128]{3,1,2,0:T(8,128)(2,1)} %param.38) | copy-start | bytes 4718596
  7.2 69.5 %all-gather.15.cloned.1.call-start = ((), (), s32[]{:S(2)}) async-start(), calls=%async_computation.14 | async-start | bytes 3932160 | tf_op jit(solution)/shard_map/all_gather | solution.py:152
  10.4 111.3 %all-gather.17.cloned.1.call-start = ((), (), s32[]{:S(2)}) async-start(), calls=%async_computation.15 | async-start | bytes 1310720 | tf_op jit(solution)/shard_map/all_gather | solution.py:154
  76.8 68.8 %all-gather.13.cloned.1.call-start = ((), (), s32[]{:S(2)}) async-start(), calls=%async_computation.13 | async-start | bytes 5013504 | tf_op jit(solution)/shard_map/all_gather | solution.py:140
  107.8 263.2 %all-to-all-start.1 = ((bf16[4,512,2304]{2,1,0:T(8,128)(2,1)}), bf16[4,512,2304]{2,1,0:T(8,128)(2,1)}, u32[]{:S(2)}, u32[]{:S(2)}) async-start(bf16[4,512,2304]{2,1,0:T(8,128)(2,1)} %pad_maximum_fusion), calls=%async_computation.2 | async-start | bytes 18874368 | tf_op jit(solution)/shard_map/all_to_all | solution.py:112
  113.7 246.5 %all-gather.27.cloned.1.call-start = ((), (), s32[]{:S(2)}) async-start(), calls=%async_computation.23 | async-start | bytes 2621440 | tf_op jit(solution)/shard_map/all_gather | solution.py:103
  121.8 254.0 %reduce-scatter.3.cloned.1.call-start = ((), (), s32[]{:S(2)}) async-start(), calls=%async_computation.16 | async-start | bytes 4718592 | tf_op jit(solution)/shard_map/reduce_scatter | solution.py:268
  360.2 397.5 %copy-start.94 = (s32[4,8,1024]{2,1,0:T(8,128)}, s32[4,8,1024]{2,1,0:T(8,128)S(1)}, u32[]{:S(2)}) copy-start(s32[4,8,1024]{2,1,0:T(8,128)S(1)} %fusion.91) | copy-start | bytes 393220
  371.0 59.5 %all-to-all-start.6 = ((bf16[8,1152,256]{2,1,0:T(8,128)(2,1)}), bf16[8,1152,256]{2,1,0:T(8,128)(2,1)}, u32[]{:S(2)}, u32[]{:S(2)}) async-start(bf16[8,1152,256]{2,1,0:T(8,128)(2,1)} %bitcast.363), calls=%async_computation.7 | async-start | bytes 9437184 | tf_op jit(solution)/shard_map/all_to_all | solution.py:198
  375.7 58.4 %all-gather.25.cloned.1.call-start = ((), (), s32[]{:S(2)}) async-start(), calls=%async_computation.22 | async-start | bytes 2621440 | tf_op jit(solution)/shard_map/all_gather | solution.py:103
  430.5 20.9 %all-to-all-start.2 = ((bf16[4,256,384]{1,2,0:T(8,128)(2,1)}), bf16[4,256,384]{1,2,0:T(8,128)(2,1)S(1)}, u32[]{:S(2)}, u32[]{:S(2)}) async-start(bf16[4,256,384]{1,2,0:T(8,128)(2,1)} %bitcast.49), calls=%async_computation.3 | async-start | bytes 1572864 | tf_op jit(solution)/shard_map/all_to_all | solution.py:112
  451.3 60.0 %all-to-all-start = ((bf16[8,1152,256]{2,1,0:T(8,128)(2,1)}), bf16[8,1152,256]{2,1,0:T(8,128)(2,1)}, u32[]{:S(2)}, u32[]{:S(2)}) async-start(bf16[8,1152,256]{2,1,0:T(8,128)(2,1)} %bitcast.362), calls=%async_computation.1 | async-start | bytes 9437184 | tf_op jit(solution)/shard_map/all_to_all | solution.py:198
  511.3 107.2 %all-to-all-start.3 = ((bf16[4,512,1152]{2,1,0:T(8,128)(2,1)}), bf16[4,512,1152]{2,1,0:T(8,128)(2,1)}, u32[]{:S(2)}, u32[]{:S(2)}) async-start(bf16[4,512,1152]{2,1,0:T(8,128)(2,1)} %pad_maximum_fusion.1), calls=%async_computation.4 | async-start | bytes 9437184 | tf_op jit(solution)/shard_map/all_to_all | solution.py:112
  681.2 76.5 %all-to-all-start.7 = ((bf16[8,1152,256]{2,1,0:T(8,128)(2,1)}), bf16[8,1152,256]{2,1,0:T(8,128)(2,1)}, u32[]{:S(2)}, u32[]{:S(2)}) async-start(bf16[8,1152,256]{2,1,0:T(8,128)(2,1)} %bitcast.364), calls=%async_computation.8 | async-start | bytes 9437184 | tf_op jit(solution)/shard_map/all_to_all | solution.py:205
  686.1 181.6 %all-gather.19.cloned.1.call-start = ((), (), s32[]{:S(2)}) async-start(), calls=%async_computation.17 | async-start | bytes 4718592 | tf_op jit(solution)/shard_map/all_gather | solution.py:351
  686.8 184.2 %all-gather.21.cloned.1.call-start = ((), (), s32[]{:S(2)}) async-start(), calls=%async_computation.18 | async-start | bytes 4718592 | tf_op jit(solution)/shard_map/all_gather | solution.py:354
  821.4 77.4 %all-gather.23.cloned.1.call-start = ((), (), s32[]{:S(2)}) async-start(), calls=%async_computation.19 | async-start | bytes 4718592 | tf_op jit(solution)/shard_map/all_gather | solution.py:352
  842.8 78.7 %all-to-all-start.10 = ((bf16[4,256,384]{1,2,0:T(8,128)(2,1)}), bf16[4,256,384]{1,2,0:T(8,128)(2,1)}, u32[]{:S(2)}, u32[]{:S(2)}) async-start(bf16[4,256,384]{1,2,0:T(8,128)(2,1)} %pad_maximum_fusion.8), calls=%async_computation.12 | async-start | bytes 1572864 | tf_op jit(solution)/shard_map/all_to_all | solution.py:116
  921.5 102.8 %all-to-all-start.4 = ((bf16[8,1152,256]{2,1,0:T(8,128)(2,1)}), bf16[8,1152,256]{2,1,0:T(8,128)(2,1)}, u32[]{:S(2)}, u32[]{:S(2)}) async-start(bf16[8,1152,256]{2,1,0:T(8,128)(2,1)} %bitcast.361), calls=%async_computation.5 | async-start | bytes 9437184 | tf_op jit(solution)/shard_map/all_to_all | solution.py:205
  926.1 81.5 %all-reduce.3.cloned.1.call-start = ((), (), s32[]{:S(2)}) async-start(), calls=%async_computation.20 | async-start | bytes 720896 | tf_op jit(solution)/shard_map/psum | solution.py:406
  1024.3 41.5 %all-to-all-start.9 = ((bf16[4,512,384]{1,2,0:T(8,128)(2,1)}), bf16[4,512,384]{1,2,0:T(8,128)(2,1)S(1)}, u32[]{:S(2)}, u32[]{:S(2)}) async-start(bf16[4,512,384]{1,2,0:T(8,128)(2,1)} %pad_maximum_fusion.4), calls=%async_computation.11 | async-start | bytes 3145728 | tf_op jit(solution)/shard_map/all_to_all | solution.py:116
  1028.9 94.9 %reduce-scatter.5.cloned.1.call-start = ((), (), s32[]{:S(2)}) async-start(), calls=%async_computation.21 | async-start | bytes 4829184 | tf_op jit(solution)/shard_map/reduce_scatter | solution.py:429
  1067.0 51.3 %all-to-all-start.5 = ((bf16[4,1024,256]{2,1,0:T(8,128)(2,1)}), bf16[4,1024,256]{2,1,0:T(8,128)(2,1)S(1)}, u32[]{:S(2)}, u32[]{:S(2)}) async-start(bf16[4,1024,256]{2,1,0:T(8,128)(2,1)} %bitcast_convert_fusion.2), calls=%async_computation.6 | async-start | bytes 4194304 | tf_op jit(solution)/shard_map/all_to_all | solution.py:106
  (101 other events, 1274.7 us)
Sparse Core Ops, SparseCore 0:
  10.5 66.1 all-gather.14
  78.3 26.6 all-gather.16
  107.4 38.0 all-gather.12
  147.0 75.8 all-gather.26
  226.1 138.8 reduce-scatter.2
  377.9 46.3 all-gather.24
  689.0 65.5 all-gather.18
  821.5 37.7 all-gather.20
  861.3 37.4 all-gather.22
  938.0 69.4 all-reduce.2
  1033.6 54.2 reduce-scatter.4

commit v2 on v1

v2 whole, which is shorter than its diff:
```python
import functools
import jax
import jax.numpy as jnp
from jax import lax
from jax.experimental import pallas as pl
from jax.experimental.pallas import tpu as pltpu
from jax.sharding import PartitionSpec as P

RANK = 16
SEQ = 1024
PIECE = 256
CAP = 288
DOWN_PARTS = 2


norm_eps = 1e-05
rope_theta = 10000.0
rank_scale = 0.5
down_scale = 4.0
bf16 = jnp.bfloat16
f32 = jnp.float32
VMEM = pl.BlockSpec(memory_space=pltpu.VMEM)
DMA = pltpu.SemaphoreType.DMA
MESH = pl.DeviceIdType.MESH
SMALL = pl.CostEstimate(flops=0, bytes_accessed=1 << 16, transcendentals=0)
CAP = 288
DOWN_PARTS = 2
SMALL = pl.CostEstimate(flops=0, bytes_accessed=1 << 16, transcendentals=0)


def place_in_column():
    me = lax.axis_index("gy")
    chip, core = lax.div(me, 2), lax.rem(me, 2)
    return me, chip, core, me + 1 - 2 * core


def chip_peer(chip, core, step, chips):
    return lax.rem(chip + step, chips) * 2 + core


def greet_chips(chip, core, sibling, chips):
    barrier = pltpu.get_barrier_semaphore()
    pl.semaphore_signal(barrier, inc=1, device_id={"gy": sibling}, device_id_type=MESH)
    for step in range(1, chips):
        pl.semaphore_signal(
            barrier,
            inc=1,
            device_id={"gy": chip_peer(chip, core, step, chips)},
            device_id_type=MESH,
        )
    pl.semaphore_wait(barrier, chips)


def remote(src, dst, send_sem, recv_sem, target):
    return pltpu.make_async_remote_copy(
        src_ref=src,
        dst_ref=dst,
        send_sem=send_sem,
        recv_sem=recv_sem,
        device_id={"gy": target},
        device_id_type=MESH,
    )


def gather_kernel(chips, x_ref, o_ref, own_sem, send_sem, recv_sem, pass_sem, passed_sem):
    me, chip, core, sibling = place_in_column()
    width = x_ref.shape[1]

    def columns(owner):
        return o_ref.at[:, pl.ds(pl.multiple_of(owner * width, width), width)]

    own = pltpu.make_async_copy(x_ref, columns(me), own_sem)
    own.start()
    greet_chips(chip, core, sibling, chips)
    out = []
    for step in list(range(1, chips)) + [0]:
        target = sibling if step == 0 else chip_peer(chip, core, step, chips)
        copy = remote(x_ref, columns(me), send_sem.at[step], recv_sem.at[step], target)
        copy.start()
        out.append(copy)
    for step in range(1, chips):
        out[step - 1].wait_recv()
        source = chip_peer(chip, core, chips - step, chips)
        copy = remote(
            columns(source), columns(source), pass_sem.at[step], passed_sem.at[step], sibling
        )
        copy.start()
        out.append(copy)
    own.wait()
    out[chips - 1].wait_recv()
    for copy in out[chips:]:
        copy.wait_recv()
    for copy in out:
        copy.wait_send()


def gather_columns(x, groups, collective_id):
    chips = groups // 2
    rows, width = x.shape
    return pl.pallas_call(
        functools.partial(gather_kernel, chips),
        out_shape=jax.ShapeDtypeStruct((rows, groups * width), x.dtype),
        in_specs=[VMEM],
        out_specs=VMEM,
        scratch_shapes=[DMA, DMA((chips,)), DMA((chips,)), DMA((chips,)), DMA((chips,))],
        compiler_params=pltpu.CompilerParams(
            collective_id=collective_id, has_side_effects=True, vmem_limit_bytes=48 << 20
        ),
        cost_estimate=SMALL,
    )(x)


def scatter_kernel(
    chips, tile, l_ref, r_ref, o_ref, part, got, pair, far, part_s, got_s, pair_s, far_s
):
    me, chip, core, sibling = place_in_column()
    rows, width = o_ref.shape
    greet_chips(chip, core, sibling, chips)
    steps = list(range(1, chips)) + [0]

    def product(owner, row):
        chunk = r_ref[pl.ds(pl.multiple_of(owner * width, width), width), :]
        return lax.dot_general(
            l_ref[pl.ds(row, tile), :],
            chunk,
            (((1,), (1,)), ((), ())),
            preferred_element_type=f32,
        )

    copies = []
    for step in steps:
        owner = chip_peer(chip, 1 - core, step, chips)

        @pl.loop(0, rows // tile)
        def _(i, owner=owner, step=step):
            row = pl.multiple_of(i * tile, tile)
            part[step, pl.ds(row, tile), :] = product(owner, row).astype(bf16)

        copy = remote(part.at[step], got.at[step], part_s.at[step], got_s.at[step], sibling)
        copy.start()
        copies.append(copy)
    for step in steps:
        owner = chip_peer(chip, core, step, chips)
        copies[steps.index(step)].wait_recv()

        @pl.loop(0, rows // tile)
        def _(i, owner=owner, step=step):
            row = pl.multiple_of(i * tile, tile)
            total = product(owner, row) + got[step, pl.ds(row, tile), :].astype(f32)
            if step == 0:
                o_ref[pl.ds(row, tile), :] = total
            else:
                pair[step - 1, pl.ds(row, tile), :] = total.astype(bf16)

        if step > 0:
            copy = remote(
                pair.at[step - 1], far.at[step - 1], pair_s.at[step - 1], far_s.at[step - 1], owner
            )
            copy.start()
            copies.append(copy)
    for step in range(1, chips):
        copies[chips + step - 1].wait_recv()

        @pl.loop(0, rows // tile)
        def _(i, step=step):
            row = pl.multiple_of(i * tile, tile)
            o_ref[pl.ds(row, tile), :] += far[step - 1, pl.ds(row, tile), :].astype(f32)

    for copy in copies:
        copy.wait_send()


def scatter_product(left, right, groups, collective_id):
    chips = groups // 2
    rows, inner = left.shape
    width = right.shape[0] // groups
    tile = min(256, rows)
    return pl.pallas_call(
        functools.partial(scatter_kernel, chips, tile),
        out_shape=jax.ShapeDtypeStruct((rows, width), f32),
        in_specs=[VMEM, VMEM],
        out_specs=VMEM,
        scratch_shapes=[
            pltpu.VMEM((chips, rows, width), bf16),
            pltpu.VMEM((chips, rows, width), bf16),
            pltpu.VMEM((chips - 1, rows, width), bf16),
            pltpu.VMEM((chips - 1, rows, width), bf16),
            DMA((chips,)),
            DMA((chips,)),
            DMA((chips - 1,)),
            DMA((chips - 1,)),
        ],
        compiler_params=pltpu.CompilerParams(
            collective_id=collective_id, has_side_effects=True, vmem_limit_bytes=48 << 20
        ),
        cost_estimate=SMALL,
    )(left, right)


def add_kernel(groups, x_ref, o_ref, got, send_sem, recv_sem):
    me = lax.axis_index("gy")
    barrier = pltpu.get_barrier_semaphore()
    for step in range(1, groups):
        target = lax.rem(me + step, groups)
        pl.semaphore_signal(barrier, inc=1, device_id={"gy": target}, device_id_type=MESH)
    pl.semaphore_wait(barrier, groups - 1)
    copies = []
    for step in range(1, groups):
        target = lax.rem(me + step, groups)
        copy = remote(
            x_ref, got.at[step - 1], send_sem.at[step - 1], recv_sem.at[step - 1], target
        )
        copy.start()
        copies.append(copy)
    total = x_ref[...]
    for step in range(1, groups):
        copies[step - 1].wait_recv()
        total = total + got[step - 1]
    o_ref[...] = total
    for copy in copies:
        copy.wait_send()


def add_small(x, groups, collective_id):
    return pl.pallas_call(
        functools.partial(add_kernel, groups),
        out_shape=jax.ShapeDtypeStruct(x.shape, f32),
        in_specs=[VMEM],
        out_specs=VMEM,
        scratch_shapes=[
            pltpu.VMEM((groups - 1,) + x.shape, f32),
            DMA((groups - 1,)),
            DMA((groups - 1,)),
        ],
        compiler_params=pltpu.CompilerParams(collective_id=collective_id, has_side_effects=True),
        cost_estimate=SMALL,
    )(x)


def add_pairs_kernel(
    chips, x_ref, o_ref, got, pair, far, done, got_s, far_s, done_s
):
    me, chip, core, sibling = place_in_column()
    half = x_ref.shape[0] // 2
    greet_chips(chip, core, sibling, chips)
    first = remote(x_ref, got, got_s.at[0], got_s.at[1], sibling)
    first.start()
    first.wait_recv()
    own = pl.ds(pl.multiple_of(core * half, 16), half)
    total = x_ref[own, :].astype(f32) + got[own, :].astype(f32)
    pair[...] = total.astype(bf16)
    copies = []
    for step in range(1, chips):
        copy = remote(
            pair,
            far.at[step - 1],
            far_s.at[0, step - 1],
            far_s.at[1, step - 1],
            chip_peer(chip, core, step, chips),
        )
        copy.start()
        copies.append(copy)
    for step in range(1, chips):
        copies[step - 1].wait_recv()
        total = total + far[step - 1].astype(f32)
    done[own, :] = total.astype(bf16)
    last = remote(done.at[own, :], done.at[own, :], done_s.at[0], done_s.at[1], sibling)
    last.start()
    last.wait_recv()
    o_ref[...] = done[...].astype(f32)
    first.wait_send()
    for copy in copies:
        copy.wait_send()
    last.wait_send()


def add_pairs(x, groups, collective_id):
    chips = groups // 2
    rows, width = x.shape
    return pl.pallas_call(
        functools.partial(add_pairs_kernel, chips),
        out_shape=jax.ShapeDtypeStruct(x.shape, f32),
        in_specs=[VMEM],
        out_specs=VMEM,
        scratch_shapes=[
            pltpu.VMEM(x.shape, bf16),
            pltpu.VMEM((rows // 2, width), bf16),
            pltpu.VMEM((chips - 1, rows // 2, width), bf16),
            pltpu.VMEM(x.shape, bf16),
            DMA((2,)),
            DMA((2, chips - 1)),
            DMA((2,)),
        ],
        compiler_params=pltpu.CompilerParams(collective_id=collective_id, has_side_effects=True),
        cost_estimate=SMALL,
    )(x)


def plane_place(planes_in_set):
    plane = lax.axis_index("gx")
    own = lax.rem(plane, planes_in_set)
    return plane, own, plane - own


def to_plane(src, dst, send_sem, recv_sem, target):
    return pltpu.make_async_remote_copy(
        src_ref=src,
        dst_ref=dst,
        send_sem=send_sem,
        recv_sem=recv_sem,
        device_id={"gx": target},
        device_id_type=MESH,
    )


def greet_all(planes, groups):
    barrier = pltpu.get_barrier_semaphore()
    plane, me = lax.axis_index("gx"), lax.axis_index("gy")

    @pl.loop(1, planes)
    def _(step):
        target = lax.rem(plane + step, planes)
        pl.semaphore_signal(barrier, inc=1, device_id={"gx": target}, device_id_type=MESH)

    @pl.loop(1, groups)
    def _(step):
        target = lax.rem(me + step, groups)
        pl.semaphore_signal(barrier, inc=1, device_id={"gy": target}, device_id_type=MESH)

    pl.semaphore_wait(barrier, planes + groups - 2)


def spread_kernel(
    planes,
    groups,
    in_set,
    x_ref,
    key_ref,
    w_ref,
    o_ref,
    full_ref,
    from_plane,
    picked,
    own_sem,
    w_send,
    w_recv,
    z_send,
    z_recv,
    g_send,
    g_recv,
):
    plane, own, base = plane_place(in_set)
    me = lax.axis_index("gy")
    width = x_ref.shape[1] // 2
    depth, inner = w_ref.shape[1], w_ref.shape[2]
    greet_all(planes, groups)
    z_copies = []
    for step in range(1, in_set):
        copy = to_plane(
            x_ref,
            from_plane.at[step - 1],
            z_send.at[step - 1],
            z_recv.at[step - 1],
            base + lax.rem(own + step, in_set),
        )
        copy.start()
        z_copies.append(copy)
    mine = full_ref.at[pl.ds(pl.multiple_of(plane * depth, depth), depth), pl.ds(0, inner)]
    own_copy = pltpu.make_async_copy(w_ref.at[own], mine, own_sem)
    own_copy.start()
    w_copies = []
    for step in range(1, planes):
        target = lax.rem(plane + step, planes)
        copy = to_plane(
            w_ref.at[lax.rem(target, in_set)],
            mine,
            w_send.at[step - 1],
            w_recv.at[step - 1],
            target,
        )
        copy.start()
        w_copies.append(copy)

    def sent(step, turn):
        target = lax.rem(me + turn, groups)
        return remote(
            picked.at[step, turn],
            o_ref.at[
                :,
                pl.ds(step * CAP, CAP),
                pl.ds(pl.multiple_of(me * width, width), width),
            ],
            g_send.at[step, turn],
            g_recv.at[step, turn],
            target,
        )

    for step in range(in_set):
        if step:
            z_copies[step - 1].wait_recv()
        block = from_plane.at[step - 1] if step else x_ref

        def choose(target):
            key = key_ref[step, pl.ds(target, 1), :]
            slot = lax.broadcasted_iota(jnp.int32, (CAP, key.shape[1]), 0)
            pick = jnp.where(slot == key, 1.0, 0.0).astype(bf16)
            return jnp.dot(pick, block[...], preferred_element_type=f32).astype(bf16)

        @pl.loop(1, groups)
        def _(turn, step=step, choose=choose):
            rows = choose(lax.rem(me + turn, groups))
            picked[step, turn, 0] = rows[:, :width]
            picked[step, turn, 1] = rows[:, width:]
            sent(step, turn).start()

        rows = choose(me)
        columns = pl.ds(pl.multiple_of(me * width, width), width)
        o_ref[0, pl.ds(step * CAP, CAP), columns] = rows[:, :width]
        o_ref[1, pl.ds(step * CAP, CAP), columns] = rows[:, width:]

    for step in range(in_set):

        @pl.loop(1, groups)
        def _(turn, step=step):
            copy = sent(step, turn)
            copy.wait_recv()
            copy.wait_send()

    for copy in z_copies:
        copy.wait_send()
    own_copy.wait()
    for copy in w_copies:
        copy.wait_recv()
        copy.wait_send()


def spread(x, key, weight, planes, groups, pad_to, collective_id):
    in_set, depth, inner = weight.shape
    rows, two = x.shape
    width = two // 2
    return pl.pallas_call(
        functools.partial(spread_kernel, planes, groups, in_set),
        out_shape=(
            jax.ShapeDtypeStruct((2, in_set * CAP, groups * width), bf16),
            jax.ShapeDtypeStruct((planes * depth, pad_to), bf16),
        ),
        in_specs=[VMEM, VMEM, pl.BlockSpec(memory_space=pl.ANY)],
        out_specs=(VMEM, pl.BlockSpec(memory_space=pl.ANY)),
        scratch_shapes=[
            pltpu.VMEM((in_set - 1, rows, two), bf16),
            pltpu.VMEM((in_set, groups, 2, CAP, width), bf16),
            DMA,
            DMA((planes - 1,)),
            DMA((planes - 1,)),
            DMA((in_set - 1,)),
            DMA((in_set - 1,)),
            DMA((in_set, groups)),
            DMA((in_set, groups)),
        ],
        compiler_params=pltpu.CompilerParams(
            collective_id=collective_id, has_side_effects=True, vmem_limit_bytes=48 << 20
        ),
        cost_estimate=SMALL,
    )(x, key, weight)


def collect_kernel(
    planes,
    groups,
    in_set,
    tile,
    u_ref,
    m_ref,
    key_ref,
    shard_ref,
    rows_ref,
    placed_ref,
    got,
    other,
    out_z,
    in_z,
    low,
    g_send,
    g_recv,
    own_sem,
    m_sem,
    z_send,
    z_recv,
    c_own,
    c_send,
    c_recv,
    p_send,
    p_recv,
):
    plane, own, base = plane_place(in_set)
    me, chip, core, sibling = place_in_column()
    chips = groups // 2
    rows, width = shard_ref.shape
    greet_all(planes, groups)
    order = list(range(1, in_set)) + [0]

    def block_of(step, owner):
        return u_ref.at[
            pl.ds(step * CAP, CAP), pl.ds(pl.multiple_of(owner * width, width), width)
        ]

    def slots_of(buffer, step, owner):
        return buffer.at[step, pl.ds(pl.multiple_of(owner * CAP, 16), CAP), :]

    def sent(step, turn):
        target = lax.rem(me + turn, groups)
        return remote(
            block_of(step, target),
            slots_of(got, step, me),
            g_send.at[step, turn],
            g_recv.at[step, turn],
            target,
        )

    def own_copy(step):
        return pltpu.make_async_copy(block_of(step, me), slots_of(got, step, me), own_sem.at[step])

    def other_copy(step, owner):
        return pltpu.make_async_copy(
            m_ref.at[owner, pl.ds(step * CAP, CAP), :],
            slots_of(other, step, owner),
            m_sem.at[step, owner],
        )

    for step in order:

        @pl.loop(1, groups)
        def _(turn, step=step):
            sent(step, turn).start()

        own_copy(step).start()

    for step in order:

        @pl.loop(0, groups)
        def _(owner, step=step):
            other_copy(step, owner).start()

    def placed(step, row, buffer):
        keys = key_ref[step, pl.ds(row, tile), :]
        pieces = []
        for start in range(0, groups * CAP, 128):
            slot = lax.broadcasted_iota(jnp.int32, (tile, 128), 1) + start
            hit = None
            for owner in range(start // CAP, min(groups, (start + 127) // CAP + 1)):
                same = slot == keys[:, owner : owner + 1]
                hit = same if hit is None else hit | same
            pieces.append(jnp.where(hit, 1.0, 0.0).astype(bf16))
        return jnp.dot(
            jnp.concatenate(pieces, axis=1), buffer[step], preferred_element_type=f32
        )

    for step in order:

        @pl.loop(0, groups)
        def _(owner, step=step):
            other_copy(step, owner).wait()

        @pl.loop(0, rows // tile)
        def _(i, step=step):
            row = pl.multiple_of(i * tile, tile)
            placed_ref[step, pl.ds(row, tile), :] = placed(step, row, other).astype(bf16)

    z_copies = []
    for step in order:
        own_copy(step).wait()

        @pl.loop(1, groups)
        def _(turn, step=step):
            sent(step, turn).wait_recv()

        @pl.loop(0, rows // tile)
        def _(i, step=step):
            row = pl.multiple_of(i * tile, tile)
            total = placed(step, row, got)
            if step:
                out_z[step - 1, pl.ds(row, tile), :] = total.astype(bf16)
            else:
                shard_ref[pl.ds(row, tile), :] = total

        if step:
            copy = to_plane(
                out_z.at[step - 1],
                in_z.at[step - 1],
                z_send.at[step - 1],
                z_recv.at[step - 1],
                base + lax.rem(own - step + in_set, in_set),
            )
            copy.start()
            z_copies.append(copy)
    for copy in z_copies:
        copy.wait_recv()

    @pl.loop(0, rows // tile)
    def _(i):
        row = pl.multiple_of(i * tile, tile)
        total = shard_ref[pl.ds(row, tile), :]
        for step in range(1, in_set):
            total = total + in_z[step - 1, pl.ds(row, tile), :].astype(f32)
        shard_ref[pl.ds(row, tile), :] = total
        low[pl.ds(row, tile), :] = total.astype(bf16)

    def columns(owner):
        return rows_ref.at[:, pl.ds(pl.multiple_of(owner * width, width), width)]

    mine = pltpu.make_async_copy(low, columns(me), c_own)
    mine.start()
    out = []
    for step in list(range(1, chips)) + [0]:
        target = sibling if step == 0 else chip_peer(chip, core, step, chips)
        copy = remote(low, columns(me), c_send.at[step], c_recv.at[step], target)
        copy.start()
        out.append(copy)
    for step in range(1, chips):
        out[step - 1].wait_recv()
        source = chip_peer(chip, core, chips - step, chips)
        copy = remote(
            columns(source), columns(source), p_send.at[step], p_recv.at[step], sibling
        )
        copy.start()
        out.append(copy)
    mine.wait()
    out[chips - 1].wait_recv()
    for copy in out[chips:]:
        copy.wait_recv()
    for copy in out + z_copies:
        copy.wait_send()
    for step in order:

        @pl.loop(1, groups)
        def _(turn, step=step):
            sent(step, turn).wait_send()


def collect(u, other, key, planes, groups, collective_id):
    in_set, rows = key.shape[0], key.shape[1]
    slot_total, full = u.shape
    width = full // groups
    chips = groups // 2
    tile = min(256, rows)
    return pl.pallas_call(
        functools.partial(collect_kernel, planes, groups, in_set, tile),
        out_shape=(
            jax.ShapeDtypeStruct((rows, width), f32),
            jax.ShapeDtypeStruct((rows, full), bf16),
            jax.ShapeDtypeStruct((in_set, rows, width), bf16),
        ),
        in_specs=[VMEM, pl.BlockSpec(memory_space=pl.ANY), VMEM],
        out_specs=(VMEM, VMEM, VMEM),
        scratch_shapes=[
            pltpu.VMEM((in_set, groups * CAP, width), bf16),
            pltpu.VMEM((in_set, groups * CAP, width), bf16),
            pltpu.VMEM((in_set - 1, rows, width), bf16),
            pltpu.VMEM((in_set - 1, rows, width), bf16),
            pltpu.VMEM((rows, width), bf16),
            DMA((in_set, groups)),
            DMA((in_set, groups)),
            DMA((in_set,)),
            DMA((in_set, groups)),
            DMA((in_set - 1,)),
            DMA((in_set - 1,)),
            DMA,
            DMA((chips,)),
            DMA((chips,)),
            DMA((chips,)),
            DMA((chips,)),
        ],
        compiler_params=pltpu.CompilerParams(
            collective_id=collective_id, has_side_effects=True, vmem_limit_bytes=48 << 20
        ),
        cost_estimate=SMALL,
    )(u, other, key)


def planes_kernel(planes, x_ref, o_ref, own_sem, send_sem, recv_sem):
    plane = lax.axis_index("gx")
    barrier = pltpu.get_barrier_semaphore()
    own = pltpu.make_async_copy(x_ref, o_ref.at[plane], own_sem)
    own.start()
    for step in range(1, planes):
        target = lax.rem(plane + step, planes)
        pl.semaphore_signal(barrier, inc=1, device_id={"gx": target}, device_id_type=MESH)
    pl.semaphore_wait(barrier, planes - 1)
    copies = []
    for step in range(1, planes):
        copy = to_plane(
            x_ref,
            o_ref.at[plane],
            send_sem.at[step - 1],
            recv_sem.at[step - 1],
            lax.rem(plane + step, planes),
        )
        copy.start()
        copies.append(copy)
    own.wait()
    for copy in copies:
        copy.wait_recv()
        copy.wait_send()


def gather_planes(x, planes, collective_id):
    return pl.pallas_call(
        functools.partial(planes_kernel, planes),
        out_shape=jax.ShapeDtypeStruct((planes,) + x.shape, x.dtype),
        in_specs=[VMEM],
        out_specs=VMEM,
        scratch_shapes=[DMA, DMA((planes - 1,)), DMA((planes - 1,))],
        compiler_params=pltpu.CompilerParams(collective_id=collective_id, has_side_effects=True),
        cost_estimate=SMALL,
    )(x)


def rope_tables(length, width):
    half_width = width // 2
    frequency = rope_theta ** (-2.0 * jnp.arange(half_width, dtype=f32) / width)
    angles = jnp.arange(length, dtype=f32)[:, None] * frequency[None, :]
    return (jnp.cos(angles), jnp.sin(angles))


def apply_rotary(values, cosine, sine):
    half_width = values.shape[-1] // 2
    first = values[..., :half_width]
    second = values[..., half_width:]
    return jnp.concatenate(
        [first * cosine - second * sine, second * cosine + first * sine], axis=-1
    )


def unrotate(grads, cosine, sine):
    half_width = grads.shape[-1] // 2
    first = grads[..., :half_width]
    second = grads[..., half_width:]
    return jnp.concatenate(
        [first * cosine + second * sine, second * cosine - first * sine], axis=-1
    )


def allowed_mask(piece_starts):
    places = jnp.arange(SEQ, dtype=jnp.int32)
    causal = places[None, :] <= places[:, None]
    inside = (places[None, None, :] >= piece_starts[:, :, None]) & (
        places[None, None, :] < piece_starts[:, :, None] + PIECE
    )
    same_piece = jnp.any(inside[:, :, :, None] & inside[:, :, None, :], axis=1)
    return causal[None] | same_piece


def dot(spec, left, right):
    return jnp.einsum(spec, left, right, preferred_element_type=f32)


def after(first, *later):
    return lax.optimization_barrier((first,) + later)[1:]


def shards(
    block_input,
    out_grad,
    routes,
    adapter_ids,
    piece_starts,
    attn_gain,
    qk_gain,
    mlp_gain,
    w_qkv,
    w_out,
    a_qkv,
    b_out,
    head_pack,
    router,
    w_gate_up,
    w_down,
    exp_wide,
    exp_hidden,
):
    planes = lax.axis_size("gx")
    groups = lax.axis_size("gy")
    plane = lax.axis_index("gx")
    column = lax.axis_index("gy")
    rows, width_local = block_input.shape
    width = width_local * groups
    heads_local = head_pack.shape[0]
    rank_cols = head_pack.shape[2]
    head_width = head_pack.shape[3]
    experts_local = w_gate_up.shape[0]
    hidden_width = w_gate_up.shape[3]
    nseq = adapter_ids.shape[0]
    inv_root = head_width ** (-0.5)
    repeats = planes // experts_local
    steps = range(experts_local)
    own = lax.rem(plane, experts_local)

    def shifted(x, step):
        if step % experts_local == 0:
            return x
        pairs = []
        for p in range(planes):
            base = p // experts_local * experts_local
            pairs.append((p, base + (p - base + step) % experts_local))
        return lax.ppermute(x, "gx", pairs)

    def own_pieces(piece_for):
        pieces = []
        for step in range(planes):
            piece = piece_for(lax.rem(plane + step, planes))
            if step:
                pairs = [(p, (p + step) % planes) for p in range(planes)]
                piece = lax.ppermute(piece, "gx", pairs)
            pieces.append((lax.rem(plane - step + planes, planes), piece))
        return pieces

    def assembled(pieces, buffer, start=0):
        for source, piece in pieces:
            buffer = lax.dynamic_update_slice(buffer, piece, (source * piece.shape[0], start))
        return buffer

    compact = nseq * RANK

    def pick(x, axis):
        return jnp.concatenate(
            [
                lax.dynamic_slice_in_dim(x, adapter_ids[n] * RANK, RANK, axis=axis)
                for n in range(nseq)
            ],
            axis=axis,
        )

    token_seq = jnp.arange(rows, dtype=jnp.int32) // SEQ
    col_seq = jnp.arange(compact, dtype=jnp.int32) // RANK
    compact_mask = (token_seq[:, None] == col_seq[None, :]).astype(f32)
    a_pick = pick(a_qkv, 2)
    b_pick = pick(b_out, 0)
    pack_pick = pick(head_pack, 2)

    routes_all = lax.all_gather(routes, "gx", axis=0, tiled=False)
    adapters_all = lax.all_gather(adapter_ids, "gx", axis=0, tiled=False)
    dl = w_gate_up.shape[1]
    hl = exp_hidden.shape[1]
    qkv_width = 3 * heads_local * head_width
    weight_shard = jnp.concatenate(
        [
            w_qkv.reshape(w_qkv.shape[0], qkv_width),
            w_out.reshape(heads_local * head_width, w_out.shape[2]).T,
        ],
        axis=1,
    )
    attn_weight = lax.all_gather(weight_shard, "gx", axis=0, tiled=True)
    gathered = gather_columns(
        jnp.concatenate(
            [block_input, a_pick.transpose(0, 2, 1).reshape(3 * compact, width_local), b_pick],
            axis=0,
        ),
        groups,
        1,
    )
    full_rows = gathered[:rows]
    a_full = gathered[rows : rows + 3 * compact]
    b_full = gathered[rows + 3 * compact :]

    set_cols = experts_local * compact
    fold = max(1, 128 // set_cols)
    sets_adapters = adapters_all.reshape(repeats, experts_local * nseq)
    rank_index = jnp.arange(rank_cols, dtype=jnp.int32)
    set_index = jnp.arange(set_cols, dtype=jnp.int32)
    set_pick = (
        (rank_index // RANK)[None, :, None] == jnp.repeat(sets_adapters, RANK, axis=1)[:, None, :]
    ) & ((rank_index % RANK)[None, :, None] == (set_index % RANK)[None, None, :])
    set_pick = set_pick.astype(bf16)

    def folded(x):
        return jnp.concatenate(jnp.split(x, fold, axis=1), axis=2)

    def unfolded(x):
        return jnp.concatenate(jnp.split(x, fold, axis=2), axis=1)

    rank_rows = jnp.concatenate(
        [exp_wide[:, :, c] for c in range(3)] + [exp_hidden[:, :, c] for c in range(3)], axis=1
    )
    rank_shard = folded(
        dot("emr,srk->semk", rank_rows, set_pick)
        .reshape(planes, rank_rows.shape[1], set_cols)
        .astype(bf16)
    )
    (rank_shard,) = after(attn_weight, rank_shard)
    rank_weight = unfolded(lax.all_to_all(rank_shard, "gx", 0, 0, tiled=True))
    down_pieces = []
    waited = attn_weight
    part_rows = dl // DOWN_PARTS
    for part in range(DOWN_PARTS):
        (down_later,) = after(waited, w_down)
        pieces = own_pieces(
            lambda p: lax.dynamic_slice(
                down_later,
                (lax.rem(p, experts_local), part * part_rows, 0),
                (1, part_rows, hidden_width),
            )[0]
        )
        waited = tuple(piece for _, piece in pieces)
        down_pieces.append(pieces)

    def rank_part(start, count):
        return rank_weight[:, start : start + count].reshape(planes * count, set_cols)

    wide_parts = [rank_part(c * dl, dl) for c in range(3)]
    hidden_gate, hidden_up, hidden_down = [rank_part(3 * dl + c * hl, hl) for c in range(3)]
    rank_end = 2 * hidden_width + 2 * set_cols
    second_weight = jnp.zeros((width, hidden_width + set_cols), bf16)
    second_weight = lax.dynamic_update_slice(second_weight, wide_parts[2], (0, hidden_width))
    for part, pieces in enumerate(down_pieces):
        for source, piece in pieces:
            second_weight = lax.dynamic_update_slice(
                second_weight, piece, (source * dl + part * part_rows, 0)
            )

    expert_ids = own + experts_local * jnp.arange(groups, dtype=jnp.int32)
    set_start = (plane // experts_local) * experts_local
    step_plane = lax.rem(own - jnp.arange(experts_local) + experts_local, experts_local)
    routes_set = routes_all[set_start + step_plane]
    hits = jnp.any(routes_set[:, :, :, None] == expert_ids, axis=2)
    order = jnp.arange(rows, dtype=jnp.int32)
    earlier = (order[None, :] < order[:, None]).astype(bf16)
    places = dot("ts,gsc->gct", earlier, hits.astype(bf16))
    slot_key = jnp.where(hits.transpose(0, 2, 1), places.astype(jnp.int32), -1)
    slots = jnp.arange(CAP, dtype=jnp.int32)
    column_key = slot_key + CAP * jnp.arange(groups, dtype=jnp.int32)[None, :, None]
    column_key = jnp.where(slot_key >= 0, column_key, -1).transpose(0, 2, 1)
    own_key = lax.dynamic_index_in_dim(slot_key, column, 1, keepdims=False)
    own_pick = (own_key[:, None, :] == slots[None, :, None]).astype(bf16)
    rank_mask = (
        (step_plane[:, None] * nseq + token_seq[None, :])[:, :, None]
        == (set_index // RANK)[None, None, :]
    ).astype(bf16)
    slot_total = experts_local * CAP
    mask_slot = dot("gst,gtr->gsr", own_pick, rank_mask).reshape(slot_total, set_cols)
    valid = jnp.max(mask_slot, axis=1)

    col_start = column * width_local
    first_norm_gain = lax.dynamic_slice_in_dim(attn_gain, col_start, width_local)
    input_f = full_rows.astype(f32)
    scale_one = lax.rsqrt(jnp.mean(input_f * input_f, axis=-1, keepdims=True) + norm_eps)
    hat_one = input_f * scale_one
    normed_bf = (hat_one * attn_gain).astype(bf16)
    base = dot("td,de->te", normed_bf, attn_weight[:, :qkv_width]).reshape(
        rows, heads_local, 3, head_width
    )
    rank_in = dot("td,kd->tk", normed_bf, a_full).reshape(rows, 3, compact)
    rank_low = (rank_in * compact_mask[:, None, :]).astype(bf16)
    projected = base + rank_scale * dot("tcr,hcre->thce", rank_low, pack_pick[:, :3])
    query_pre = projected[:, :, 0]
    key_pre = projected[:, :, 1]
    value_bf = projected[:, :, 2].astype(bf16)
    square_sums = jnp.stack(
        [jnp.sum(query_pre * query_pre, axis=(1, 2)), jnp.sum(key_pre * key_pre, axis=(1, 2))]
    )
    square_sums = add_small(square_sums.reshape(-1, 128), groups, 2).reshape(2, rows)
    query_scale = lax.rsqrt(square_sums[0] / width + norm_eps)[:, None, None]
    key_scale = lax.rsqrt(square_sums[1] / width + norm_eps)[:, None, None]
    head_start = column * heads_local * head_width
    gains_local = lax.dynamic_slice_in_dim(
        qk_gain, head_start, heads_local * head_width, axis=1
    ).reshape(2, heads_local, head_width)
    query_hat = query_pre * query_scale
    key_hat = key_pre * key_scale
    cosine, sine = rope_tables(SEQ, head_width)
    cosine = cosine[None, :, None, :]
    sine = sine[None, :, None, :]
    query_bf = apply_rotary(
        (query_hat * gains_local[0]).reshape(nseq, SEQ, heads_local, head_width), cosine, sine
    ).astype(bf16)
    key_bf = apply_rotary(
        (key_hat * gains_local[1]).reshape(nseq, SEQ, heads_local, head_width), cosine, sine
    ).astype(bf16)
    values_seq = value_bf.reshape(nseq, SEQ, heads_local, head_width)
    allowed = allowed_mask(piece_starts)[:, None]
    scores = dot("nqhe,nkhe->nhqk", query_bf, key_bf) * inv_root
    scores = jnp.where(allowed, scores, -1e30)
    row_peak = jnp.max(scores, axis=-1, keepdims=True)
    raised = jnp.exp(scores - row_peak)
    row_total = jnp.sum(raised, axis=-1, keepdims=True)
    log_total = row_peak + jnp.log(row_total)
    weights = raised / row_total
    attended = dot("nhqk,nkhe->nqhe", weights.astype(bf16), values_seq)
    attn_bf = attended.reshape(rows, heads_local, head_width).astype(bf16)
    rank_out = dot("the,hre->thr", attn_bf, pack_pick[:, 3])
    rank_out_low = (rank_out * compact_mask[:, None, :]).astype(bf16)
    out_weight = attn_weight[:, qkv_width:]
    b_turned = (rank_scale * b_full.T).astype(bf16)
    branch = scatter_product(
        jnp.concatenate(
            [
                attn_bf.reshape(rows, heads_local * head_width),
                rank_out_low.reshape(rows, heads_local * compact),
            ],
            axis=1,
        ),
        jnp.concatenate([out_weight] + [b_turned] * heads_local, axis=1),
        groups,
        3,
    )
    middle = block_input.astype(f32) + branch
    middle_low = middle.astype(bf16)

    (spread_rows,) = after(waited, jnp.concatenate([middle_low, out_grad], axis=1))
    slot_rows, first_weight = spread(
        spread_rows,
        slot_key,
        w_gate_up.reshape(experts_local, dl, 2 * hidden_width),
        planes,
        groups,
        rank_end + 2 * router.shape[1],
        4,
    )
    middle_slot, grad_slot = slot_rows[0], slot_rows[1]
    first_weight = lax.dynamic_update_slice(
        first_weight,
        jnp.concatenate([wide_parts[0], wide_parts[1], router, router], axis=1),
        (0, 2 * hidden_width),
    )
    both_rows = lax.all_gather(
        jnp.concatenate([middle_low, out_grad], axis=0), "gy", axis=1, tiled=True
    )
    middle_slot = middle_slot.astype(f32)
    slot_scale = lax.rsqrt(jnp.mean(middle_slot * middle_slot, axis=-1, keepdims=True) + norm_eps)
    expert_in = (middle_slot * slot_scale * mlp_gain).astype(bf16)
    pre_wide = jnp.dot(expert_in, first_weight, preferred_element_type=f32)
    logits = pre_wide[:, rank_end : rank_end + router.shape[1]]
    logit_raised = jnp.exp(logits - jnp.max(logits, axis=-1, keepdims=True))
    route_probs = logit_raised / jnp.sum(logit_raised, axis=-1, keepdims=True)
    own_id = column * experts_local + own
    is_own = (jnp.arange(router.shape[1], dtype=jnp.int32) == own_id).astype(f32)[None, :]
    gate = jnp.sum(route_probs * is_own, axis=1, keepdims=True) * valid[:, None]
    two_masks = jnp.concatenate([mask_slot, mask_slot], axis=1)
    rank_gu_low = (pre_wide[:, 2 * hidden_width : rank_end] * two_masks).astype(bf16)
    gate_pre = pre_wide[:, :hidden_width] + rank_scale * dot(
        "sr,fr->sf", rank_gu_low[:, :set_cols], hidden_gate
    )
    up_pre = pre_wide[:, hidden_width : 2 * hidden_width] + rank_scale * dot(
        "sr,fr->sf", rank_gu_low[:, set_cols:], hidden_up
    )
    sigma = jax.nn.sigmoid(gate_pre)
    activated = gate_pre * sigma
    inner_bf = (activated * up_pre).astype(bf16)
    rank_down = dot("sf,fr->sr", inner_bf, hidden_down)
    rank_down_low = (rank_down * mask_slot).astype(bf16)
    inner_wide = jnp.concatenate([inner_bf, (down_scale * rank_down_low).astype(bf16)], axis=1)
    expert_output = dot("sf,df->sd", inner_wide, second_weight)
    grad_slot_f = grad_slot.astype(f32)
    gate_grad = jnp.sum(grad_slot_f * expert_output, axis=-1, keepdims=True)
    out_grad_bf = (gate * grad_slot_f).astype(bf16)
    inner_wide_grad = dot("sd,df->sf", out_grad_bf, second_weight)
    rank_down_grad = (down_scale * inner_wide_grad[:, hidden_width:] * mask_slot).astype(bf16)
    inner_grad = inner_wide_grad[:, :hidden_width] + dot("sr,fr->sf", rank_down_grad, hidden_down)
    gate_pre_grad = (inner_grad * up_pre * sigma * (1.0 + gate_pre * (1.0 - sigma))).astype(bf16)
    up_pre_grad = (inner_grad * activated).astype(bf16)
    rank_gu_grad = (
        rank_scale
        * jnp.concatenate(
            [
                dot("sf,fr->sr", gate_pre_grad, hidden_gate),
                dot("sf,fr->sr", up_pre_grad, hidden_up),
            ],
            axis=1,
        )
        * two_masks
    ).astype(bf16)
    logit_grad = (is_own - route_probs) * (gate * gate_grad)
    logit_high = logit_grad.astype(bf16)
    logit_rest = (logit_grad - logit_high.astype(f32)).astype(bf16)
    pre_wide_grad = jnp.concatenate(
        [gate_pre_grad, up_pre_grad, rank_gu_grad, logit_high, logit_rest], axis=1
    )
    rows_grad = dot("sf,df->sd", pre_wide_grad, first_weight)
    weighted = (gate * expert_output).astype(bf16)
    weighted = weighted.reshape(slot_total, groups, width_local).transpose(1, 0, 2)
    normed_two_part, normed_two_rows, moe_planes = collect(
        rows_grad.astype(bf16),
        lax.all_to_all(weighted, "gy", 0, 0, tiled=True),
        column_key,
        planes,
        groups,
        5,
    )
    moe_part = moe_planes[0].astype(f32)
    for step in range(1, experts_local):
        moe_part = moe_part + shifted(moe_planes[step], experts_local - step).astype(f32)
    layer_out = (middle + moe_part).astype(bf16)

    wide_grads = [
        dot("sd,sr->dr", expert_in, rank_gu_grad[:, :set_cols]),
        dot("sd,sr->dr", expert_in, rank_gu_grad[:, set_cols:]),
        down_scale * dot("sd,sr->dr", out_grad_bf, rank_down_low),
    ]
    hidden_grads = [
        rank_scale * dot("sf,sr->fr", gate_pre_grad, rank_gu_low[:, :set_cols]),
        rank_scale * dot("sf,sr->fr", up_pre_grad, rank_gu_low[:, set_cols:]),
        dot("sf,sr->fr", inner_bf, rank_down_grad),
    ]
    rank_grads = jnp.concatenate(
        [x.astype(bf16).reshape(planes, dl, set_cols) for x in wide_grads]
        + [x.astype(bf16).reshape(planes, hl, set_cols) for x in hidden_grads],
        axis=1,
    )
    (rank_grads,) = after(normed_two_rows, rank_grads)
    rank_grads = unfolded(lax.all_to_all(folded(rank_grads), "gx", 0, 0, tiled=True))
    rank_grads = rank_grads.reshape((repeats, experts_local) + rank_grads.shape[1:])
    wide_sum = jnp.stack(
        [
            dot("semk,srk->emr", rank_grads[:, :, c * dl : (c + 1) * dl], set_pick)
            for c in range(3)
        ],
        axis=2,
    )
    hidden_sum = jnp.stack(
        [
            dot(
                "semk,srk->emr",
                rank_grads[:, :, 3 * dl + c * hl : 3 * dl + (c + 1) * hl],
                set_pick,
            )
            for c in range(3)
        ],
        axis=2,
    )

    middle_rows = both_rows[:rows].astype(f32)
    grad_rows = both_rows[rows:].astype(f32)
    scale_two = lax.rsqrt(jnp.mean(middle_rows * middle_rows, axis=-1, keepdims=True) + norm_eps)
    normed_two_grad = normed_two_rows.astype(f32)
    hat_two = middle_rows * scale_two
    scaled_two = normed_two_grad * mlp_gain
    stat_two = jnp.mean(scaled_two * hat_two, axis=-1, keepdims=True)
    branch_rows = (grad_rows + scale_two * (scaled_two - hat_two * stat_two)).astype(bf16)
    gain_two_local = lax.dynamic_slice_in_dim(mlp_gain, col_start, width_local)
    middle_grad = out_grad.astype(f32) + scale_two * (
        normed_two_part * gain_two_local - middle_low.astype(f32) * scale_two * stat_two
    )
    rank_out_grad = rank_scale * dot("td,rd->tr", branch_rows, b_full)
    rank_out_bf = (rank_out_grad * compact_mask).astype(bf16)
    pack_out_grad = dot("the,tr->hre", attn_bf, rank_out_bf)
    attention_gradient = dot("td,de->te", branch_rows, out_weight).reshape(
        rows, heads_local, head_width
    ) + dot(
        "tr,hre->the", rank_out_bf, pack_pick[:, 3]
    )
    attn_grad_bf = attention_gradient.reshape(nseq, SEQ, heads_local, head_width).astype(bf16)
    scores_again = dot("nqhe,nkhe->nhqk", query_bf, key_bf) * inv_root
    scores_again = jnp.where(allowed, scores_again, -1e30)
    weights_again = jnp.exp(scores_again - log_total)
    value_grad = dot("nhqk,nqhe->nkhe", weights_again.astype(bf16), attn_grad_bf)
    weight_grad = dot("nqhe,nkhe->nhqk", attn_grad_bf, values_seq)
    row_dot = jnp.sum(weight_grad * weights_again, axis=-1, keepdims=True)
    score_grad = (weights_again * (weight_grad - row_dot)).astype(bf16)
    query_grad = dot("nhqk,nkhe->nqhe", score_grad, key_bf) * inv_root
    key_grad = dot("nhqk,nqhe->nkhe", score_grad, query_bf) * inv_root
    query_hat_grad = (
        unrotate(query_grad, cosine, sine).reshape(rows, heads_local, head_width) * gains_local[0]
    )
    key_hat_grad = (
        unrotate(key_grad, cosine, sine).reshape(rows, heads_local, head_width) * gains_local[1]
    )
    value_pre_grad = value_grad.reshape(rows, heads_local, head_width)
    stat_query = jnp.sum(query_hat_grad * query_hat, axis=(1, 2))
    stat_key = jnp.sum(key_hat_grad * key_hat, axis=(1, 2))

    def rank_terms(values, which):
        return dot("the,hre->rt", values.astype(bf16), pack_pick[:, which])

    sums = jnp.concatenate(
        [
            rank_terms(query_hat_grad, 0),
            rank_terms(key_hat_grad, 1),
            rank_terms(value_pre_grad, 2),
            rank_terms(query_hat, 0),
            rank_terms(key_hat, 1),
            jnp.sum(rank_out_low.astype(f32), axis=1).T,
            jnp.stack([stat_query, stat_key]),
        ],
        axis=0,
    )
    padding = -sums.shape[0] % 32
    sums = add_pairs(jnp.pad(sums.astype(bf16), ((0, padding), (0, 0))), groups, 6)
    first_total = sums[: 3 * compact].reshape(3, compact, rows)
    second_total = sums[3 * compact : 5 * compact].reshape(2, compact, rows)
    mean_qk = sums[6 * compact : 6 * compact + 2] / width
    branch_local = lax.dynamic_slice_in_dim(branch_rows, col_start, width_local, axis=1)
    b_out_sum = rank_scale * dot(
        "rt,td->rd", sums[5 * compact : 6 * compact].astype(bf16), branch_local
    )
    scales_qk = jnp.stack([query_scale[:, 0, 0], key_scale[:, 0, 0]])
    rank_qk = scales_qk[:, None, :] * (first_total[:2] - second_total * mean_qk[:, None, :])
    rank_grad_full = rank_scale * jnp.concatenate([rank_qk, first_total[2:]], axis=0)
    rank_grad_bf = (rank_grad_full * compact_mask.T[None]).astype(bf16)
    query_pre_grad = query_scale * (query_hat_grad - query_hat * mean_qk[0][:, None, None])
    key_pre_grad = key_scale * (key_hat_grad - key_hat * mean_qk[1][:, None, None])
    pre_grad = jnp.stack([query_pre_grad, key_pre_grad, value_pre_grad], axis=2).astype(bf16)
    pack_b_grad = rank_scale * dot("tcr,thce->rhce", rank_low, pre_grad)
    normed_one_grad = scatter_product(
        pre_grad.reshape(rows, qkv_width), attn_weight[:, :qkv_width], groups, 7
    )
    adapter_input_gradient = dot("crt,cdr->td", rank_grad_bf, a_pick)
    first_normalized_shard = lax.dynamic_slice_in_dim(hat_one, col_start, width_local, axis=1)
    normed_local_bf = lax.dynamic_slice_in_dim(normed_bf, col_start, width_local, axis=1)
    a_rows_grad = dot("td,crt->rcd", normed_local_bf, rank_grad_bf)
    scaled_one = (normed_one_grad + adapter_input_gradient) * first_norm_gain
    stat_one = jnp.sum(scaled_one * first_normalized_shard, axis=-1)
    stat_one_sum = add_small(stat_one.reshape(-1, 128), groups, 8).reshape(rows, 1)
    input_grad = middle_grad + scale_one * (
        scaled_one - first_normalized_shard * stat_one_sum / width
    )
    pack_grad = jnp.concatenate(
        [
            pack_b_grad.transpose(1, 2, 0, 3),
            pack_out_grad[:, None],
        ],
        axis=1,
    )
    small = jnp.concatenate(
        [
            a_rows_grad.reshape(compact, 3 * width_local),
            b_out_sum,
            pack_grad.transpose(2, 0, 1, 3).reshape(compact, heads_local * 4 * head_width),
        ],
        axis=1,
    )
    small_all = gather_planes(small.astype(bf16), planes, 9)
    small_all = small_all.reshape(planes * compact, small.shape[1])
    row_at = (
        adapters_all[:, :, None] * RANK + jnp.arange(RANK, dtype=jnp.int32)[None, None, :]
    ).reshape(-1)
    put = (jnp.arange(rank_cols, dtype=jnp.int32)[:, None] == row_at[None, :]).astype(bf16)
    small_sum = jnp.dot(put, small_all, preferred_element_type=f32)
    a_end = 3 * width_local
    b_end = a_end + width_local
    a_sum = small_sum[:, :a_end].reshape(rank_cols, 3, width_local).transpose(1, 2, 0)
    b_sum = small_sum[:, a_end:b_end]
    head_sum = small_sum[:, b_end:].reshape(rank_cols, heads_local, 4, head_width)
    head_sum = head_sum.transpose(1, 2, 0, 3)
    return (layer_out, input_grad, a_sum, b_sum, head_sum, wide_sum, hidden_sum)


def solution(mesh):
    return jax.shard_map(
        shards,
        mesh=mesh,
        in_specs=(
            P("gx", "gy"),
            P("gx", "gy"),
            P("gx", None),
            P("gx"),
            P("gx", None),
            P(),
            P(),
            P(),
            P("gx", "gy", None, None),
            P("gy", None, "gx"),
            P(None, "gy", None),
            P(None, "gy"),
            P("gy", None, None, None),
            P(),
            P("gy", "gx", None, None),
            P("gy", "gx", None),
            P("gy", "gx", None, None),
            P("gy", "gx", None, None),
        ),
        out_specs=(
            P("gx", "gy"),
            P("gx", "gy"),
            P(None, "gy", None),
            P(None, "gy"),
            P("gy", None, None, None),
            P("gy", "gx", None, None),
            P("gy", "gx", None, None),
        ),
        check_vma=False,
    )
```

time: 1170 us -> 1060 us (0.906)
  Pallas kernels: 0 us -> 538 us
  waiting for transfers between devices: 441 us -> 91.4 us
  blocking collectives: 253 us -> 24 us
  matrix products: 182 us -> 122 us
  local copies, waits for them, and re-layouts: 115 us -> 148 us
  other arithmetic: 107 us -> 79.7 us
  starting transfers between devices: 47.2 us -> 30.2 us
    pallas_call x0 -> x9, Pallas kernels: none -> 538 us  [the longest x1 264 us: spread(): pl.pallas_call(functools.partial(spread_kernel, planes, groups, in_set),...]
    all_to_all x10 -> x3, waiting for transfers between devices: 260 us -> 13.9 us  [the longest x1 13.8 us: shards(): lax.all_to_all(weighted, 'gy', 0, 0, tiled=True)]
    all_gather x2 -> x1, blocking collectives: 185 us -> 15.8 us  [shards(): routes_all = lax.all_gather(routes, 'gx', axis=0, tiled=False)]
    all_gather x8 -> x2, waiting for transfers between devices: 113 us -> 0.01 us  [the longest x1 0.01 us: shards(): attn_weight = lax.all_gather(weight_shard, 'gx', axis=0, tiled=True)]
    ppermute x0 -> x9, waiting for transfers between devices: none -> 77.5 us  [the longest x3 62.6 us: shifted(): return lax.ppermute(x, 'gx', pairs)]
    psum x1 -> x0, waiting for transfers between devices: 66.2 us -> none  [shards(): sums = lax.psum(sums, 'gy')]
    dot_general x46 -> x47, matrix products: 162 us -> 103 us  [dot(): return jnp.einsum(spec, left, right, preferred_element_type=f32)]
    all_to_all x1 -> x0, blocking collectives: 48.4 us -> none  [sum_planes(): parts = lax.all_to_all(x, 'gx', 0, 0, tiled=True, axis_index_groups=sets)]
  transfers between devices with their start and end apart: 21 -> 14, of which waited for: 11 -> 4; matrix products, arithmetic and copies ran while one was open for 27% -> 21% of each run, Pallas kernels for 0% -> 45%
where the time goes in v2:
time: 1060 us; the launch traced here: 1050 us
  Pallas kernels  538 us (51%)
  local copies, waits for them, and re-layouts  148 us (14%)
  matrix products  122 us (12%)
  waiting for transfers between devices  91.4 us (9%)
  other arithmetic  79.7 us (8%)
  starting transfers between devices  30.2 us (3%)
  blocking collectives  24 us (2%)
  between operations  17.5 us (2%)
    pallas_call x1, Pallas kernels, spread(): pl.pallas_call(functools.partial(spread_kernel, planes, groups, in_set),...  264 us
    pallas_call x1, Pallas kernels, collect(): pl.pallas_call(functools.partial(collect_kernel, planes, groups, in_set,...  144 us
    dot_general x47, matrix products, dot(): return jnp.einsum(spec, left, right, preferred_element_type=f32)  103 us
    ppermute x3, waiting for transfers between devices, shifted(): return lax.ppermute(x, 'gx', pairs)  62.6 us
    pallas_call x2, Pallas kernels, scatter_product(): pl.pallas_call(functools.partial(scatter_kernel, chips, tile), out_shape=...  62.4 us
    unnamed x308, local copies, waits for them, and re-layouts  36.5 us
    pallas_call x1, Pallas kernels, gather_columns(): pl.pallas_call(functools.partial(gather_kernel, chips), out_shape=jax.Sha...  31.4 us
  transfers between devices with their start and end apart: 14, of which 4 were waited for; matrix products, arithmetic and copies ran while one was open for 21% of the time, Pallas kernels for 45%

profile of v2, /device:TPU:0, one launch (start us, length us, event | category | flops | bytes accessed | tf_op | source)
XLA Modules:
  0.0 1051.4 jit_solution(9526788128285435264)
XLA Ops:
  14.5 31.4 %shard_map.225 = bf16[1088,2048]{1,0:T(8,128)(2,1)S(1)} custom-call(bf16[1088,256]{1,0:T(8,128)(2,1)S(1)} %pad_maximum_fusion.11.x_ref), custom_call_target="tpu_custom_call" | custom-call | bytes 65536 | tf_op jit(solution)/shard_map/pallas_call | solution.py:100
  53.7 15.8 %all-gather = s32[4096,8]{0,1:T(8,128)S(1)} all-gather(s32[1024,8]{0,1:T(8,128)S(1)} %copy-done.95), channel_id=2, replica_groups=mesh['gx'=4,'gy'=8] {'gx'}, dimensions={0}, use_global_device_ids=true | all-gather | bytes 163840 | tf_op jit(solution)/shard_map/all_gather | solution.py:840
  75.7 14.5 %reshape.1253.w_ref = bf16[4,512,2048]{2,1,0:T(8,128)(2,1)} reshape(bf16[4,512,2,1024]{3,2,1,0:T(2,128)(2,1)} %param.32) | data formatting | bytes 16777216 | tf_op jit(solution)/shard_map/reshape | solution.py:1012
  90.2 8.2 all-reduce.2
  122.0 6.7 fusion.170
  169.5 31.0 %shard_map.227 = f32[1024,256]{1,0:T(8,128)S(1)} custom-call(bf16[1024,288]{1,0:T(8,128)(2,1)S(1)} %pad_maximum_fusion.10.l_ref, bf16[2048,288]{1,0:T(8,128)(2,1)S(1)} %pad_maximum_fusion.1.r_ref), custom_call_target="tpu_custom_call" | custom-call | bytes 65536 | tf_op jit(solution)/shard_map/pallas_call | solution.py:178
  229.6 14.9 %collective-permute-done.4 = bf16[256,1024]{0,1:T(8,128)(2,1)} collective-permute-done((bf16[256,1024]{0,1:T(8,128)(2,1)}, bf16[256,1024]{0,1:T(8,128)(2,1)}, u32[]{:S(2)}, u32[]{:S(2)}) %collective-permute-start.4) | collective-permute-done | bytes 524320 | tf_op jit(solution)/shard_map/ppermute | solution.py:813
  244.6 264.3 %shard_map.228 = (bf16[2,1152,2048]{2,1,0:T(8,128)(2,1)}, bf16[2048,2240]{1,0:T(8,128)(2,1)}) custom-call(bf16[1024,512]{1,0:T(8,128)(2,1)S(1)} %pad_maximum_fusion.6.x_ref, s32[4,8,1024]{2,1,0:T(8,128)S(1)} %copy.173.key_ref, bf16[4,512,2048]{2,1,0:T(8,128)(2,1)} %reshape.1253.w_ref), custom_call_target="tpu_custom_call" | custom-call | bytes 65536 | tf_op jit(solution)/shard_map/pallas_call | solution.py:441
  525.7 17.6 %fusion.186 = f32[1152,2240]{0,1:T(8,128)S(1)} fusion(bf16[1152,2048]{1,0:T(8,128)(2,1)} %fusion.4, bf16[2048,2240]{1,0:T(8,128)(2,1)} %maximum_dynamic-update-slice_fusion), kind=kOutput, calls=%fused_computation.396 | convolution fusion | flops 10569646080 | bytes 24215552 | tf_op jit(solution)/shard_map/dot_general | solution.py:1030
  549.4 7.1 multiply_convert_fusion.3
  567.1 8.8 fusion.6
  576.0 9.5 fusion.39
  588.1 6.8 copy.189
  594.9 6.7 copy.190
  606.7 7.6 constant_dynamic-update-slice_fusion.4
  634.6 13.0 %convolution_convert_fusion.u_ref = bf16[1152,2048]{1,0:T(8,128)(2,1)} fusion(bf16[1152,2240]{0,1:T(8,128)(2,1)S(1)} %fusion.127, bf16[2048,2240]{1,0:T(8,128)(2,1)S(1)} %bitcast.496), kind=kOutput, calls=%fused_computation.33 | convolution fusion | flops 10572005376 | bytes 19054592 | tf_op jit(solution)/shard_map/sf,df->sd/dot_general | solution.py:754
  647.6 13.8 %all-to-all-done.1.m_ref = bf16[8,1152,256]{2,1,0:T(8,128)(2,1)} async-done(((bf16[8,1152,256]{2,1,0:T(8,128)(2,1)}), bf16[8,1152,256]{2,1,0:T(8,128)(2,1)}, u32[]{:S(2)}, u32[]{:S(2)}) %all-to-all-start.1) | async-done | bytes 4718624 | tf_op jit(solution)/shard_map/all_to_all | solution.py:1082
  661.4 143.6 %shard_map.229 = (f32[1024,256]{1,0:T(8,128)S(1)}, bf16[1024,2048]{1,0:T(8,128)(2,1)}, bf16[4,1024,256]{2,1,0:T(8,128)(2,1)S(1)}) custom-call(bf16[1152,2048]{1,0:T(8,128)(2,1)} %convolution_convert_fusion.u_ref, bf16[8,1152,256]{2,1,0:T(8,128)(2,1)} %all-to-all-done.1.m_ref, s32[4,1024,8]{2,1,0:T(8,128)S(1)} %add_select_fusion.key_ref), custom_call_target="tpu_custom_call" | custom-call | bytes 65536 | tf_op jit(solution)/shard_map/pallas_call | solution.py:646
  826.2 21.6 %collective-permute-done.6 = bf16[1024,256]{1,0:T(8,128)(2,1)S(1)} collective-permute-done((bf16[1024,256]{1,0:T(8,128)(2,1)S(1)}, bf16[1024,256]{1,0:T(8,128)(2,1)S(1)}, u32[]{:S(2)}, u32[]{:S(2)}) %collective-permute-start.6) | collective-permute-done | bytes 524320 | tf_op jit(solution)/shard_map/ppermute | solution.py:805
  847.7 41.0 %collective-permute-done.7 = bf16[1024,256]{1,0:T(8,128)(2,1)S(1)} collective-permute-done((bf16[1024,256]{1,0:T(8,128)(2,1)S(1)}, bf16[1024,256]{1,0:T(8,128)(2,1)S(1)}, u32[]{:S(2)}, u32[]{:S(2)}) %collective-permute-start.7) | collective-permute-done | bytes 524320 | tf_op jit(solution)/shard_map/ppermute | solution.py:805
  937.2 6.6 concatenate.118
  945.5 13.6 %shard_map.230 = f32[128,1024]{1,0:T(8,128)} custom-call(bf16[128,1024]{1,0:T(8,128)(2,1)} %pad.5.x_ref), custom_call_target="tpu_custom_call" | custom-call | bytes 65536 | tf_op jit(solution)/shard_map/pallas_call | solution.py:280
  975.6 10.3 shard_map.233
  1000.8 31.4 %shard_map.231 = f32[1024,256]{1,0:T(8,128)S(1)} custom-call(bf16[1024,768]{1,0:T(8,128)(2,1)S(1)} %copy-done.4, bf16[2048,768]{1,0:T(8,128)(2,1)S(1)} %slice.316.r_ref), custom_call_target="tpu_custom_call" | custom-call | bytes 65536 | tf_op jit(solution)/shard_map/pallas_call | solution.py:178
  (539 shorter events, 288.1 us)
Async XLA Ops:
  7.2 121.5 %copy-start = (bf16[2,4,128,128]{3,2,1,0:T(8,128)(2,1)S(1)}, bf16[2,4,128,128]{3,2,1,0:T(8,128)(2,1)}, u32[]{:S(2)}) copy-start(bf16[2,4,128,128]{3,2,1,0:T(8,128)(2,1)} %param.30) | copy-start | bytes 786436
  7.2 114.8 %all-gather.5.cloned.1.call-start = ((), (), s32[]{:S(2)}) async-start(), calls=%async_computation.3 | async-start | bytes 5242880 | tf_op jit(solution)/shard_map/all_gather | solution.py:852
  12.1 96.0 %copy-start.74 = (s32[1024]{0:T(1024)}, s32[1024]{0:T(1024)S(1)}, u32[]{:S(2)}) copy-start(s32[1024]{0:T(1024)S(1)} %add_select_fusion.1) | copy-start | bytes 12292
  12.1 96.0 %copy-start.113 = (s32[16]{0:T(128)}, s32[16]{0:T(128)S(1)}, u32[]{:S(2)}) copy-start(s32[16]{0:T(128)S(1)} %and_select_fusion.4) | copy-start | bytes 196
  12.2 98.8 %copy-start.104 = (s32[128]{0:T(128)}, s32[128]{0:T(128)S(1)}, u32[]{:S(2)}) copy-start(s32[128]{0:T(128)S(1)} %get-tuple-element.133) | copy-start | bytes 1540
  12.3 98.8 %copy-start.106 = (s32[128]{0:T(128)}, s32[128]{0:T(128)S(1)}, u32[]{:S(2)}) copy-start(s32[128]{0:T(128)S(1)} %get-tuple-element.134) | copy-start | bytes 1540
  12.3 98.8 %copy-start.108 = (s32[64]{0:T(128)}, s32[64]{0:T(128)S(1)}, u32[]{:S(2)}) copy-start(s32[64]{0:T(128)S(1)} %and_select_fusion.1) | copy-start | bytes 772
  155.5 45.0 %collective-permute-start = (bf16[256,1024]{0,1:T(8,128)(2,1)}, bf16[256,1024]{0,1:T(8,128)(2,1)}, u32[]{:S(2)}, u32[]{:S(2)}) collective-permute-start(bf16[256,1024]{0,1:T(8,128)(2,1)} %bitcast.466), channel_id=1, source_target_pairs={{0,8},{8,16},{16,24},{24,0},{1,9},{9,17},{17,25},{25,1},{2,10},{10... | collective-permute-start | bytes 1572872 | tf_op jit(solution)/shard_map/ppermute | solution.py:813
  158.8 41.7 %collective-permute-start.1 = (bf16[256,1024]{0,1:T(8,128)(2,1)}, bf16[256,1024]{0,1:T(8,128)(2,1)}, u32[]{:S(2)}, u32[]{:S(2)}) collective-permute-start(bf16[256,1024]{0,1:T(8,128)(2,1)} %bitcast.467), channel_id=1, source_target_pairs={{0,16},{8,24},{16,0},{24,8},{1,17},{9,25},{17,1},{25,9},{2,18},{10... | collective-permute-start | bytes 1572872 | tf_op jit(solution)/shard_map/ppermute | solution.py:813
  159.9 40.6 %collective-permute-start.2 = (bf16[256,1024]{0,1:T(8,128)(2,1)}, bf16[256,1024]{0,1:T(8,128)(2,1)}, u32[]{:S(2)}, u32[]{:S(2)}) collective-permute-start(bf16[256,1024]{0,1:T(8,128)(2,1)} %bitcast.468), channel_id=1, source_target_pairs={{0,24},{8,0},{16,8},{24,16},{1,25},{9,1},{17,9},{25,17},{2,26},{10... | collective-permute-start | bytes 1572872 | tf_op jit(solution)/shard_map/ppermute | solution.py:813
  204.1 25.6 %collective-permute-start.3 = (bf16[256,1024]{0,1:T(8,128)(2,1)}, bf16[256,1024]{0,1:T(8,128)(2,1)}, u32[]{:S(2)}, u32[]{:S(2)}) collective-permute-start(bf16[256,1024]{0,1:T(8,128)(2,1)} %bitcast.463), channel_id=1, source_target_pairs={{0,8},{8,16},{16,24},{24,0},{1,9},{9,17},{17,25},{25,1},{2,10},{10... | collective-permute-start | bytes 1572872 | tf_op jit(solution)/shard_map/ppermute | solution.py:813
  211.3 33.2 %collective-permute-start.4 = (bf16[256,1024]{0,1:T(8,128)(2,1)}, bf16[256,1024]{0,1:T(8,128)(2,1)}, u32[]{:S(2)}, u32[]{:S(2)}) collective-permute-start(bf16[256,1024]{0,1:T(8,128)(2,1)} %bitcast.464), channel_id=1, source_target_pairs={{0,16},{8,24},{16,0},{24,8},{1,17},{9,25},{17,1},{25,9},{2,18},{10... | collective-permute-start | bytes 1572872 | tf_op jit(solution)/shard_map/ppermute | solution.py:813
  213.4 31.1 %collective-permute-start.5 = (bf16[256,1024]{0,1:T(8,128)(2,1)}, bf16[256,1024]{0,1:T(8,128)(2,1)}, u32[]{:S(2)}, u32[]{:S(2)}) collective-permute-start(bf16[256,1024]{0,1:T(8,128)(2,1)} %bitcast.465), channel_id=1, source_target_pairs={{0,24},{8,0},{16,8},{24,16},{1,25},{9,1},{17,9},{25,17},{2,26},{10... | collective-permute-start | bytes 1572872 | tf_op jit(solution)/shard_map/ppermute | solution.py:813
  217.7 300.2 %all-to-all-start = ((bf16[4,1152,128]{1,2,0:T(8,128)(2,1)}), bf16[4,1152,128]{1,2,0:T(8,128)(2,1)}, u32[]{:S(2)}, u32[]{:S(2)}) async-start(bf16[4,1152,128]{1,2,0:T(8,128)(2,1)} %pad_maximum_fusion.3), calls=%async_computation | async-start | bytes 2359296 | tf_op jit(solution)/shard_map/all_to_all | solution.py:890
  222.0 675.9 %all-gather.7.cloned.1.call-start = ((), (), s32[]{:S(2)}) async-start(), calls=%async_computation.4 | async-start | bytes 9437184 | tf_op jit(solution)/shard_map/all_gather | solution.py:1024
  601.6 59.9 %all-to-all-start.1 = ((bf16[8,1152,256]{2,1,0:T(8,128)(2,1)}), bf16[8,1152,256]{2,1,0:T(8,128)(2,1)}, u32[]{:S(2)}, u32[]{:S(2)}) async-start(bf16[8,1152,256]{2,1,0:T(8,128)(2,1)} %bitcast.432), calls=%async_computation.1 | async-start | bytes 9437184 | tf_op jit(solution)/shard_map/all_to_all | solution.py:1082
  810.1 80.8 %all-to-all-start.2 = ((bf16[4,1152,128]{1,2,0:T(8,128)(2,1)}), bf16[4,1152,128]{1,2,0:T(8,128)(2,1)}, u32[]{:S(2)}, u32[]{:S(2)}) async-start(bf16[4,1152,128]{1,2,0:T(8,128)(2,1)} %pad_maximum_fusion.4), calls=%async_computation.2 | async-start | bytes 2359296 | tf_op jit(solution)/shard_map/all_to_all | solution.py:1109
  817.9 29.8 %collective-permute-start.6 = (bf16[1024,256]{1,0:T(8,128)(2,1)S(1)}, bf16[1024,256]{1,0:T(8,128)(2,1)S(1)}, u32[]{:S(2)}, u32[]{:S(2)}) collective-permute-start(bf16[1024,256]{1,0:T(8,128)(2,1)S(1)} %get-tuple-element.74), channel_id=1, source_target_pairs={{0,24},{8,0},{16,8},{24,16},{1,25},{9,1},{17,9},{25,17},{2,26},{10... | collective-permute-start | bytes 1572872 | tf_op jit(solution)/shard_map/ppermute | solution.py:805
  821.8 66.9 %collective-permute-start.7 = (bf16[1024,256]{1,0:T(8,128)(2,1)S(1)}, bf16[1024,256]{1,0:T(8,128)(2,1)S(1)}, u32[]{:S(2)}, u32[]{:S(2)}) collective-permute-start(bf16[1024,256]{1,0:T(8,128)(2,1)S(1)} %get-tuple-element.76), channel_id=1, source_target_pairs={{0,16},{8,24},{16,0},{24,8},{1,17},{9,25},{17,1},{25,9},{2,18},{10... | collective-permute-start | bytes 1572872 | tf_op jit(solution)/shard_map/ppermute | solution.py:805
  821.8 66.9 %collective-permute-start.8 = (bf16[1024,256]{1,0:T(8,128)(2,1)S(1)}, bf16[1024,256]{1,0:T(8,128)(2,1)S(1)}, u32[]{:S(2)}, u32[]{:S(2)}) collective-permute-start(bf16[1024,256]{1,0:T(8,128)(2,1)S(1)} %get-tuple-element.75), channel_id=1, source_target_pairs={{0,8},{8,16},{16,24},{24,0},{1,9},{9,17},{17,25},{25,1},{2,10},{10... | collective-permute-start | bytes 1572872 | tf_op jit(solution)/shard_map/ppermute | solution.py:805
  826.1 66.2 %copy-start.93 = (s32[64]{0:T(128)S(1)}, s32[64]{0:T(128)}, u32[]{:S(2)}) copy-start(s32[64]{0:T(128)} %copy-done.92) | copy-start | bytes 772
  826.1 66.2 %copy-start.105 = (s32[128]{0:T(128)S(1)}, s32[128]{0:T(128)}, u32[]{:S(2)}) copy-start(s32[128]{0:T(128)} %copy-done.104) | copy-start | bytes 1540
  826.1 66.2 %copy-start.107 = (s32[128]{0:T(128)S(1)}, s32[128]{0:T(128)}, u32[]{:S(2)}) copy-start(s32[128]{0:T(128)} %copy-done.106) | copy-start | bytes 1540
  826.1 66.2 %copy-start.109 = (s32[64]{0:T(128)S(1)}, s32[64]{0:T(128)}, u32[]{:S(2)}) copy-start(s32[64]{0:T(128)} %copy-done.108) | copy-start | bytes 772
  (134 other events, 1285.4 us)
Sparse Core Ops, SparseCore 0:
  12.2 85.5 all-gather.4
  226.4 74.0 all-gather.6

commit v3 on v2

--- a/solution.py
+++ b/solution.py
@@ -10,7 +10,6 @@
 SEQ = 1024
 PIECE = 256
 CAP = 288
-DOWN_PARTS = 2
 
 
 norm_eps = 1e-05
@@ -24,7 +23,6 @@
 MESH = pl.DeviceIdType.MESH
 SMALL = pl.CostEstimate(flops=0, bytes_accessed=1 << 16, transcendentals=0)
 CAP = 288
-DOWN_PARTS = 2
 SMALL = pl.CostEstimate(flops=0, bytes_accessed=1 << 16, transcendentals=0)
 
 
@@ -38,8 +36,11 @@
     return lax.rem(chip + step, chips) * 2 + core
 
 
-def greet_chips(chip, core, sibling, chips):
+def greet_chips(chip, core, sibling, chips, planes=1):
     barrier = pltpu.get_barrier_semaphore()
+    for step in range(1, planes):
+        target = lax.rem(lax.axis_index("gx") + step, planes)
+        pl.semaphore_signal(barrier, inc=1, device_id={"gx": target}, device_id_type=MESH)
     pl.semaphore_signal(barrier, inc=1, device_id={"gy": sibling}, device_id_type=MESH)
     for step in range(1, chips):
         pl.semaphore_signal(
@@ -48,7 +49,7 @@
             device_id={"gy": chip_peer(chip, core, step, chips)},
             device_id_type=MESH,
         )
-    pl.semaphore_wait(barrier, chips)
+    pl.semaphore_wait(barrier, chips + planes - 1)
 
 
 def remote(src, dst, send_sem, recv_sem, target):
@@ -62,12 +63,27 @@
     )
 
 
-def gather_kernel(chips, x_ref, o_ref, own_sem, send_sem, recv_sem, pass_sem, passed_sem):
+def gather_kernel(
+    chips,
+    rows,
+    tile,
+    x_ref,
+    gain_ref,
+    normed_ref,
+    scale_ref,
+    rest_ref,
+    whole,
+    own_sem,
+    send_sem,
+    recv_sem,
+    pass_sem,
+    passed_sem,
+):
     me, chip, core, sibling = place_in_column()
     width = x_ref.shape[1]
 
     def columns(owner):
-        return o_ref.at[:, pl.ds(pl.multiple_of(owner * width, width), width)]
+        return whole.at[:, pl.ds(pl.multiple_of(owner * width, width), width)]
 
     own = pltpu.make_async_copy(x_ref, columns(me), own_sem)
     own.start()
@@ -90,32 +106,101 @@
     out[chips - 1].wait_recv()
     for copy in out[chips:]:
         copy.wait_recv()
+
+    @pl.loop(0, rows // tile)
+    def _(i):
+        at = pl.ds(pl.multiple_of(i * tile, tile), tile)
+        values = whole[at, :].astype(f32)
+        scale = lax.rsqrt(jnp.mean(values * values, axis=-1, keepdims=True) + norm_eps)
+        scale_ref[at, :] = jnp.broadcast_to(scale, (tile, 128))
+        normed_ref[at, :] = (values * scale * gain_ref[...]).astype(bf16)
+
+    rest_ref[...] = whole[pl.ds(rows, rest_ref.shape[0]), :]
     for copy in out:
         copy.wait_send()
 
 
-def gather_columns(x, groups, collective_id):
+def gather_normed(x, gain, rows, groups, collective_id):
     chips = groups // 2
-    rows, width = x.shape
+    total, width = x.shape
+    full = groups * width
     return pl.pallas_call(
-        functools.partial(gather_kernel, chips),
-        out_shape=jax.ShapeDtypeStruct((rows, groups * width), x.dtype),
-        in_specs=[VMEM],
-        out_specs=VMEM,
-        scratch_shapes=[DMA, DMA((chips,)), DMA((chips,)), DMA((chips,)), DMA((chips,))],
+        functools.partial(gather_kernel, chips, rows, 64),
+        out_shape=(
+            jax.ShapeDtypeStruct((rows, full), bf16),
+            jax.ShapeDtypeStruct((rows, 128), f32),
+            jax.ShapeDtypeStruct((total - rows, full), bf16),
+        ),
+        in_specs=[VMEM, VMEM],
+        out_specs=(VMEM, VMEM, VMEM),
+        scratch_shapes=[
+            pltpu.VMEM((total, full), bf16),
+            DMA,
+            DMA((chips,)),
+            DMA((chips,)),
+            DMA((chips,)),
+            DMA((chips,)),
+        ],
         compiler_params=pltpu.CompilerParams(
             collective_id=collective_id, has_side_effects=True, vmem_limit_bytes=48 << 20
         ),
         cost_estimate=SMALL,
-    )(x)
+    )(x, gain.reshape(1, full))
+
+
+def scatter_and_carry_kernel(
+    planes, first, chips, tile, l_ref, r_ref, w_ref, o_ref, w_out, *rest
+):
+    *scratch, w_own, w_send, w_recv = rest
+    plane = lax.axis_index("gx")
+    in_set, count = w_ref.shape[0], w_out.shape[1]
+
+    def piece(target):
+        return w_ref.at[lax.rem(target, in_set), pl.ds(first, count), :]
+
+    def carry():
+        own = pltpu.make_async_copy(piece(plane), w_out.at[plane], w_own)
+        own.start()
+        copies = []
+        for step in range(1, planes):
+            target = lax.rem(plane + step, planes)
+            copy = to_plane(
+                piece(target), w_out.at[plane], w_send.at[step - 1], w_recv.at[step - 1], target
+            )
+            copy.start()
+            copies.append(copy)
+        return own, copies
+
+    own, copies = scatter_kernel(
+        chips, tile, l_ref, r_ref, o_ref, *scratch, planes=planes, after_greeting=carry
+    )
+    own.wait()
+    for copy in copies:
+        copy.wait_recv()
+        copy.wait_send()
 
 
 def scatter_kernel(
-    chips, tile, l_ref, r_ref, o_ref, part, got, pair, far, part_s, got_s, pair_s, far_s
+    chips,
+    tile,
+    l_ref,
+    r_ref,
+    o_ref,
+    part,
+    got,
+    pair,
+    far,
+    part_s,
+    got_s,
+    pair_s,
+    far_s,
+    planes=1,
+    after_greeting=None,
 ):
     me, chip, core, sibling = place_in_column()
     rows, width = o_ref.shape
-    greet_chips(chip, core, sibling, chips)
+    greet_chips(chip, core, sibling, chips, planes)
+    carried = after_greeting() if after_greeting else None
     steps = list(range(1, chips)) + [0]
 
     def product(owner, row):
@@ -168,33 +253,47 @@
 
     for copy in copies:
         copy.wait_send()
-
-
-def scatter_product(left, right, groups, collective_id):
+    return carried
+
+
+def scatter_product(left, right, groups, collective_id, weight=None, first=0, planes=1):
     chips = groups // 2
     rows, inner = left.shape
     width = right.shape[0] // groups
     tile = min(256, rows)
+    body = functools.partial(scatter_kernel, chips, tile)
+    out_shape = (jax.ShapeDtypeStruct((rows, width), f32),)
+    in_specs, out_specs = [VMEM, VMEM], (VMEM,)
+    scratch = [
+        pltpu.VMEM((chips, rows, width), bf16),
+        pltpu.VMEM((chips, rows, width), bf16),
+        pltpu.VMEM((chips - 1, rows, width), bf16),
+        pltpu.VMEM((chips - 1, rows, width), bf16),
+        DMA((chips,)),
+        DMA((chips,)),
+        DMA((chips - 1,)),
+        DMA((chips - 1,)),
+    ]
+    operands = (left, right)
+    if weight is not None:
+        body = functools.partial(scatter_and_carry_kernel, planes, first, chips, tile)
+        carried = (planes, weight.shape[1] - first, weight.shape[2])
+        out_shape += (jax.ShapeDtypeStruct(carried, bf16),)
+        in_specs = in_specs + [pl.BlockSpec(memory_space=pl.ANY)]
+        out_specs += (pl.BlockSpec(memory_space=pl.ANY),)
+        scratch = scratch + [DMA, DMA((planes - 1,)), DMA((planes - 1,))]
+        operands += (weight,)
     return pl.pallas_call(
-        functools.partial(scatter_kernel, chips, tile),
-        out_shape=jax.ShapeDtypeStruct((rows, width), f32),
-        in_specs=[VMEM, VMEM],
-        out_specs=VMEM,
-        scratch_shapes=[
-            pltpu.VMEM((chips, rows, width), bf16),
-            pltpu.VMEM((chips, rows, width), bf16),
-            pltpu.VMEM((chips - 1, rows, width), bf16),
-            pltpu.VMEM((chips - 1, rows, width), bf16),
-            DMA((chips,)),
-            DMA((chips,)),
-            DMA((chips - 1,)),
-            DMA((chips - 1,)),
-        ],
+        body,
+        out_shape=out_shape,
+        in_specs=in_specs,
+        out_specs=out_specs,
+        scratch_shapes=scratch,
         compiler_params=pltpu.CompilerParams(
             collective_id=collective_id, has_side_effects=True, vmem_limit_bytes=48 << 20
         ),
         cost_estimate=SMALL,
-    )(left, right)
+    )(*operands)
 
 
 def add_kernel(groups, x_ref, o_ref, got, send_sem, recv_sem):
@@ -354,32 +453,47 @@
     width = x_ref.shape[1] // 2
     depth, inner = w_ref.shape[1], w_ref.shape[2]
     greet_all(planes, groups)
-    z_copies = []
-    for step in range(1, in_set):
+    last = in_set - 1
+
+    def handed(step, up):
+        side = 0 if up else 1
+        distance = step if up else in_set - step
+        there = own + (1 if up else -1)
+        holds = own - (step - 1) if up else own + (step - 1)
+        here = own - step if up else own + step
+        sends = (there <= last) & (there >= 0) & (holds >= 0) & (holds <= last)
+        waits = (here >= 0) & (here <= last)
+        before = step - 1 if up else in_set - (step - 1)
+        source = x_ref if step == 1 else from_plane.at[before - 1]
         copy = to_plane(
-            x_ref,
-            from_plane.at[step - 1],
-            z_send.at[step - 1],
-            z_recv.at[step - 1],
-            base + lax.rem(own + step, in_set),
-        )
-        copy.start()
-        z_copies.append(copy)
+            source,
+            from_plane.at[distance - 1],
+            z_send.at[side, step - 1],
+            z_recv.at[side, step - 1],
+            base + lax.rem(there + in_set, in_set),
+        )
+        return copy, sends, waits
+
+    def start_hand(step):
+        for up in (True, False):
+            copy, sends, _ = handed(step, up)
+            pl.when(sends)(copy.start)
+
+    def await_hand(step):
+        for up in (True, False):
+            copy, _, waits = handed(step, up)
+            pl.when(waits)(copy.wait_recv)
+
+    def end_hands():
+        for step in range(1, in_set):
+            for up in (True, False):
+                copy, sends, _ = handed(step, up)
+                pl.when(sends)(copy.wait_send)
+
+    start_hand(1)
     mine = full_ref.at[pl.ds(pl.multiple_of(plane * depth, depth), depth), pl.ds(0, inner)]
     own_copy = pltpu.make_async_copy(w_ref.at[own], mine, own_sem)
     own_copy.start()
-    w_copies = []
-    for step in range(1, planes):
-        target = lax.rem(plane + step, planes)
-        copy = to_plane(
-            w_ref.at[lax.rem(target, in_set)],
-            mine,
-            w_send.at[step - 1],
-            w_recv.at[step - 1],
-            target,
-        )
-        copy.start()
-        w_copies.append(copy)
 
     def sent(step, turn):
         target = lax.rem(me + turn, groups)
@@ -395,9 +509,7 @@
             target,
         )
 
-    for step in range(in_set):
-        if step:
-            z_copies[step - 1].wait_recv()
+    def work(step):
         block = from_plane.at[step - 1] if step else x_ref
 
         def choose(target):
@@ -407,7 +519,7 @@
             return jnp.dot(pick, block[...], preferred_element_type=f32).astype(bf16)
 
         @pl.loop(1, groups)
-        def _(turn, step=step, choose=choose):
+        def _(turn):
             rows = choose(lax.rem(me + turn, groups))
             picked[step, turn, 0] = rows[:, :width]
             picked[step, turn, 1] = rows[:, width:]
@@ -417,6 +529,26 @@
         columns = pl.ds(pl.multiple_of(me * width, width), width)
         o_ref[0, pl.ds(step * CAP, CAP), columns] = rows[:, :width]
         o_ref[1, pl.ds(step * CAP, CAP), columns] = rows[:, width:]
+
+    for step in range(1, in_set - 1):
+        await_hand(step)
+        start_hand(step + 1)
+    w_copies = []
+    for step in range(1, planes):
+        target = lax.rem(plane + step, planes)
+        copy = to_plane(
+            w_ref.at[lax.rem(target, in_set)],
+            mine,
+            w_send.at[step - 1],
+            w_recv.at[step - 1],
+            target,
+        )
+        copy.start()
+        w_copies.append(copy)
+    work(0)
+    await_hand(in_set - 1)
+    for step in range(1, in_set):
+        work(step)
 
     for step in range(in_set):
 
@@ -426,8 +558,7 @@
             copy.wait_recv()
             copy.wait_send()
 
-    for copy in z_copies:
-        copy.wait_send()
+    end_hands()
     own_copy.wait()
     for copy in w_copies:
         copy.wait_recv()
@@ -452,8 +583,8 @@
             DMA,
             DMA((planes - 1,)),
             DMA((planes - 1,)),
-            DMA((in_set - 1,)),
-            DMA((in_set - 1,)),
+            DMA((2, in_set - 1)),
+            DMA((2, in_set - 1)),
             DMA((in_set, groups)),
             DMA((in_set, groups)),
         ],
@@ -464,26 +595,45 @@
     )(x, key, weight)
 
 
-def collect_kernel(
+def experts_kernel(
     planes,
     groups,
     in_set,
     tile,
-    u_ref,
-    m_ref,
+    names,
+    slots_ref,
+    w1_ref,
+    w2_ref,
+    hg_ref,
+    hu_ref,
+    hd_ref,
+    mask_ref,
+    mask_down_ref,
+    own_ref,
+    gain_ref,
     key_ref,
     shard_ref,
     rows_ref,
     placed_ref,
+    wide_ref,
+    wide_down_ref,
+    hg_grad_ref,
+    hu_grad_ref,
+    hd_grad_ref,
+    slot_buf,
+    u_stage,
+    m_stage,
     got,
     other,
     out_z,
     in_z,
     low,
+    slot_sem,
     g_send,
     g_recv,
+    m_send,
+    m_recv,
     own_sem,
-    m_sem,
     z_send,
     z_recv,
     c_own,
@@ -496,53 +646,84 @@
     me, chip, core, sibling = place_in_column()
     chips = groups // 2
     rows, width = shard_ref.shape
-    greet_all(planes, groups)
+    hidden = hd_ref.shape[0]
+    rank = mask_ref.shape[1]
     order = list(range(1, in_set)) + [0]
-
-    def block_of(step, owner):
-        return u_ref.at[
-            pl.ds(step * CAP, CAP), pl.ds(pl.multiple_of(owner * width, width), width)
-        ]
+    last = in_set - 1
+
+    def columns_of(owner):
+        return pl.ds(pl.multiple_of(owner * width, width), width)
 
     def slots_of(buffer, step, owner):
         return buffer.at[step, pl.ds(pl.multiple_of(owner * CAP, 16), CAP), :]
 
-    def sent(step, turn):
+    def load(index):
+        return pltpu.make_async_copy(
+            slots_ref.at[:, pl.ds(order[index] * CAP, CAP), :],
+            slot_buf.at[index % 2],
+            slot_sem.at[index % 2],
+        )
+
+    def sent(index, turn, stage, landing, send_sem, recv_sem):
         target = lax.rem(me + turn, groups)
+        step = order[index]
         return remote(
-            block_of(step, target),
-            slots_of(got, step, me),
-            g_send.at[step, turn],
-            g_recv.at[step, turn],
+            stage.at[index % 2, :, columns_of(target)],
+            slots_of(landing, step, me),
+            send_sem.at[step, turn],
+            recv_sem.at[step, turn],
             target,
         )
 
-    def own_copy(step):
-        return pltpu.make_async_copy(block_of(step, me), slots_of(got, step, me), own_sem.at[step])
-
-    def other_copy(step, owner):
+    def kept(index, stage, landing, which):
+        step = order[index]
         return pltpu.make_async_copy(
-            m_ref.at[owner, pl.ds(step * CAP, CAP), :],
-            slots_of(other, step, owner),
-            m_sem.at[step, owner],
-        )
-
-    for step in order:
+            stage.at[index % 2, :, columns_of(me)],
+            slots_of(landing, step, me),
+            own_sem.at[which, step],
+        )
+
+    flows = (
+        (u_stage, got, g_send, g_recv, 0),
+        (m_stage, other, m_send, m_recv, 1),
+    )
+
+    def start_flow(index, flow):
+        stage, landing, send_sem, recv_sem, which = flow
 
         @pl.loop(1, groups)
-        def _(turn, step=step):
-            sent(step, turn).start()
-
-        own_copy(step).start()
-
-    for step in order:
-
-        @pl.loop(0, groups)
-        def _(owner, step=step):
-            other_copy(step, owner).start()
+        def _(turn):
+            sent(index, turn, stage, landing, send_sem, recv_sem).start()
+
+        kept(index, stage, landing, which).start()
+
+    def left_flow(index, flow):
+        stage, landing, send_sem, recv_sem, which = flow
+
+        @pl.loop(1, groups)
+        def _(turn):
+            sent(index, turn, stage, landing, send_sem, recv_sem).wait_send()
+
+        if index < last - 1:
+            kept(index, stage, landing, which).wait()
+
+    def await_flow(index, flow):
+        stage, landing, send_sem, recv_sem, which = flow
+
+        @pl.loop(1, groups)
+        def _(turn):
+            sent(index, turn, stage, landing, send_sem, recv_sem).wait_recv()
+
+        if index >= last - 1:
+            kept(index, stage, landing, which).wait()
+
+    def mul(left, right, over_left, over_right):
+        return lax.dot_general(
+            left, right, (((over_left,), (over_right,)), ((), ())), preferred_element_type=f32
+        )
 
     def placed(step, row, buffer):
-        keys = key_ref[step, pl.ds(row, tile), :]
+        keys = jnp.transpose(key_ref[step, :, pl.ds(row, tile)])
         pieces = []
         for start in range(0, groups * CAP, 128):
             slot = lax.broadcasted_iota(jnp.int32, (tile, 128), 1) + start
@@ -555,27 +736,21 @@
             jnp.concatenate(pieces, axis=1), buffer[step], preferred_element_type=f32
         )
 
-    for step in order:
-
-        @pl.loop(0, groups)
-        def _(owner, step=step):
-            other_copy(step, owner).wait()
+    def back(step):
+        return to_plane(
+            out_z.at[step - 1],
+            in_z.at[step - 1],
+            z_send.at[step - 1],
+            z_recv.at[step - 1],
+            base + lax.rem(own - step + in_set, in_set),
+        )
+
+    def gather_own(index):
+        step = order[index]
+        await_flow(index, flows[0])
 
         @pl.loop(0, rows // tile)
-        def _(i, step=step):
-            row = pl.multiple_of(i * tile, tile)
-            placed_ref[step, pl.ds(row, tile), :] = placed(step, row, other).astype(bf16)
-
-    z_copies = []
-    for step in order:
-        own_copy(step).wait()
-
-        @pl.loop(1, groups)
-        def _(turn, step=step):
-            sent(step, turn).wait_recv()
-
-        @pl.loop(0, rows // tile)
-        def _(i, step=step):
+        def _(i):
             row = pl.multiple_of(i * tile, tile)
             total = placed(step, row, got)
             if step:
@@ -584,17 +759,103 @@
                 shard_ref[pl.ds(row, tile), :] = total
 
         if step:
-            copy = to_plane(
-                out_z.at[step - 1],
-                in_z.at[step - 1],
-                z_send.at[step - 1],
-                z_recv.at[step - 1],
-                base + lax.rem(own - step + in_set, in_set),
-            )
-            copy.start()
-            z_copies.append(copy)
-    for copy in z_copies:
-        copy.wait_recv()
+            back(step).start()
+
+    def gather_other(index):
+        step = order[index]
+        await_flow(index, flows[1])
+
+        @pl.loop(0, rows // tile)
+        def _(i):
+            row = pl.multiple_of(i * tile, tile)
+            placed_ref[step, pl.ds(row, tile), :] = placed(step, row, other).astype(bf16)
+
+    load(0).start()
+    load(1).start()
+    greet_all(planes, groups)
+    lane = lax.broadcasted_iota(jnp.int32, (CAP, 128), 1)
+    for index, step in enumerate(order):
+        at = pl.ds(step * CAP, CAP)
+        load(index).wait()
+        middle = slot_buf[index % 2, 0].astype(f32)
+        scale = lax.rsqrt(jnp.mean(middle * middle, axis=-1, keepdims=True) + norm_eps)
+        expert_in = (middle * scale * gain_ref[...]).astype(bf16)
+        pre = mul(expert_in, w1_ref[...], 1, 0)
+        both_masks = mask_ref[at, :]
+        mask_down = mask_down_ref[at, :]
+        valid = jnp.max(mask_down, axis=1, keepdims=True)
+        rank_gu = (pre[:, 2 * hidden : 2 * hidden + rank] * both_masks).astype(bf16)
+        logits = pre[:, 2 * hidden + rank :]
+        first = lane < names // 2
+        peak = jnp.max(jnp.where(first, logits, -1e30), axis=1, keepdims=True)
+        raised = jnp.exp(jnp.where(lane < names, logits, -1e30) - peak)
+        probs = raised / jnp.sum(jnp.where(first, raised, 0.0), axis=1, keepdims=True)
+        is_own = own_ref[...]
+        gate = jnp.sum(jnp.where(first, probs * is_own, 0.0), axis=1, keepdims=True) * valid
+        gate_pre = pre[:, :hidden] + rank_scale * mul(rank_gu, hg_ref[...], 1, 1)
+        up_pre = pre[:, hidden : 2 * hidden] + rank_scale * mul(rank_gu, hu_ref[...], 1, 1)
+        sigma = 1.0 / (1.0 + jnp.exp(-gate_pre))
+        activated = gate_pre * sigma
+        inner = (activated * up_pre).astype(bf16)
+        rank_down = (mul(inner, hd_ref[...], 1, 0) * mask_down).astype(bf16)
+        inner_wide = jnp.concatenate(
+            [inner, (down_scale * rank_down.astype(f32)).astype(bf16)], axis=1
+        )
+        output = mul(inner_wide, w2_ref[...], 1, 1)
+        cotangent = slot_buf[index % 2, 1].astype(f32)
+        gate_grad = jnp.sum(cotangent * output, axis=1, keepdims=True)
+        if index >= 2:
+            left_flow(index - 2, flows[1])
+            left_flow(index - 2, flows[0])
+        m_stage[index % 2] = (gate * output).astype(bf16)
+        if index < last:
+            start_flow(index, flows[1])
+        weighted = (gate * cotangent).astype(bf16)
+        inner_grads = mul(weighted, w2_ref[...], 1, 0)
+        rank_down_grad = (down_scale * inner_grads[:, hidden:] * mask_down).astype(bf16)
+        inner_grad = inner_grads[:, :hidden] + mul(rank_down_grad, hd_ref[...], 1, 1)
+        gate_pre_grad = (
+            inner_grad * up_pre * sigma * (1.0 + gate_pre * (1.0 - sigma))
+        ).astype(bf16)
+        up_pre_grad = (inner_grad * activated).astype(bf16)
+        rank_gu_grad = (
+            rank_scale
+            * (mul(gate_pre_grad, hg_ref[...], 1, 0) + mul(up_pre_grad, hu_ref[...], 1, 0))
+            * both_masks
+        ).astype(bf16)
+        logit_grad = (is_own - probs) * (gate * gate_grad)
+        logit_high = logit_grad.astype(bf16)
+        logit_rest = logit_grad - logit_high.astype(f32)
+        logit_two = jnp.where(first, logit_high.astype(f32), logit_rest)
+        logit_two = jnp.where(lane < names, logit_two, 0.0).astype(bf16)
+        wide = jnp.concatenate([gate_pre_grad, up_pre_grad, rank_gu_grad, logit_two], axis=1)
+        u_stage[index % 2] = mul(wide, w1_ref[...], 1, 1).astype(bf16)
+        start_flow(index, flows[0])
+        if index == last:
+            start_flow(index, flows[1])
+        if index + 2 <= last:
+            load(index + 2).start()
+
+        def add(ref, value):
+            if index:
+                ref[...] += value
+            else:
+                ref[...] = value
+
+        add(wide_ref, mul(rank_gu_grad, expert_in, 0, 0))
+        add(wide_down_ref, down_scale * mul(rank_down, weighted, 0, 0))
+        add(hg_grad_ref, rank_scale * mul(rank_gu, gate_pre_grad, 0, 0))
+        add(hu_grad_ref, rank_scale * mul(rank_gu, up_pre_grad, 0, 0))
+        add(hd_grad_ref, mul(rank_down_grad, inner, 0, 0))
+        if index >= 2:
+            gather_own(index - 2)
+    for index in range(max(0, last - 1), last):
+        gather_own(index)
+    for index in range(max(0, last - 1)):
+        gather_other(index)
+    gather_own(last)
+    for step in range(1, in_set):
+        back(step).wait_recv()
 
     @pl.loop(0, rows // tile)
     def _(i):
@@ -606,7 +867,7 @@
         low[pl.ds(row, tile), :] = total.astype(bf16)
 
     def columns(owner):
-        return rows_ref.at[:, pl.ds(pl.multiple_of(owner * width, width), width)]
+        return rows_ref.at[:, columns_of(owner)]
 
     mine = pltpu.make_async_copy(low, columns(me), c_own)
     mine.start()
@@ -616,6 +877,8 @@
         copy = remote(low, columns(me), c_send.at[step], c_recv.at[step], target)
         copy.start()
         out.append(copy)
+    for index in range(max(0, last - 1), last + 1):
+        gather_other(index)
     for step in range(1, chips):
         out[step - 1].wait_recv()
         source = chip_peer(chip, core, chips - step, chips)
@@ -628,40 +891,55 @@
     out[chips - 1].wait_recv()
     for copy in out[chips:]:
         copy.wait_recv()
-    for copy in out + z_copies:
+    for copy in out:
         copy.wait_send()
-    for step in order:
-
-        @pl.loop(1, groups)
-        def _(turn, step=step):
-            sent(step, turn).wait_send()
-
-
-def collect(u, other, key, planes, groups, collective_id):
-    in_set, rows = key.shape[0], key.shape[1]
-    slot_total, full = u.shape
+    for step in range(1, in_set):
+        back(step).wait_send()
+    for index in range(max(0, last - 1), last + 1):
+        left_flow(index, flows[0])
+        left_flow(index, flows[1])
+
+
+def experts(
+    slots, w1, w2, hg, hu, hd, masks, mask_down, own, gain, key, names, planes, groups, collective_id
+):
+    in_set, rows = key.shape[0], key.shape[2]
+    full = slots.shape[2]
     width = full // groups
     chips = groups // 2
     tile = min(256, rows)
+    hidden, rank = hg.shape
+    down = hd.shape[1]
+    anywhere = pl.BlockSpec(memory_space=pl.ANY)
     return pl.pallas_call(
-        functools.partial(collect_kernel, planes, groups, in_set, tile),
+        functools.partial(experts_kernel, planes, groups, in_set, tile, names),
         out_shape=(
             jax.ShapeDtypeStruct((rows, width), f32),
             jax.ShapeDtypeStruct((rows, full), bf16),
             jax.ShapeDtypeStruct((in_set, rows, width), bf16),
+            jax.ShapeDtypeStruct((rank, full), f32),
+            jax.ShapeDtypeStruct((down, full), f32),
+            jax.ShapeDtypeStruct((rank, hidden), f32),
+            jax.ShapeDtypeStruct((rank, hidden), f32),
+            jax.ShapeDtypeStruct((down, hidden), f32),
         ),
-        in_specs=[VMEM, pl.BlockSpec(memory_space=pl.ANY), VMEM],
-        out_specs=(VMEM, VMEM, VMEM),
+        in_specs=[anywhere] + [VMEM] * 10,
+        out_specs=(VMEM, anywhere) + (VMEM,) * 6,
         scratch_shapes=[
+            pltpu.VMEM((2, 2, CAP, full), bf16),
+            pltpu.VMEM((2, CAP, full), bf16),
+            pltpu.VMEM((2, CAP, full), bf16),
             pltpu.VMEM((in_set, groups * CAP, width), bf16),
             pltpu.VMEM((in_set, groups * CAP, width), bf16),
             pltpu.VMEM((in_set - 1, rows, width), bf16),
             pltpu.VMEM((in_set - 1, rows, width), bf16),
             pltpu.VMEM((rows, width), bf16),
+            DMA((2,)),
             DMA((in_set, groups)),
             DMA((in_set, groups)),
-            DMA((in_set,)),
             DMA((in_set, groups)),
+            DMA((in_set, groups)),
+            DMA((2, in_set)),
             DMA((in_set - 1,)),
             DMA((in_set - 1,)),
             DMA,
@@ -671,10 +949,10 @@
             DMA((chips,)),
         ],
         compiler_params=pltpu.CompilerParams(
-            collective_id=collective_id, has_side_effects=True, vmem_limit_bytes=48 << 20
+            collective_id=collective_id, has_side_effects=True, vmem_limit_bytes=62 << 20
         ),
         cost_estimate=SMALL,
-    )(u, other, key)
+    )(slots, w1, w2, hg, hu, hd, masks, mask_down, own, gain, key)
 
 
 def planes_kernel(planes, x_ref, o_ref, own_sem, send_sem, recv_sem):
@@ -837,8 +1115,14 @@
     b_pick = pick(b_out, 0)
     pack_pick = pick(head_pack, 2)
 
-    routes_all = lax.all_gather(routes, "gx", axis=0, tiled=False)
-    adapters_all = lax.all_gather(adapter_ids, "gx", axis=0, tiled=False)
+    top = routes.shape[1]
+    whole = jnp.concatenate(
+        [routes.reshape(rows * top // 128, 128), jnp.zeros((8, 128), jnp.int32)], axis=0
+    )
+    whole = lax.dynamic_update_slice(whole, adapter_ids[None, :], (rows * top // 128, 0))
+    whole = gather_planes(whole, planes, 10)
+    routes_all = whole[:, : rows * top // 128].reshape(planes, rows, top)
+    adapters_all = whole[:, rows * top // 128, :nseq]
     dl = w_gate_up.shape[1]
     hl = exp_hidden.shape[1]
     qkv_width = 3 * heads_local * head_width
@@ -850,17 +1134,19 @@
         axis=1,
     )
     attn_weight = lax.all_gather(weight_shard, "gx", axis=0, tiled=True)
-    gathered = gather_columns(
+    normed_bf, scale_one, gathered = gather_normed(
         jnp.concatenate(
             [block_input, a_pick.transpose(0, 2, 1).reshape(3 * compact, width_local), b_pick],
             axis=0,
         ),
+        attn_gain,
+        rows,
         groups,
         1,
     )
-    full_rows = gathered[:rows]
-    a_full = gathered[rows : rows + 3 * compact]
-    b_full = gathered[rows + 3 * compact :]
+    scale_one = scale_one[:, :1]
+    a_full = gathered[: 3 * compact]
+    b_full = gathered[3 * compact :]
 
     set_cols = experts_local * compact
     fold = max(1, 128 // set_cols)
@@ -888,35 +1174,22 @@
     )
     (rank_shard,) = after(attn_weight, rank_shard)
     rank_weight = unfolded(lax.all_to_all(rank_shard, "gx", 0, 0, tiled=True))
-    down_pieces = []
-    waited = attn_weight
-    part_rows = dl // DOWN_PARTS
-    for part in range(DOWN_PARTS):
-        (down_later,) = after(waited, w_down)
-        pieces = own_pieces(
-            lambda p: lax.dynamic_slice(
-                down_later,
-                (lax.rem(p, experts_local), part * part_rows, 0),
-                (1, part_rows, hidden_width),
-            )[0]
-        )
-        waited = tuple(piece for _, piece in pieces)
-        down_pieces.append(pieces)
+    (down_later,) = after(attn_weight, w_down)
+    early_rows = dl * 5 // 8
+    early_pieces = own_pieces(
+        lambda p: lax.dynamic_slice(
+            down_later, (lax.rem(p, experts_local), 0, 0), (1, early_rows, hidden_width)
+        )[0]
+    )
 
     def rank_part(start, count):
         return rank_weight[:, start : start + count].reshape(planes * count, set_cols)
 
     wide_parts = [rank_part(c * dl, dl) for c in range(3)]
     hidden_gate, hidden_up, hidden_down = [rank_part(3 * dl + c * hl, hl) for c in range(3)]
-    rank_end = 2 * hidden_width + 2 * set_cols
-    second_weight = jnp.zeros((width, hidden_width + set_cols), bf16)
+    down_pad = -set_cols % 128
+    second_weight = jnp.zeros((width, hidden_width + set_cols + down_pad), bf16)
     second_weight = lax.dynamic_update_slice(second_weight, wide_parts[2], (0, hidden_width))
-    for part, pieces in enumerate(down_pieces):
-        for source, piece in pieces:
-            second_weight = lax.dynamic_update_slice(
-                second_weight, piece, (source * dl + part * part_rows, 0)
-            )
-
     expert_ids = own + experts_local * jnp.arange(groups, dtype=jnp.int32)
     set_start = (plane // experts_local) * experts_local
     step_plane = lax.rem(own - jnp.arange(experts_local) + experts_local, experts_local)
@@ -928,7 +1201,7 @@
     slot_key = jnp.where(hits.transpose(0, 2, 1), places.astype(jnp.int32), -1)
     slots = jnp.arange(CAP, dtype=jnp.int32)
     column_key = slot_key + CAP * jnp.arange(groups, dtype=jnp.int32)[None, :, None]
-    column_key = jnp.where(slot_key >= 0, column_key, -1).transpose(0, 2, 1)
+    column_key = jnp.where(slot_key >= 0, column_key, -1)
     own_key = lax.dynamic_index_in_dim(slot_key, column, 1, keepdims=False)
     own_pick = (own_key[:, None, :] == slots[None, :, None]).astype(bf16)
     rank_mask = (
@@ -937,14 +1210,14 @@
     ).astype(bf16)
     slot_total = experts_local * CAP
     mask_slot = dot("gst,gtr->gsr", own_pick, rank_mask).reshape(slot_total, set_cols)
-    valid = jnp.max(mask_slot, axis=1)
+
+    gate_up_flat = w_gate_up.reshape(experts_local, dl, 2 * hidden_width)
+    attn_weight, slot_key, column_key, mask_slot, gate_up_flat = lax.optimization_barrier(
+        (attn_weight, slot_key, column_key, mask_slot, gate_up_flat)
+    )
 
     col_start = column * width_local
     first_norm_gain = lax.dynamic_slice_in_dim(attn_gain, col_start, width_local)
-    input_f = full_rows.astype(f32)
-    scale_one = lax.rsqrt(jnp.mean(input_f * input_f, axis=-1, keepdims=True) + norm_eps)
-    hat_one = input_f * scale_one
-    normed_bf = (hat_one * attn_gain).astype(bf16)
     base = dot("td,de->te", normed_bf, attn_weight[:, :qkv_width]).reshape(
         rows, heads_local, 3, head_width
     )
@@ -990,142 +1263,104 @@
     rank_out_low = (rank_out * compact_mask[:, None, :]).astype(bf16)
     out_weight = attn_weight[:, qkv_width:]
     b_turned = (rank_scale * b_full.T).astype(bf16)
-    branch = scatter_product(
-        jnp.concatenate(
-            [
-                attn_bf.reshape(rows, heads_local * head_width),
-                rank_out_low.reshape(rows, heads_local * compact),
-            ],
-            axis=1,
-        ),
+    branch_left = jnp.concatenate(
+        [
+            attn_bf.reshape(rows, heads_local * head_width),
+            rank_out_low.reshape(rows, heads_local * compact),
+        ],
+        axis=1,
+    )
+    branch_left, *early = after(
+        query_scale, branch_left, *[piece for _, piece in early_pieces]
+    )
+    branch, late_pieces = scatter_product(
+        branch_left,
         jnp.concatenate([out_weight] + [b_turned] * heads_local, axis=1),
         groups,
         3,
-    )
+        w_down,
+        early_rows,
+        planes,
+    )
+    for (source, _), piece in zip(early_pieces, early):
+        second_weight = lax.dynamic_update_slice(second_weight, piece, (source * dl, 0))
+    for p in range(planes):
+        second_weight = lax.dynamic_update_slice(
+            second_weight, late_pieces[p], (p * dl + early_rows, 0)
+        )
     middle = block_input.astype(f32) + branch
     middle_low = middle.astype(bf16)
 
-    (spread_rows,) = after(waited, jnp.concatenate([middle_low, out_grad], axis=1))
     slot_rows, first_weight = spread(
-        spread_rows,
+        jnp.concatenate([middle_low, out_grad], axis=1),
         slot_key,
-        w_gate_up.reshape(experts_local, dl, 2 * hidden_width),
+        gate_up_flat,
         planes,
         groups,
-        rank_end + 2 * router.shape[1],
+        2 * hidden_width + 2 * set_cols + 128,
         4,
     )
-    middle_slot, grad_slot = slot_rows[0], slot_rows[1]
+    names = 2 * router.shape[1]
     first_weight = lax.dynamic_update_slice(
         first_weight,
-        jnp.concatenate([wide_parts[0], wide_parts[1], router, router], axis=1),
+        jnp.pad(
+            jnp.concatenate([wide_parts[0], wide_parts[1], router, router], axis=1),
+            ((0, 0), (0, 128 - names)),
+        ),
         (0, 2 * hidden_width),
     )
     both_rows = lax.all_gather(
         jnp.concatenate([middle_low, out_grad], axis=0), "gy", axis=1, tiled=True
     )
-    middle_slot = middle_slot.astype(f32)
-    slot_scale = lax.rsqrt(jnp.mean(middle_slot * middle_slot, axis=-1, keepdims=True) + norm_eps)
-    expert_in = (middle_slot * slot_scale * mlp_gain).astype(bf16)
-    pre_wide = jnp.dot(expert_in, first_weight, preferred_element_type=f32)
-    logits = pre_wide[:, rank_end : rank_end + router.shape[1]]
-    logit_raised = jnp.exp(logits - jnp.max(logits, axis=-1, keepdims=True))
-    route_probs = logit_raised / jnp.sum(logit_raised, axis=-1, keepdims=True)
+    no_rank = jnp.zeros((hidden_width, set_cols), bf16)
     own_id = column * experts_local + own
-    is_own = (jnp.arange(router.shape[1], dtype=jnp.int32) == own_id).astype(f32)[None, :]
-    gate = jnp.sum(route_probs * is_own, axis=1, keepdims=True) * valid[:, None]
-    two_masks = jnp.concatenate([mask_slot, mask_slot], axis=1)
-    rank_gu_low = (pre_wide[:, 2 * hidden_width : rank_end] * two_masks).astype(bf16)
-    gate_pre = pre_wide[:, :hidden_width] + rank_scale * dot(
-        "sr,fr->sf", rank_gu_low[:, :set_cols], hidden_gate
-    )
-    up_pre = pre_wide[:, hidden_width : 2 * hidden_width] + rank_scale * dot(
-        "sr,fr->sf", rank_gu_low[:, set_cols:], hidden_up
-    )
-    sigma = jax.nn.sigmoid(gate_pre)
-    activated = gate_pre * sigma
-    inner_bf = (activated * up_pre).astype(bf16)
-    rank_down = dot("sf,fr->sr", inner_bf, hidden_down)
-    rank_down_low = (rank_down * mask_slot).astype(bf16)
-    inner_wide = jnp.concatenate([inner_bf, (down_scale * rank_down_low).astype(bf16)], axis=1)
-    expert_output = dot("sf,df->sd", inner_wide, second_weight)
-    grad_slot_f = grad_slot.astype(f32)
-    gate_grad = jnp.sum(grad_slot_f * expert_output, axis=-1, keepdims=True)
-    out_grad_bf = (gate * grad_slot_f).astype(bf16)
-    inner_wide_grad = dot("sd,df->sf", out_grad_bf, second_weight)
-    rank_down_grad = (down_scale * inner_wide_grad[:, hidden_width:] * mask_slot).astype(bf16)
-    inner_grad = inner_wide_grad[:, :hidden_width] + dot("sr,fr->sf", rank_down_grad, hidden_down)
-    gate_pre_grad = (inner_grad * up_pre * sigma * (1.0 + gate_pre * (1.0 - sigma))).astype(bf16)
-    up_pre_grad = (inner_grad * activated).astype(bf16)
-    rank_gu_grad = (
-        rank_scale
-        * jnp.concatenate(
-            [
-                dot("sf,fr->sr", gate_pre_grad, hidden_gate),
-                dot("sf,fr->sr", up_pre_grad, hidden_up),
-            ],
-            axis=1,
-        )
-        * two_masks
-    ).astype(bf16)
-    logit_grad = (is_own - route_probs) * (gate * gate_grad)
-    logit_high = logit_grad.astype(bf16)
-    logit_rest = (logit_grad - logit_high.astype(f32)).astype(bf16)
-    pre_wide_grad = jnp.concatenate(
-        [gate_pre_grad, up_pre_grad, rank_gu_grad, logit_high, logit_rest], axis=1
-    )
-    rows_grad = dot("sf,df->sd", pre_wide_grad, first_weight)
-    weighted = (gate * expert_output).astype(bf16)
-    weighted = weighted.reshape(slot_total, groups, width_local).transpose(1, 0, 2)
-    normed_two_part, normed_two_rows, moe_planes = collect(
-        rows_grad.astype(bf16),
-        lax.all_to_all(weighted, "gy", 0, 0, tiled=True),
+    is_own = (jnp.arange(names, dtype=jnp.int32) % router.shape[1] == own_id).astype(f32)
+    (
+        normed_two_part,
+        normed_two_rows,
+        moe_planes,
+        wide_gu_grad,
+        wide_down_grad,
+        gate_rank_grad,
+        up_rank_grad,
+        down_rank_grad,
+    ) = experts(
+        slot_rows,
+        first_weight,
+        second_weight,
+        jnp.concatenate([hidden_gate, no_rank], axis=1),
+        jnp.concatenate([no_rank, hidden_up], axis=1),
+        jnp.pad(hidden_down, ((0, 0), (0, down_pad))),
+        jnp.concatenate([mask_slot, mask_slot], axis=1),
+        jnp.pad(mask_slot, ((0, 0), (0, down_pad))),
+        jnp.pad(is_own, (0, 128 - names)).reshape(1, 128),
+        mlp_gain.reshape(1, width),
         column_key,
+        names,
         planes,
         groups,
         5,
     )
-    moe_part = moe_planes[0].astype(f32)
-    for step in range(1, experts_local):
-        moe_part = moe_part + shifted(moe_planes[step], experts_local - step).astype(f32)
-    layer_out = (middle + moe_part).astype(bf16)
+    moe_pieces = [
+        shifted(moe_planes[step], experts_local - step) for step in range(1, experts_local)
+    ]
 
     wide_grads = [
-        dot("sd,sr->dr", expert_in, rank_gu_grad[:, :set_cols]),
-        dot("sd,sr->dr", expert_in, rank_gu_grad[:, set_cols:]),
-        down_scale * dot("sd,sr->dr", out_grad_bf, rank_down_low),
+        wide_gu_grad[:set_cols],
+        wide_gu_grad[set_cols:],
+        wide_down_grad[:set_cols],
     ]
     hidden_grads = [
-        rank_scale * dot("sf,sr->fr", gate_pre_grad, rank_gu_low[:, :set_cols]),
-        rank_scale * dot("sf,sr->fr", up_pre_grad, rank_gu_low[:, set_cols:]),
-        dot("sf,sr->fr", inner_bf, rank_down_grad),
+        gate_rank_grad[:set_cols],
+        up_rank_grad[set_cols:],
+        down_rank_grad[:set_cols],
     ]
     rank_grads = jnp.concatenate(
-        [x.astype(bf16).reshape(planes, dl, set_cols) for x in wide_grads]
-        + [x.astype(bf16).reshape(planes, hl, set_cols) for x in hidden_grads],
+        [x.astype(bf16).T.reshape(planes, dl, set_cols) for x in wide_grads]
+        + [x.astype(bf16).T.reshape(planes, hl, set_cols) for x in hidden_grads],
         axis=1,
     )
-    (rank_grads,) = after(normed_two_rows, rank_grads)
-    rank_grads = unfolded(lax.all_to_all(folded(rank_grads), "gx", 0, 0, tiled=True))
-    rank_grads = rank_grads.reshape((repeats, experts_local) + rank_grads.shape[1:])
-    wide_sum = jnp.stack(
-        [
-            dot("semk,srk->emr", rank_grads[:, :, c * dl : (c + 1) * dl], set_pick)
-            for c in range(3)
-        ],
-        axis=2,
-    )
-    hidden_sum = jnp.stack(
-        [
-            dot(
-                "semk,srk->emr",
-                rank_grads[:, :, 3 * dl + c * hl : 3 * dl + (c + 1) * hl],
-                set_pick,
-            )
-            for c in range(3)
-        ],
-        axis=2,
-    )
+    rank_grads = lax.all_to_all(folded(rank_grads), "gx", 0, 0, tiled=True)
 
     middle_rows = both_rows[:rows].astype(f32)
     grad_rows = both_rows[rows:].astype(f32)
@@ -1201,9 +1436,9 @@
     pack_b_grad = rank_scale * dot("tcr,thce->rhce", rank_low, pre_grad)
     normed_one_grad = scatter_product(
         pre_grad.reshape(rows, qkv_width), attn_weight[:, :qkv_width], groups, 7
-    )
+    )[0]
     adapter_input_gradient = dot("crt,cdr->td", rank_grad_bf, a_pick)
-    first_normalized_shard = lax.dynamic_slice_in_dim(hat_one, col_start, width_local, axis=1)
+    first_normalized_shard = block_input.astype(f32) * scale_one
     normed_local_bf = lax.dynamic_slice_in_dim(normed_bf, col_start, width_local, axis=1)
     a_rows_grad = dot("td,crt->rcd", normed_local_bf, rank_grad_bf)
     scaled_one = (normed_one_grad + adapter_input_gradient) * first_norm_gain
@@ -1212,6 +1447,32 @@
     input_grad = middle_grad + scale_one * (
         scaled_one - first_normalized_shard * stat_one_sum / width
     )
+    rank_grads, *moe_pieces = after(normed_one_grad, rank_grads, *moe_pieces)
+    moe_part = moe_planes[0].astype(f32)
+    for piece in moe_pieces:
+        moe_part = moe_part + piece.astype(f32)
+    layer_out = (middle + moe_part).astype(bf16)
+    rank_grads = unfolded(rank_grads)
+    rank_grads = rank_grads.reshape((repeats, experts_local) + rank_grads.shape[1:])
+    wide_sum = jnp.stack(
+        [
+            dot("semk,srk->emr", rank_grads[:, :, c * dl : (c + 1) * dl], set_pick)
+            for c in range(3)
+        ],
+        axis=2,
+    )
+    hidden_sum = jnp.stack(
+        [
+            dot(
+                "semk,srk->emr",
+                rank_grads[:, :, 3 * dl + c * hl : 3 * dl + (c + 1) * hl],
+                set_pick,
+            )
+            for c in range(3)
+        ],
+        axis=2,
+    )
+
     pack_grad = jnp.concatenate(
         [
             pack_b_grad.transpose(1, 2, 0, 3),

time: 1060 us -> 855 us (0.81)
  matrix products: 122 us -> 53.3 us
  waiting for transfers between devices: 91.4 us -> 32.9 us
  other arithmetic: 79.7 us -> 46 us
  local copies, waits for them, and re-layouts: 148 us -> 122 us
  blocking collectives: 24 us -> 0 us
    ppermute x3, waiting for transfers between devices: 62.6 us -> 0.01 us  [shifted(): return lax.ppermute(x, 'gx', pairs)]
    dot_general x47 -> x32, matrix products: 103 us -> 52.1 us  [dot(): return jnp.einsum(spec, left, right, preferred_element_type=f32)]
    dynamic_slice x10 -> x0, local copies, waits for them, and re-layouts: 19.5 us -> none  [shards(): lax.dynamic_slice(down_later, (lax.rem(p, experts_local), part * part_row...]
    dot_general x1 -> x0, matrix products: 17.6 us -> none  [shards(): pre_wide = jnp.dot(expert_in, first_weight, preferred_element_type=f32)]
    pallas_call x4, Pallas kernels: 237 us -> 254 us  [the longest x1 148 us: experts(): pl.pallas_call(functools.partial(experts_kernel, planes, groups, in_set,...]
    pallas_call x1, Pallas kernels: 264 us -> 247 us  [spread(): pl.pallas_call(functools.partial(spread_kernel, planes, groups, in_set),...]
    ppermute x6 -> x3, waiting for transfers between devices: 14.9 us -> 31.4 us  [own_pieces(): piece = lax.ppermute(piece, 'gx', pairs)]
    all_gather x1 -> x0, blocking collectives: 15.8 us -> none  [shards(): routes_all = lax.all_gather(routes, 'gx', axis=0, tiled=False)]
  transfers between devices with their start and end apart: 14 -> 10, of which waited for: 4 -> 3; matrix products, arithmetic and copies ran while one was open for 21% -> 20% of each run, Pallas kernels for 45% -> 58%
where the time goes in v3:
time: 855 us; the launch traced here: 843 us
  Pallas kernels  548 us (64%)
  local copies, waits for them, and re-layouts  122 us (14%)
  matrix products  53.3 us (6%)
  other arithmetic  46 us (5%)
  waiting for transfers between devices  32.9 us (4%)
  starting transfers between devices  23.5 us (3%)
  between operations  17.1 us (2%)
    pallas_call x1, Pallas kernels, spread(): pl.pallas_call(functools.partial(spread_kernel, planes, groups, in_set),...  247 us
    pallas_call x1, Pallas kernels, experts(): pl.pallas_call(functools.partial(experts_kernel, planes, groups, in_set,...  148 us
    pallas_call x2, Pallas kernels, scatter_product(): pl.pallas_call(body, out_shape=out_shape, in_specs=in_specs, out_specs=ou...  75.9 us
    dot_general x32, matrix products, dot(): return jnp.einsum(spec, left, right, preferred_element_type=f32)  52.1 us
    ppermute x3, waiting for transfers between devices, own_pieces(): piece = lax.ppermute(piece, 'gx', pairs)  31.4 us
    pallas_call x1, Pallas kernels, gather_normed(): pl.pallas_call(functools.partial(gather_kernel, chips, rows, 64), out_sha...  31 us
    unnamed x243, local copies, waits for them, and re-layouts  25.5 us
    pallas_call x2, Pallas kernels, gather_planes(): pl.pallas_call(functools.partial(planes_kernel, planes), out_shape=jax.Sh...  21.7 us
  transfers between devices with their start and end apart: 10, of which 3 were waited for; matrix products, arithmetic and copies ran while one was open for 20% of the time, Pallas kernels for 58%

profile of v3, /device:TPU:0, one launch (start us, length us, event | category | flops | bytes accessed | tf_op | source)
XLA Modules:
  0.0 843.4 jit_solution(1677090073405013570)
XLA Ops:
  14.9 10.2 %shard_map.226 = s32[4,72,128]{2,1,0:T(8,128)} custom-call(s32[72,128]{1,0:T(8,128)} %copy-done.67), custom_call_target="tpu_custom_call" | custom-call | bytes 65536 | tf_op jit(solution)/shard_map/pallas_call | solution.py:985
  32.8 14.5 %reshape.1209.w_ref = bf16[4,512,2048]{2,1,0:T(8,128)(2,1)} reshape(bf16[4,512,2,1024]{3,2,1,0:T(2,128)(2,1)} %param.32) | data formatting | bytes 16777216 | tf_op jit(solution)/shard_map/reshape | solution.py:1214
  52.6 31.0 %shard_map.225 = (bf16[1024,2048]{1,0:T(8,128)(2,1)S(1)}, f32[1024,128]{1,0:T(8,128)S(1)}, bf16[64,2048]{1,0:T(8,128)(2,1)S(1)}) custom-call(bf16[1088,256]{1,0:T(8,128)(2,1)S(1)} %pad_maximum_fusion.16.x_ref, f32[1,2048]{1,0:T(1,128)S(1)} %bitcast.406), custom_call_target="tpu_custom_call" | custom-call | bytes 65536 | tf_op jit(solution)/shard_map/pallas_call | solution.py:127
  90.5 3.6 fusion.111
  95.7 6.2 fusion.162
  105.1 6.2 shard_map.227
  131.7 4.1 collective-permute-done
  135.8 27.3 %collective-permute-done.1 = bf16[320,1024]{1,0:T(8,128)(2,1)} collective-permute-done((bf16[320,1024]{1,0:T(8,128)(2,1)}, bf16[320,1024]{1,0:T(8,128)(2,1)}, u32[]{:S(2)}, u32[]{:S(2)}) %collective-permute-start.1) | collective-permute-done | bytes 655392 | tf_op jit(solution)/shard_map/ppermute | solution.py:1091
  163.1 44.1 %shard_map.228 = (f32[1024,256]{1,0:T(8,128)S(1)}, bf16[4,192,1024]{2,1,0:T(8,128)(2,1)S(1)}) custom-call(bf16[1024,288]{1,0:T(8,128)(2,1)S(1)} %pad_maximum_fusion.14.l_ref, bf16[2048,288]{1,0:T(8,128)(2,1)S(1)} %pad_maximum_fusion.1.r_ref, bf16[4,512,1024]{2,1,0:T(8,128)(2,1)} %w_ref.1), custom_call_target="tpu_custom_call" | custom-call | bytes 65536 | tf_op jit(solution)/shard_map/pallas_call | solution.py:286
  219.9 9.9 %all-to-all-start = ((bf16[4,1152,128]{1,2,0:T(8,128)(2,1)}), bf16[4,1152,128]{1,2,0:T(8,128)(2,1)}, u32[]{:S(2)}, u32[]{:S(2)}) async-start(bf16[4,1152,128]{1,2,0:T(8,128)(2,1)} %pad_maximum_fusion.8), calls=%async_computation | async-start | bytes 2359296 | tf_op jit(solution)/shard_map/all_to_all | solution.py:1176
  238.0 3.9 slice.248.r_ref
  245.5 247.3 %shard_map.229 = (bf16[2,1152,2048]{2,1,0:T(8,128)(2,1)}, bf16[2048,2304]{1,0:T(8,128)(2,1)}) custom-call(bf16[1024,512]{1,0:T(8,128)(2,1)S(1)} %pad_maximum_fusion.10.x_ref, s32[4,8,1024]{2,1,0:T(8,128)S(1)} %get-tuple-element.44.key_ref, bf16[4,512,2048]{2,1,0:T(8,128)(2,1)} %reshape.1209.w_ref), custom_call_target="tpu_custom_call" | custom-call | bytes 65536 | tf_op jit(solution)/shard_map/pallas_call | solution.py:572
  501.0 3.7 dynamic_update_slice.35
  524.4 147.6 %shard_map.230 = (f32[1024,256]{1,0:T(8,128)}, bf16[1024,2048]{1,0:T(8,128)(2,1)}, bf16[4,1024,256]{2,1,0:T(8,128)(2,1)}, f32[128,2048]{1,0:T(8,128)}, f32[128,2...) custom-call(bf16[2,1152,2048]{2,1,0:T(8,128)(2,1)} %get-tuple-element.46.slots_ref, ...), custom_call_target="tpu_custom_call" | custom-call | bytes 65536 | tf_op jit(solution)/shard_map/pallas_call | solution.py:914
  677.5 4.3 all-to-all-start.1
  683.0 3.8 collective-permute-start.3
  691.5 4.1 fusion.2
  703.0 5.1 fusion.11
  708.2 4.6 multiply_reduce_fusion
  723.3 7.3 concatenate.122
  732.3 12.4 %shard_map.231 = f32[128,1024]{1,0:T(8,128)} custom-call(bf16[128,1024]{1,0:T(8,128)(2,1)} %pad.29.x_ref), custom_call_target="tpu_custom_call" | custom-call | bytes 65536 | tf_op jit(solution)/shard_map/pallas_call | solution.py:379
  756.6 11.5 %shard_map.234 = bf16[4,16,2048]{2,1,0:T(8,128)(2,1)} custom-call(bf16[16,2048]{1,0:T(8,128)(2,1)} %pad_maximum_fusion.24.x_ref), custom_call_target="tpu_custom_call" | custom-call | bytes 65536 | tf_op jit(solution)/shard_map/pallas_call | solution.py:985
  774.5 31.7 %shard_map.232 = f32[1024,256]{1,0:T(8,128)S(1)} custom-call(bf16[1024,768]{1,0:T(8,128)(2,1)S(1)} %copy.182.l_ref, bf16[2048,768]{1,0:T(8,128)(2,1)S(1)} %copy-done.1), custom_call_target="tpu_custom_call" | custom-call | bytes 65536 | tf_op jit(solution)/shard_map/pallas_call | solution.py:286
  817.4 6.3 shard_map.233
  (432 shorter events, 175.8 us)
Async XLA Ops:
  7.2 94.8 %copy-start = (bf16[2,4,128,128]{3,2,1,0:T(8,128)(2,1)S(1)}, bf16[2,4,128,128]{3,2,1,0:T(8,128)(2,1)}, u32[]{:S(2)}) copy-start(bf16[2,4,128,128]{3,2,1,0:T(8,128)(2,1)} %param.30) | copy-start | bytes 786436
  7.2 88.5 %all-gather.3.cloned.1.call-start = ((), (), s32[]{:S(2)}) async-start(), calls=%async_computation.2 | async-start | bytes 5242880 | tf_op jit(solution)/shard_map/all_gather | solution.py:1136
  12.1 676.0 %all-gather.5.cloned.1.call-start = ((), (), s32[]{:S(2)}) async-start(), calls=%async_computation.3 | async-start | bytes 9437184 | tf_op jit(solution)/shard_map/all_gather | solution.py:1312
  32.8 14.5 %copy-start.112 = (s32[1,2]{1,0:T(1,128)S(1)}, s32[1,2]{1,0:T(1,128)}, u32[]{:S(2)}) copy-start(s32[1,2]{1,0:T(1,128)} %param.22) | copy-start | bytes 28
  87.4 32.8 %copy-start.94 = (f32[1,256]{1,0:T(1,128)}, f32[1,256]{1,0:T(1,128)S(1)}, u32[]{:S(2)}) copy-start(f32[1,256]{1,0:T(1,128)S(1)} %get-tuple-element.138) | copy-start | bytes 3076
  87.4 32.8 %copy-start.96 = (f32[1,256]{1,0:T(1,128)}, f32[1,256]{1,0:T(1,128)S(1)}, u32[]{:S(2)}) copy-start(f32[1,256]{1,0:T(1,128)S(1)} %get-tuple-element.139) | copy-start | bytes 3076
  87.4 149.3 %copy-start.77 = (s32[1024]{0:T(1024)}, s32[1024]{0:T(1024)S(1)}, u32[]{:S(2)}) copy-start(s32[1024]{0:T(1024)S(1)} %add_select_fusion.1) | copy-start | bytes 12292
  87.6 14.4 %copy-start.58 = (f32[1024,16]{0,1:T(8,128)}, f32[1024,16]{0,1:T(8,128)S(1)}, u32[]{:S(2)}) copy-start(f32[1024,16]{0,1:T(8,128)S(1)} %compare_convert_fusion) | copy-start | bytes 196612
  88.6 31.9 %copy-start.31 = (f32[1024,64]{0,1:T(8,128)}, f32[1024,64]{0,1:T(8,128)S(1)}, u32[]{:S(2)}) copy-start(f32[1024,64]{0,1:T(8,128)S(1)} %get-tuple-element.146) | copy-start | bytes 786436
  88.6 31.9 %copy-start.33 = (f32[1024,64]{0,1:T(8,128)}, f32[1024,64]{0,1:T(8,128)S(1)}, u32[]{:S(2)}) copy-start(f32[1024,64]{0,1:T(8,128)S(1)} %get-tuple-element.147) | copy-start | bytes 786436
  116.0 19.8 %collective-permute-start = (bf16[320,1024]{1,0:T(8,128)(2,1)}, bf16[320,1024]{1,0:T(8,128)(2,1)}, u32[]{:S(2)}, u32[]{:S(2)}) collective-permute-start(bf16[320,1024]{1,0:T(8,128)(2,1)} %get-tuple-element.98), channel_id=1, source_target_pairs={{0,8},{8,16},{16,24},{24,0},{1,9},{9,17},{17,25},{25,1},{2,10},{10... | collective-permute-start | bytes 1966088 | tf_op jit(solution)/shard_map/ppermute | solution.py:1091
  116.8 46.3 %collective-permute-start.1 = (bf16[320,1024]{1,0:T(8,128)(2,1)}, bf16[320,1024]{1,0:T(8,128)(2,1)}, u32[]{:S(2)}, u32[]{:S(2)}) collective-permute-start(bf16[320,1024]{1,0:T(8,128)(2,1)} %get-tuple-element.97), channel_id=1, source_target_pairs={{0,16},{8,24},{16,0},{24,8},{1,17},{9,25},{17,1},{25,9},{2,18},{10... | collective-permute-start | bytes 1966088 | tf_op jit(solution)/shard_map/ppermute | solution.py:1091
  119.1 44.0 %collective-permute-start.2 = (bf16[320,1024]{1,0:T(8,128)(2,1)}, bf16[320,1024]{1,0:T(8,128)(2,1)}, u32[]{:S(2)}, u32[]{:S(2)}) collective-permute-start(bf16[320,1024]{1,0:T(8,128)(2,1)} %get-tuple-element.96), channel_id=1, source_target_pairs={{0,24},{8,0},{16,8},{24,16},{1,25},{9,1},{17,9},{25,17},{2,26},{10... | collective-permute-start | bytes 1966088 | tf_op jit(solution)/shard_map/ppermute | solution.py:1091
  163.1 44.2 %copy-start.15 = (bf16[1024,256]{1,0:T(8,128)(2,1)S(1)}, bf16[1024,256]{1,0:T(8,128)(2,1)}, u32[]{:S(2)}) copy-start(bf16[1024,256]{1,0:T(8,128)(2,1)} %param.18) | copy-start | bytes 1572868
  163.1 45.1 %copy-start.21 = (bf16[1024,256]{1,0:T(8,128)(2,1)S(1)}, bf16[1024,256]{1,0:T(8,128)(2,1)}, u32[]{:S(2)}) copy-start(bf16[1024,256]{1,0:T(8,128)(2,1)} %param.19) | copy-start | bytes 1572868
  218.8 15.3 %copy-start.106 = (s32[4,1,1,16]{3,0,2,1:T(4,128)S(1)}, s32[4,1,1,16]{3,0,2,1:T(4,128)}, u32[]{:S(2)}) copy-start(s32[4,1,1,16]{3,0,2,1:T(4,128)} %iota_add_fusion) | copy-start | bytes 772
  219.9 272.9 %all-to-all-start = ((bf16[4,1152,128]{1,2,0:T(8,128)(2,1)}), bf16[4,1152,128]{1,2,0:T(8,128)(2,1)}, u32[]{:S(2)}, u32[]{:S(2)}) async-start(bf16[4,1152,128]{1,2,0:T(8,128)(2,1)} %pad_maximum_fusion.8), calls=%async_computation | async-start | bytes 2359296 | tf_op jit(solution)/shard_map/all_to_all | solution.py:1176
  677.5 129.8 %all-to-all-start.1 = ((bf16[4,1152,128]{1,2,0:T(8,128)(2,1)}), bf16[4,1152,128]{1,2,0:T(8,128)(2,1)}, u32[]{:S(2)}, u32[]{:S(2)}) async-start(bf16[4,1152,128]{1,2,0:T(8,128)(2,1)} %fusion.33), calls=%async_computation.1 | async-start | bytes 2359296 | tf_op jit(solution)/shard_map/all_to_all | solution.py:1363
  683.0 124.2 %collective-permute-start.3 = (bf16[1024,256]{1,0:T(8,128)(2,1)}, bf16[1024,256]{1,0:T(8,128)(2,1)}, u32[]{:S(2)}, u32[]{:S(2)}) collective-permute-start(bf16[1024,256]{1,0:T(8,128)(2,1)} %get-tuple-element.106), channel_id=1, source_target_pairs={{0,24},{8,0},{16,8},{24,16},{1,25},{9,1},{17,9},{25,17},{2,26},{10... | collective-permute-start | bytes 1572872 | tf_op jit(solution)/shard_map/ppermute | solution.py:1083
  686.8 120.5 %collective-permute-start.4 = (bf16[1024,256]{1,0:T(8,128)(2,1)}, bf16[1024,256]{1,0:T(8,128)(2,1)}, u32[]{:S(2)}, u32[]{:S(2)}) collective-permute-start(bf16[1024,256]{1,0:T(8,128)(2,1)} %get-tuple-element.105), channel_id=1, source_target_pairs={{0,16},{8,24},{16,0},{24,8},{1,17},{9,25},{17,1},{25,9},{2,18},{10... | collective-permute-start | bytes 1572872 | tf_op jit(solution)/shard_map/ppermute | solution.py:1083
  686.8 120.5 %collective-permute-start.5 = (bf16[1024,256]{1,0:T(8,128)(2,1)}, bf16[1024,256]{1,0:T(8,128)(2,1)}, u32[]{:S(2)}, u32[]{:S(2)}) collective-permute-start(bf16[1024,256]{1,0:T(8,128)(2,1)} %get-tuple-element.104), channel_id=1, source_target_pairs={{0,8},{8,16},{16,24},{24,0},{1,9},{9,17},{17,25},{25,1},{2,10},{10... | collective-permute-start | bytes 1572872 | tf_op jit(solution)/shard_map/ppermute | solution.py:1083
  708.1 14.4 %copy-start.26 = (bf16[2,128,1024]{2,1,0:T(8,128)(2,1)}, bf16[2,128,1024]{2,1,0:T(8,128)(2,1)S(1)}, u32[]{:S(2)}) copy-start(bf16[2,128,1024]{2,1,0:T(8,128)(2,1)S(1)} %fusion.11) | copy-start | bytes 1572868
  720.9 27.7 %copy-start.89 = (f32[2,1024]{1,0:T(2,128)S(1)}, f32[2,1024]{1,0:T(2,128)}, u32[]{:S(2)}) copy-start(f32[2,1024]{1,0:T(2,128)} %pad_maximum_fusion.26) | copy-start | bytes 24580
  752.8 15.3 %copy-start.111 = (s32[64]{0:T(128)S(1)}, s32[64]{0:T(128)}, u32[]{:S(2)}) copy-start(s32[64]{0:T(128)} %add.387) | copy-start | bytes 772
  (103 other events, 404.9 us)
Sparse Core Ops, SparseCore 0:
  12.2 83.4 all-gather.2
  209.4 60.7 all-gather.4

commit v4 on v3

--- a/solution.py
+++ b/solution.py
@@ -602,8 +602,10 @@
     tile,
     names,
     slots_ref,
-    w1_ref,
-    w2_ref,
+    w1_main_ref,
+    w1_tail_ref,
+    late_ref,
+    w2_tail_ref,
     hg_ref,
     hu_ref,
     hd_ref,
@@ -612,36 +614,44 @@
     own_ref,
     gain_ref,
     key_ref,
-    shard_ref,
-    rows_ref,
-    placed_ref,
-    wide_ref,
-    wide_down_ref,
-    hg_grad_ref,
-    hu_grad_ref,
-    hd_grad_ref,
-    slot_buf,
-    u_stage,
-    m_stage,
-    got,
-    other,
-    out_z,
-    in_z,
-    low,
-    slot_sem,
-    g_send,
-    g_recv,
-    m_send,
-    m_recv,
-    own_sem,
-    z_send,
-    z_recv,
-    c_own,
-    c_send,
-    c_recv,
-    p_send,
-    p_recv,
+    *rest,
 ):
+    early_refs = rest[:planes]
+    (
+        shard_ref,
+        rows_ref,
+        placed_ref,
+        wide_ref,
+        wide_down_ref,
+        hg_grad_ref,
+        hu_grad_ref,
+        hd_grad_ref,
+        w1_ref,
+        w2_ref,
+        slot_buf,
+        u_stage,
+        m_stage,
+        got,
+        other,
+        out_z,
+        in_z,
+        low,
+        w1_sem,
+        w2_sem,
+        slot_sem,
+        g_send,
+        g_recv,
+        m_send,
+        m_recv,
+        own_sem,
+        z_send,
+        z_recv,
+        c_own,
+        c_send,
+        c_recv,
+        p_send,
+        p_recv,
+    ) = rest[planes:]
     plane, own, base = plane_place(in_set)
     me, chip, core, sibling = place_in_column()
     chips = groups // 2
@@ -772,6 +782,42 @@
 
     load(0).start()
     load(1).start()
+    first_cols = w1_main_ref.shape[1]
+    w1_loads = [
+        pltpu.make_async_copy(w1_main_ref, w1_ref.at[:, pl.ds(0, first_cols)], w1_sem.at[0]),
+        pltpu.make_async_copy(
+            w1_tail_ref,
+            w1_ref.at[:, pl.ds(first_cols, w1_tail_ref.shape[1])],
+            w1_sem.at[1],
+        ),
+    ]
+    early_rows, late_rows = early_refs[0].shape[0], late_ref.shape[1]
+    depth = early_rows + late_rows
+    w2_loads = [
+        pltpu.make_async_copy(
+            w2_tail_ref, w2_ref.at[:, pl.ds(hidden, w2_tail_ref.shape[1])], w2_sem.at[2 * planes]
+        )
+    ]
+    for number in range(planes):
+        source = lax.rem(plane - number + planes, planes)
+        w2_loads.append(
+            pltpu.make_async_copy(
+                early_refs[number],
+                w2_ref.at[
+                    pl.ds(pl.multiple_of(source * depth, 16), early_rows), pl.ds(0, hidden)
+                ],
+                w2_sem.at[number],
+            )
+        )
+        w2_loads.append(
+            pltpu.make_async_copy(
+                late_ref.at[number],
+                w2_ref.at[pl.ds(number * depth + early_rows, late_rows), pl.ds(0, hidden)],
+                w2_sem.at[planes + number],
+            )
+        )
+    for copy in w1_loads + w2_loads:
+        copy.start()
     greet_all(planes, groups)
     lane = lax.broadcasted_iota(jnp.int32, (CAP, 128), 1)
     for index, step in enumerate(order):
@@ -780,6 +826,9 @@
         middle = slot_buf[index % 2, 0].astype(f32)
         scale = lax.rsqrt(jnp.mean(middle * middle, axis=-1, keepdims=True) + norm_eps)
         expert_in = (middle * scale * gain_ref[...]).astype(bf16)
+        if index == 0:
+            for copy in w1_loads:
+                copy.wait()
         pre = mul(expert_in, w1_ref[...], 1, 0)
         both_masks = mask_ref[at, :]
         mask_down = mask_down_ref[at, :]
@@ -801,6 +850,9 @@
         inner_wide = jnp.concatenate(
             [inner, (down_scale * rank_down.astype(f32)).astype(bf16)], axis=1
         )
+        if index == 0:
+            for copy in w2_loads:
+                copy.wait()
         output = mul(inner_wide, w2_ref[...], 1, 1)
         cotangent = slot_buf[index % 2, 1].astype(f32)
         gate_grad = jnp.sum(cotangent * output, axis=1, keepdims=True)
@@ -901,7 +953,24 @@
 
 
 def experts(
-    slots, w1, w2, hg, hu, hd, masks, mask_down, own, gain, key, names, planes, groups, collective_id
+    slots,
+    w1_main,
+    w1_tail,
+    early,
+    late,
+    w2_tail,
+    hg,
+    hu,
+    hd,
+    masks,
+    mask_down,
+    own,
+    gain,
+    key,
+    names,
+    planes,
+    groups,
+    collective_id,
 ):
     in_set, rows = key.shape[0], key.shape[2]
     full = slots.shape[2]
@@ -923,9 +992,11 @@
             jax.ShapeDtypeStruct((rank, hidden), f32),
             jax.ShapeDtypeStruct((down, hidden), f32),
         ),
-        in_specs=[anywhere] + [VMEM] * 10,
+        in_specs=[anywhere] * 5 + [VMEM] * 8 + [anywhere] * planes,
         out_specs=(VMEM, anywhere) + (VMEM,) * 6,
         scratch_shapes=[
+            pltpu.VMEM((full, w1_main.shape[1] + w1_tail.shape[1]), bf16),
+            pltpu.VMEM((full, hidden + w2_tail.shape[1]), bf16),
             pltpu.VMEM((2, 2, CAP, full), bf16),
             pltpu.VMEM((2, CAP, full), bf16),
             pltpu.VMEM((2, CAP, full), bf16),
@@ -934,6 +1005,8 @@
             pltpu.VMEM((in_set - 1, rows, width), bf16),
             pltpu.VMEM((in_set - 1, rows, width), bf16),
             pltpu.VMEM((rows, width), bf16),
+            DMA((2,)),
+            DMA((2 * planes + 1,)),
             DMA((2,)),
             DMA((in_set, groups)),
             DMA((in_set, groups)),
@@ -952,7 +1025,9 @@
             collective_id=collective_id, has_side_effects=True, vmem_limit_bytes=62 << 20
         ),
         cost_estimate=SMALL,
-    )(slots, w1, w2, hg, hu, hd, masks, mask_down, own, gain, key)
+    )(
+        slots, w1_main, w1_tail, late, w2_tail, hg, hu, hd, masks, mask_down, own, gain, key, *early
+    )
 
 
 def planes_kernel(planes, x_ref, o_ref, own_sem, send_sem, recv_sem):
@@ -1092,11 +1167,6 @@
             pieces.append((lax.rem(plane - step + planes, planes), piece))
         return pieces
 
-    def assembled(pieces, buffer, start=0):
-        for source, piece in pieces:
-            buffer = lax.dynamic_update_slice(buffer, piece, (source * piece.shape[0], start))
-        return buffer
-
     compact = nseq * RANK
 
     def pick(x, axis):
@@ -1172,24 +1242,6 @@
         .reshape(planes, rank_rows.shape[1], set_cols)
         .astype(bf16)
     )
-    (rank_shard,) = after(attn_weight, rank_shard)
-    rank_weight = unfolded(lax.all_to_all(rank_shard, "gx", 0, 0, tiled=True))
-    (down_later,) = after(attn_weight, w_down)
-    early_rows = dl * 5 // 8
-    early_pieces = own_pieces(
-        lambda p: lax.dynamic_slice(
-            down_later, (lax.rem(p, experts_local), 0, 0), (1, early_rows, hidden_width)
-        )[0]
-    )
-
-    def rank_part(start, count):
-        return rank_weight[:, start : start + count].reshape(planes * count, set_cols)
-
-    wide_parts = [rank_part(c * dl, dl) for c in range(3)]
-    hidden_gate, hidden_up, hidden_down = [rank_part(3 * dl + c * hl, hl) for c in range(3)]
-    down_pad = -set_cols % 128
-    second_weight = jnp.zeros((width, hidden_width + set_cols + down_pad), bf16)
-    second_weight = lax.dynamic_update_slice(second_weight, wide_parts[2], (0, hidden_width))
     expert_ids = own + experts_local * jnp.arange(groups, dtype=jnp.int32)
     set_start = (plane // experts_local) * experts_local
     step_plane = lax.rem(own - jnp.arange(experts_local) + experts_local, experts_local)
@@ -1212,8 +1264,62 @@
     mask_slot = dot("gst,gtr->gsr", own_pick, rank_mask).reshape(slot_total, set_cols)
 
     gate_up_flat = w_gate_up.reshape(experts_local, dl, 2 * hidden_width)
-    attn_weight, slot_key, column_key, mask_slot, gate_up_flat = lax.optimization_barrier(
-        (attn_weight, slot_key, column_key, mask_slot, gate_up_flat)
+    names = 2 * router.shape[1]
+    down_pad = -set_cols % 128
+    own_id = column * experts_local + own
+    is_own = (jnp.arange(names, dtype=jnp.int32) % router.shape[1] == own_id).astype(f32)
+    is_own = jnp.pad(is_own, (0, 128 - names)).reshape(1, 128)
+    two_masks = jnp.concatenate([mask_slot, mask_slot], axis=1)
+    down_mask = jnp.pad(mask_slot, ((0, 0), (0, down_pad)))
+    router_twice = jnp.pad(
+        jnp.concatenate([router, router], axis=1), ((0, 0), (0, 128 - names))
+    )
+    (
+        attn_weight,
+        slot_key,
+        column_key,
+        two_masks,
+        down_mask,
+        is_own,
+        router_twice,
+        gate_up_flat,
+        rank_shard,
+    ) = lax.optimization_barrier(
+        (
+            attn_weight,
+            slot_key,
+            column_key,
+            two_masks,
+            down_mask,
+            is_own,
+            router_twice,
+            gate_up_flat,
+            rank_shard,
+        )
+    )
+    rank_sent = lax.all_to_all(rank_shard, "gx", 0, 0, tiled=True)
+
+    (down_later,) = after(rank_sent, w_down)
+    early_rows = dl * 5 // 8
+    early_pieces = own_pieces(
+        lambda p: lax.dynamic_slice(
+            down_later, (lax.rem(p, experts_local), 0, 0), (1, early_rows, hidden_width)
+        )[0]
+    )
+    rank_weight = unfolded(rank_sent)
+
+    def rank_part(start, count):
+        return rank_weight[:, start : start + count].reshape(planes * count, set_cols)
+
+    wide_parts = [rank_part(c * dl, dl) for c in range(3)]
+    hidden_gate, hidden_up, hidden_down = [rank_part(3 * dl + c * hl, hl) for c in range(3)]
+    no_rank = jnp.zeros((hidden_width, set_cols), bf16)
+    rank_operands = (
+        jnp.concatenate([wide_parts[0], wide_parts[1], router_twice], axis=1),
+        jnp.pad(wide_parts[2], ((0, 0), (0, down_pad))),
+        jnp.concatenate([hidden_gate, no_rank], axis=1),
+        jnp.concatenate([no_rank, hidden_up], axis=1),
+        jnp.pad(hidden_down, ((0, 0), (0, down_pad))),
     )
 
     col_start = column * width_local
@@ -1230,6 +1336,7 @@
     square_sums = jnp.stack(
         [jnp.sum(query_pre * query_pre, axis=(1, 2)), jnp.sum(key_pre * key_pre, axis=(1, 2))]
     )
+    (square_sums,) = after(rank_sent, square_sums)
     square_sums = add_small(square_sums.reshape(-1, 128), groups, 2).reshape(2, rows)
     query_scale = lax.rsqrt(square_sums[0] / width + norm_eps)[:, None, None]
     key_scale = lax.rsqrt(square_sums[1] / width + norm_eps)[:, None, None]
@@ -1270,8 +1377,9 @@
         ],
         axis=1,
     )
-    branch_left, *early = after(
-        query_scale, branch_left, *[piece for _, piece in early_pieces]
+    branch_left, *rank_operands = lax.optimization_barrier((branch_left,) + rank_operands)
+    branch_left, *early = lax.optimization_barrier(
+        (branch_left,) + tuple(piece for _, piece in early_pieces)
     )
     branch, late_pieces = scatter_product(
         branch_left,
@@ -1282,39 +1390,21 @@
         early_rows,
         planes,
     )
-    for (source, _), piece in zip(early_pieces, early):
-        second_weight = lax.dynamic_update_slice(second_weight, piece, (source * dl, 0))
-    for p in range(planes):
-        second_weight = lax.dynamic_update_slice(
-            second_weight, late_pieces[p], (p * dl + early_rows, 0)
-        )
     middle = block_input.astype(f32) + branch
     middle_low = middle.astype(bf16)
 
-    slot_rows, first_weight = spread(
+    slot_rows, gate_up_weight = spread(
         jnp.concatenate([middle_low, out_grad], axis=1),
         slot_key,
         gate_up_flat,
         planes,
         groups,
-        2 * hidden_width + 2 * set_cols + 128,
+        2 * hidden_width,
         4,
-    )
-    names = 2 * router.shape[1]
-    first_weight = lax.dynamic_update_slice(
-        first_weight,
-        jnp.pad(
-            jnp.concatenate([wide_parts[0], wide_parts[1], router, router], axis=1),
-            ((0, 0), (0, 128 - names)),
-        ),
-        (0, 2 * hidden_width),
     )
     both_rows = lax.all_gather(
         jnp.concatenate([middle_low, out_grad], axis=0), "gy", axis=1, tiled=True
     )
-    no_rank = jnp.zeros((hidden_width, set_cols), bf16)
-    own_id = column * experts_local + own
-    is_own = (jnp.arange(names, dtype=jnp.int32) % router.shape[1] == own_id).astype(f32)
     (
         normed_two_part,
         normed_two_rows,
@@ -1326,14 +1416,14 @@
         down_rank_grad,
     ) = experts(
         slot_rows,
-        first_weight,
-        second_weight,
-        jnp.concatenate([hidden_gate, no_rank], axis=1),
-        jnp.concatenate([no_rank, hidden_up], axis=1),
-        jnp.pad(hidden_down, ((0, 0), (0, down_pad))),
-        jnp.concatenate([mask_slot, mask_slot], axis=1),
-        jnp.pad(mask_slot, ((0, 0), (0, down_pad))),
-        jnp.pad(is_own, (0, 128 - names)).reshape(1, 128),
+        gate_up_weight,
+        rank_operands[0],
+        early,
+        late_pieces,
+        *rank_operands[1:],
+        two_masks,
+        down_mask,
+        is_own,
         mlp_gain.reshape(1, width),
         column_key,
         names,
@@ -1405,20 +1495,23 @@
     def rank_terms(values, which):
         return dot("the,hre->rt", values.astype(bf16), pack_pick[:, which])
 
+    pad_rows = -6 * compact % 32 or 32
     sums = jnp.concatenate(
         [
-            rank_terms(query_hat_grad, 0),
-            rank_terms(key_hat_grad, 1),
-            rank_terms(value_pre_grad, 2),
-            rank_terms(query_hat, 0),
-            rank_terms(key_hat, 1),
-            jnp.sum(rank_out_low.astype(f32), axis=1).T,
-            jnp.stack([stat_query, stat_key]),
+            piece.astype(bf16)
+            for piece in (
+                rank_terms(query_hat_grad, 0),
+                rank_terms(key_hat_grad, 1),
+                rank_terms(value_pre_grad, 2),
+                rank_terms(query_hat, 0),
+                rank_terms(key_hat, 1),
+                jnp.sum(rank_out_low.astype(f32), axis=1).T,
+                jnp.pad(jnp.stack([stat_query, stat_key]), ((0, pad_rows - 2), (0, 0))),
+            )
         ],
         axis=0,
     )
-    padding = -sums.shape[0] % 32
-    sums = add_pairs(jnp.pad(sums.astype(bf16), ((0, padding), (0, 0))), groups, 6)
+    sums = add_pairs(sums, groups, 6)
     first_total = sums[: 3 * compact].reshape(3, compact, rows)
     second_total = sums[3 * compact : 5 * compact].reshape(2, compact, rows)
     mean_qk = sums[6 * compact : 6 * compact + 2] / width

time: 855 us -> 838 us (0.980)
  local copies, waits for them, and re-layouts: 122 us -> 105 us
    all_to_all x1, waiting for transfers between devices: 0.01 us -> 18.9 us  [shards(): rank_sent = lax.all_to_all(rank_shard, 'gx', 0, 0, tiled=True)]
    ppermute x3, waiting for transfers between devices: 31.4 us -> 13.4 us  [own_pieces(): piece = lax.ppermute(piece, 'gx', pairs)]
    dynamic_update_slice x9 -> x0, local copies, waits for them, and re-layouts: 13.7 us -> none  [the longest x4 6.96 us: shards(): lax.dynamic_update_slice(second_weight, piece, (source * dl, 0))]
    unnamed x243 -> x214, local copies, waits for them, and re-layouts: 25.5 us -> 24.2 us
  transfers between devices with their start and end apart: 10 -> 10, of which waited for: 3 -> 2; matrix products, arithmetic and copies ran while one was open for 20% -> 20% of each run, Pallas kernels for 58% -> 59%
where the time goes in v4:
time: 838 us; the launch traced here: 827 us
  Pallas kernels  543 us (65%)
  local copies, waits for them, and re-layouts  105 us (13%)
  matrix products  57.8 us (7%)
  other arithmetic  54.3 us (6%)
  waiting for transfers between devices  32.3 us (4%)
  starting transfers between devices  17.9 us (2%)
  between operations  17 us (2%)
    pallas_call x1, Pallas kernels, spread(): pl.pallas_call(functools.partial(spread_kernel, planes, groups, in_set),...  244 us
    pallas_call x1, Pallas kernels, experts(): pl.pallas_call(functools.partial(experts_kernel, planes, groups, in_set,...  145 us
    pallas_call x2, Pallas kernels, scatter_product(): pl.pallas_call(body, out_shape=out_shape, in_specs=in_specs, out_specs=ou...  75.3 us
    dot_general x32, matrix products, dot(): return jnp.einsum(spec, left, right, preferred_element_type=f32)  56.5 us
    pallas_call x1, Pallas kernels, gather_normed(): pl.pallas_call(functools.partial(gather_kernel, chips, rows, 64), out_sha...  31 us
    unnamed x214, local copies, waits for them, and re-layouts  24.2 us
    pallas_call x2, Pallas kernels, gather_planes(): pl.pallas_call(functools.partial(planes_kernel, planes), out_shape=jax.Sh...  21.3 us
    all_to_all x1, waiting for transfers between devices, shards(): rank_sent = lax.all_to_all(rank_shard, 'gx', 0, 0, tiled=True)  18.9 us
  transfers between devices with their start and end apart: 10, of which 2 were waited for; matrix products, arithmetic and copies ran while one was open for 20% of the time, Pallas kernels for 59%

profile of v4, /device:TPU:0, one launch (start us, length us, event | category | flops | bytes accessed | tf_op | source)
XLA Modules:
  0.0 827.0 jit_solution(5722894156083047636)
XLA Ops:
  14.8 10.2 %shard_map.226 = s32[4,72,128]{2,1,0:T(8,128)} custom-call(s32[72,128]{1,0:T(8,128)} %copy-done.59), custom_call_target="tpu_custom_call" | custom-call | bytes 65536 | tf_op jit(solution)/shard_map/pallas_call | solution.py:1060
  34.3 14.5 %reshape.1212.w_ref = bf16[4,512,2048]{2,1,0:T(8,128)(2,1)} reshape(bf16[4,512,2,1024]{3,2,1,0:T(2,128)(2,1)} %param.32) | data formatting | bytes 16777216 | tf_op jit(solution)/shard_map/reshape | solution.py:1266
  55.9 31.0 %shard_map.225 = (bf16[1024,2048]{1,0:T(8,128)(2,1)S(1)}, f32[1024,128]{1,0:T(8,128)S(1)}, bf16[64,2048]{1,0:T(8,128)(2,1)S(1)}) custom-call(bf16[1088,256]{1,0:T(8,128)(2,1)S(1)} %pad_maximum_fusion.17.x_ref, f32[1,2048]{1,0:T(1,128)S(1)} %bitcast.409), custom_call_target="tpu_custom_call" | custom-call | bytes 65536 | tf_op jit(solution)/shard_map/pallas_call | solution.py:127
  107.0 4.5 all-to-all-start
  111.7 6.3 fusion.166
  122.4 18.9 %all-to-all-done = bf16[4,1152,128]{1,2,0:T(8,128)(2,1)} async-done(((bf16[4,1152,128]{1,2,0:T(8,128)(2,1)}), bf16[4,1152,128]{1,2,0:T(8,128)(2,1)}, u32[]{:S(2)}, u32[]{:S(2)}) %all-to-all-start) | async-done | bytes 1179680 | tf_op jit(solution)/shard_map/all_to_all | solution.py:1300
  141.9 6.0 shard_map.227
  157.0 3.4 fusion.26
  195.6 13.4 %collective-permute-done.1.rest_2_ = bf16[320,1024]{1,0:T(8,128)(2,1)} collective-permute-done((bf16[320,1024]{1,0:T(8,128)(2,1)}, bf16[320,1024]{1,0:T(8,128)(2,1)}, u32[]{:S(2)}, u32[]{:S(2)}) %collective-permute-start.1) | collective-permute-done | bytes 655392 | tf_op jit(solution)/shard_map/ppermute | solution.py:1166
  209.0 43.3 %shard_map.228 = (f32[1024,256]{1,0:T(8,128)S(1)}, bf16[4,192,1024]{2,1,0:T(8,128)(2,1)S(1)}) custom-call(bf16[1024,288]{1,0:T(8,128)(2,1)S(1)} %pad_maximum_fusion.15.l_ref, bf16[2048,288]{1,0:T(8,128)(2,1)S(1)} %pad_maximum_fusion.1.r_ref, bf16[4,512,1024]{2,1,0:T(8,128)(2,1)} %w_ref.1), custom_call_target="tpu_custom_call" | custom-call | bytes 65536 | tf_op jit(solution)/shard_map/pallas_call | solution.py:286
  258.9 3.8 slice.243.r_ref
  263.4 243.6 %shard_map.229 = (bf16[2,1152,2048]{2,1,0:T(8,128)(2,1)}, bf16[2048,2048]{1,0:T(8,128)(2,1)}) custom-call(bf16[1024,512]{1,0:T(8,128)(2,1)S(1)} %pad_maximum_fusion.11.x_ref, s32[4,8,1024]{2,1,0:T(8,128)S(1)} %get-tuple-element.58.key_ref, bf16[4,512,2048]{2,1,0:T(8,128)(2,1)} %reshape.1212.w_ref), custom_call_target="tpu_custom_call" | custom-call | bytes 65536 | tf_op jit(solution)/shard_map/pallas_call | solution.py:572
  507.0 145.1 %shard_map.230 = (f32[1024,256]{1,0:T(8,128)}, bf16[1024,2048]{1,0:T(8,128)(2,1)}, bf16[4,1024,256]{2,1,0:T(8,128)(2,1)}, f32[128,2048]{1,0:T(8,128)}, f32[128,2...) custom-call(bf16[2,1152,2048]{2,1,0:T(8,128)(2,1)} %get-tuple-element.60.slots_ref, ...), custom_call_target="tpu_custom_call" | custom-call | bytes 65536 | tf_op jit(solution)/shard_map/pallas_call | solution.py:983
  657.7 4.3 all-to-all-start.1
  664.6 3.8 collective-permute-start.3
  669.7 3.2 fusion.7
  673.1 4.1 fusion.2
  686.2 5.1 fusion.11
  691.3 5.7 multiply_reduce_fusion
  712.9 14.1 %shard_map.231 = f32[128,1024]{1,0:T(8,128)} custom-call(bf16[128,1024]{1,0:T(8,128)(2,1)} %fusion.117.x_ref), custom_call_target="tpu_custom_call" | custom-call | bytes 65536 | tf_op jit(solution)/shard_map/pallas_call | solution.py:379
  739.6 11.2 %shard_map.234 = bf16[4,16,2048]{2,1,0:T(8,128)(2,1)} custom-call(bf16[16,2048]{1,0:T(8,128)(2,1)} %pad_maximum_fusion.25.x_ref), custom_call_target="tpu_custom_call" | custom-call | bytes 65536 | tf_op jit(solution)/shard_map/pallas_call | solution.py:1060
  756.7 32.0 %shard_map.232 = f32[1024,256]{1,0:T(8,128)S(1)} custom-call(bf16[1024,768]{1,0:T(8,128)(2,1)S(1)} %copy.182.l_ref, bf16[2048,768]{1,0:T(8,128)(2,1)S(1)} %copy-done.1), custom_call_target="tpu_custom_call" | custom-call | bytes 65536 | tf_op jit(solution)/shard_map/pallas_call | solution.py:286
  799.9 6.3 shard_map.233
  816.6 3.2 fusion.60
  (396 shorter events, 173.3 us)
Async XLA Ops:
  7.2 110.8 %copy-start = (bf16[2,4,128,128]{3,2,1,0:T(8,128)(2,1)S(1)}, bf16[2,4,128,128]{3,2,1,0:T(8,128)(2,1)}, u32[]{:S(2)}) copy-start(bf16[2,4,128,128]{3,2,1,0:T(8,128)(2,1)} %param.30) | copy-start | bytes 786436
  7.2 99.8 %all-gather.3.cloned.1.call-start = ((), (), s32[]{:S(2)}) async-start(), calls=%async_computation.2 | async-start | bytes 5242880 | tf_op jit(solution)/shard_map/all_gather | solution.py:1206
  34.3 14.5 %copy-start.97 = (s32[1,2]{1,0:T(1,128)S(1)}, s32[1,2]{1,0:T(1,128)}, u32[]{:S(2)}) copy-start(s32[1,2]{1,0:T(1,128)} %param.22) | copy-start | bytes 28
  50.8 41.4 %copy-start.32 = (bf16[2048,32]{1,0:T(8,128)(2,1)S(1)}, bf16[2048,32]{1,0:T(8,128)(2,1)}, u32[]{:S(2)}) copy-start(bf16[2048,32]{1,0:T(8,128)(2,1)} %copy.146) | copy-start | bytes 393220
  52.6 48.3 %copy-start.71 = (s32[64]{0:T(128)}, s32[64]{0:T(128)S(1)}, u32[]{:S(2)}) copy-start(s32[64]{0:T(128)S(1)} %broadcast_in_dim.29) | copy-start | bytes 772
  55.9 40.8 %copy-start.54 = (bf16[4,256,3,128]{3,1,2,0:T(8,128)(2,1)S(1)}, bf16[4,256,3,128]{3,1,2,0:T(8,128)(2,1)}, u32[]{:S(2)}) copy-start(bf16[4,256,3,128]{3,1,2,0:T(8,128)(2,1)} %param.35) | copy-start | bytes 2359300
  89.3 16.6 %copy-start.22 = (bf16[64,2048]{0,1:T(8,128)(2,1)}, bf16[64,2048]{0,1:T(8,128)(2,1)S(1)}, u32[]{:S(2)}) copy-start(bf16[64,2048]{0,1:T(8,128)(2,1)S(1)} %copy.169) | copy-start | bytes 786436
  105.9 12.0 %copy-start.36 = (f32[1024,48]{0,1:T(8,128)}, f32[1024,48]{0,1:T(8,128)S(1)}, u32[]{:S(2)}) copy-start(f32[1024,48]{0,1:T(8,128)S(1)} %fusion.111) | copy-start | bytes 589828
  107.0 34.3 %all-to-all-start = ((bf16[4,1152,128]{1,2,0:T(8,128)(2,1)}), bf16[4,1152,128]{1,2,0:T(8,128)(2,1)}, u32[]{:S(2)}, u32[]{:S(2)}) async-start(bf16[4,1152,128]{1,2,0:T(8,128)(2,1)} %pad_maximum_fusion.8), calls=%async_computation | async-start | bytes 2359296 | tf_op jit(solution)/shard_map/all_to_all | solution.py:1300
  111.4 558.2 %all-gather.5.cloned.1.call-start = ((), (), s32[]{:S(2)}) async-start(), calls=%async_computation.3 | async-start | bytes 9437184 | tf_op jit(solution)/shard_map/all_gather | solution.py:1405
  162.1 33.5 %collective-permute-start = (bf16[320,1024]{1,0:T(8,128)(2,1)}, bf16[320,1024]{1,0:T(8,128)(2,1)}, u32[]{:S(2)}, u32[]{:S(2)}) collective-permute-start(bf16[320,1024]{1,0:T(8,128)(2,1)} %get-tuple-element.118), channel_id=1, source_target_pairs={{0,8},{8,16},{16,24},{24,0},{1,9},{9,17},{17,25},{25,1},{2,10},{10... | collective-permute-start | bytes 1966088 | tf_op jit(solution)/shard_map/ppermute | solution.py:1166
  162.1 46.9 %collective-permute-start.1 = (bf16[320,1024]{1,0:T(8,128)(2,1)}, bf16[320,1024]{1,0:T(8,128)(2,1)}, u32[]{:S(2)}, u32[]{:S(2)}) collective-permute-start(bf16[320,1024]{1,0:T(8,128)(2,1)} %get-tuple-element.117), channel_id=1, source_target_pairs={{0,16},{8,24},{16,0},{24,8},{1,17},{9,25},{17,1},{25,9},{2,18},{10... | collective-permute-start | bytes 1966088 | tf_op jit(solution)/shard_map/ppermute | solution.py:1166
  164.1 44.9 %collective-permute-start.2 = (bf16[320,1024]{1,0:T(8,128)(2,1)}, bf16[320,1024]{1,0:T(8,128)(2,1)}, u32[]{:S(2)}, u32[]{:S(2)}) collective-permute-start(bf16[320,1024]{1,0:T(8,128)(2,1)} %get-tuple-element.116), channel_id=1, source_target_pairs={{0,24},{8,0},{16,8},{24,16},{1,25},{9,1},{17,9},{25,17},{2,26},{10... | collective-permute-start | bytes 1966088 | tf_op jit(solution)/shard_map/ppermute | solution.py:1166
  177.6 15.5 %copy-start.31 = (bf16[2048,128]{1,0:T(8,128)(2,1)S(1)}, bf16[2048,128]{1,0:T(8,128)(2,1)}, u32[]{:S(2)}) copy-start(bf16[2048,128]{1,0:T(8,128)(2,1)} %fusion.87) | copy-start | bytes 1572868
  209.0 44.5 %copy-start.14 = (bf16[1024,256]{1,0:T(8,128)(2,1)S(1)}, bf16[1024,256]{1,0:T(8,128)(2,1)}, u32[]{:S(2)}) copy-start(bf16[1024,256]{1,0:T(8,128)(2,1)} %param.18) | copy-start | bytes 1572868
  209.0 44.6 %copy-start.19 = (bf16[1024,256]{1,0:T(8,128)(2,1)S(1)}, bf16[1024,256]{1,0:T(8,128)(2,1)}, u32[]{:S(2)}) copy-start(bf16[1024,256]{1,0:T(8,128)(2,1)} %param.19) | copy-start | bytes 1572868
  657.7 132.0 %all-to-all-start.1 = ((bf16[4,1152,128]{1,2,0:T(8,128)(2,1)}), bf16[4,1152,128]{1,2,0:T(8,128)(2,1)}, u32[]{:S(2)}, u32[]{:S(2)}) async-start(bf16[4,1152,128]{1,2,0:T(8,128)(2,1)} %fusion.29), calls=%async_computation.1 | async-start | bytes 2359296 | tf_op jit(solution)/shard_map/all_to_all | solution.py:1453
  664.6 125.1 %collective-permute-start.3 = (bf16[1024,256]{1,0:T(8,128)(2,1)}, bf16[1024,256]{1,0:T(8,128)(2,1)}, u32[]{:S(2)}, u32[]{:S(2)}) collective-permute-start(bf16[1024,256]{1,0:T(8,128)(2,1)} %get-tuple-element.126), channel_id=1, source_target_pairs={{0,24},{8,0},{16,8},{24,16},{1,25},{9,1},{17,9},{25,17},{2,26},{10... | collective-permute-start | bytes 1572872 | tf_op jit(solution)/shard_map/ppermute | solution.py:1158
  668.4 121.3 %collective-permute-start.4 = (bf16[1024,256]{1,0:T(8,128)(2,1)}, bf16[1024,256]{1,0:T(8,128)(2,1)}, u32[]{:S(2)}, u32[]{:S(2)}) collective-permute-start(bf16[1024,256]{1,0:T(8,128)(2,1)} %get-tuple-element.125), channel_id=1, source_target_pairs={{0,16},{8,24},{16,0},{24,8},{1,17},{9,25},{17,1},{25,9},{2,18},{10... | collective-permute-start | bytes 1572872 | tf_op jit(solution)/shard_map/ppermute | solution.py:1158
  668.4 121.3 %collective-permute-start.5 = (bf16[1024,256]{1,0:T(8,128)(2,1)}, bf16[1024,256]{1,0:T(8,128)(2,1)}, u32[]{:S(2)}, u32[]{:S(2)}) collective-permute-start(bf16[1024,256]{1,0:T(8,128)(2,1)} %get-tuple-element.124), channel_id=1, source_target_pairs={{0,8},{8,16},{16,24},{24,0},{1,9},{9,17},{17,25},{25,1},{2,10},{10... | collective-permute-start | bytes 1572872 | tf_op jit(solution)/shard_map/ppermute | solution.py:1158
  691.3 15.4 %copy-start.24 = (bf16[2,128,1024]{2,1,0:T(8,128)(2,1)}, bf16[2,128,1024]{2,1,0:T(8,128)(2,1)S(1)}, u32[]{:S(2)}) copy-start(bf16[2,128,1024]{2,1,0:T(8,128)(2,1)S(1)} %fusion.11) | copy-start | bytes 1572868
  735.8 15.0 %copy-start.95 = (s32[64]{0:T(128)S(1)}, s32[64]{0:T(128)}, u32[]{:S(2)}) copy-start(s32[64]{0:T(128)} %add.355) | copy-start | bytes 772
  794.0 12.3 %slice-start.3 = ((f32[128,2048]{1,0:T(8,128)}), f32[128,768]{1,0:T(8,128)S(1)}, s32[]{:S(2)}) async-start(f32[128,2048]{1,0:T(8,128)} %copy-done.28), calls=%async_computation.7 | async-start | bytes 786432 | tf_op jit(solution)/shard_map/slice | solution.py:1593
  795.3 11.9 %slice-start.4 = ((f32[128,2048]{1,0:T(8,128)}), f32[128,1024]{1,0:T(8,128)S(1)}, s32[]{:S(2)}) async-start(f32[128,2048]{1,0:T(8,128)} %copy-done.28), calls=%async_computation.8 | async-start | bytes 1048576 | tf_op jit(solution)/shard_map/slice | solution.py:1595
  (89 other events, 354.2 us)
Sparse Core Ops, SparseCore 0:
  12.2 83.4 all-gather.2
  254.9 60.8 all-gather.4

commit v5 on v4

--- a/solution.py
+++ b/solution.py
@@ -10,6 +10,7 @@
 SEQ = 1024
 PIECE = 256
 CAP = 288
+EARLY_PARTS = 2
 
 
 norm_eps = 1e-05
@@ -616,7 +617,7 @@
     key_ref,
     *rest,
 ):
-    early_refs = rest[:planes]
+    early_refs = rest[: planes * EARLY_PARTS]
     (
         shard_ref,
         rows_ref,
@@ -651,7 +652,7 @@
         c_recv,
         p_send,
         p_recv,
-    ) = rest[planes:]
+    ) = rest[planes * EARLY_PARTS :]
     plane, own, base = plane_place(in_set)
     me, chip, core, sibling = place_in_column()
     chips = groups // 2
@@ -791,31 +792,32 @@
             w1_sem.at[1],
         ),
     ]
-    early_rows, late_rows = early_refs[0].shape[0], late_ref.shape[1]
+    late_rows = late_ref.shape[1]
+    early_rows = sum(early_refs[planes * part].shape[0] for part in range(EARLY_PARTS))
     depth = early_rows + late_rows
     w2_loads = [
         pltpu.make_async_copy(
-            w2_tail_ref, w2_ref.at[:, pl.ds(hidden, w2_tail_ref.shape[1])], w2_sem.at[2 * planes]
+            w2_tail_ref, w2_ref.at[:, pl.ds(hidden, w2_tail_ref.shape[1])], w2_sem.at[0]
         )
     ]
+
+    def place_rows(piece_ref, start):
+        w2_loads.append(
+            pltpu.make_async_copy(
+                piece_ref,
+                w2_ref.at[pl.ds(pl.multiple_of(start, 16), piece_ref.shape[0]), pl.ds(0, hidden)],
+                w2_sem.at[len(w2_loads)],
+            )
+        )
+
     for number in range(planes):
         source = lax.rem(plane - number + planes, planes)
-        w2_loads.append(
-            pltpu.make_async_copy(
-                early_refs[number],
-                w2_ref.at[
-                    pl.ds(pl.multiple_of(source * depth, 16), early_rows), pl.ds(0, hidden)
-                ],
-                w2_sem.at[number],
-            )
-        )
-        w2_loads.append(
-            pltpu.make_async_copy(
-                late_ref.at[number],
-                w2_ref.at[pl.ds(number * depth + early_rows, late_rows), pl.ds(0, hidden)],
-                w2_sem.at[planes + number],
-            )
-        )
+        start = source * depth
+        for part in range(EARLY_PARTS):
+            piece_ref = early_refs[planes * part + number]
+            place_rows(piece_ref, start)
+            start = start + piece_ref.shape[0]
+        place_rows(late_ref.at[number], number * depth + early_rows)
     for copy in w1_loads + w2_loads:
         copy.start()
     greet_all(planes, groups)
@@ -992,7 +994,7 @@
             jax.ShapeDtypeStruct((rank, hidden), f32),
             jax.ShapeDtypeStruct((down, hidden), f32),
         ),
-        in_specs=[anywhere] * 5 + [VMEM] * 8 + [anywhere] * planes,
+        in_specs=[anywhere] * 5 + [VMEM] * 8 + [anywhere] * (planes * EARLY_PARTS),
         out_specs=(VMEM, anywhere) + (VMEM,) * 6,
         scratch_shapes=[
             pltpu.VMEM((full, w1_main.shape[1] + w1_tail.shape[1]), bf16),
@@ -1006,7 +1008,7 @@
             pltpu.VMEM((in_set - 1, rows, width), bf16),
             pltpu.VMEM((rows, width), bf16),
             DMA((2,)),
-            DMA((2 * planes + 1,)),
+            DMA(((EARLY_PARTS + 1) * planes + 1,)),
             DMA((2,)),
             DMA((in_set, groups)),
             DMA((in_set, groups)),
@@ -1282,7 +1284,6 @@
         down_mask,
         is_own,
         router_twice,
-        gate_up_flat,
         rank_shard,
     ) = lax.optimization_barrier(
         (
@@ -1293,19 +1294,26 @@
             down_mask,
             is_own,
             router_twice,
-            gate_up_flat,
             rank_shard,
         )
     )
     rank_sent = lax.all_to_all(rank_shard, "gx", 0, 0, tiled=True)
 
     (down_later,) = after(rank_sent, w_down)
-    early_rows = dl * 5 // 8
-    early_pieces = own_pieces(
-        lambda p: lax.dynamic_slice(
-            down_later, (lax.rem(p, experts_local), 0, 0), (1, early_rows, hidden_width)
-        )[0]
-    )
+    early_rows = 0
+    early_parts = []
+    for eighths in (2, 3):
+        count = dl * eighths // 8
+        pieces = own_pieces(
+            lambda p: lax.dynamic_slice(
+                down_later,
+                (lax.rem(p, experts_local), early_rows, 0),
+                (1, count, hidden_width),
+            )[0]
+        )
+        early_parts.append([piece for _, piece in pieces])
+        early_rows += count
+        (down_later,) = after(early_parts[-1][-1], w_down)
     rank_weight = unfolded(rank_sent)
 
     def rank_part(start, count):
@@ -1355,6 +1363,7 @@
     key_bf = apply_rotary(
         (key_hat * gains_local[1]).reshape(nseq, SEQ, heads_local, head_width), cosine, sine
     ).astype(bf16)
+    query_bf, *first_early = lax.optimization_barrier((query_bf, *early_parts[0]))
     values_seq = value_bf.reshape(nseq, SEQ, heads_local, head_width)
     allowed = allowed_mask(piece_starts)[:, None]
     scores = dot("nqhe,nkhe->nhqk", query_bf, key_bf) * inv_root
@@ -1377,10 +1386,11 @@
         ],
         axis=1,
     )
-    branch_left, *rank_operands = lax.optimization_barrier((branch_left,) + rank_operands)
-    branch_left, *early = lax.optimization_barrier(
-        (branch_left,) + tuple(piece for _, piece in early_pieces)
-    )
+    branch_left, qkv_weight, gate_up_flat, *rank_operands = lax.optimization_barrier(
+        (branch_left, attn_weight[:, :qkv_width], gate_up_flat) + rank_operands
+    )
+    branch_left, *second_early = lax.optimization_barrier((branch_left, *early_parts[1]))
+    early = first_early + second_early
     branch, late_pieces = scatter_product(
         branch_left,
         jnp.concatenate([out_weight] + [b_turned] * heads_local, axis=1),
@@ -1450,8 +1460,6 @@
         + [x.astype(bf16).T.reshape(planes, hl, set_cols) for x in hidden_grads],
         axis=1,
     )
-    rank_grads = lax.all_to_all(folded(rank_grads), "gx", 0, 0, tiled=True)
-
     middle_rows = both_rows[:rows].astype(f32)
     grad_rows = both_rows[rows:].astype(f32)
     scale_two = lax.rsqrt(jnp.mean(middle_rows * middle_rows, axis=-1, keepdims=True) + norm_eps)
@@ -1527,20 +1535,42 @@
     key_pre_grad = key_scale * (key_hat_grad - key_hat * mean_qk[1][:, None, None])
     pre_grad = jnp.stack([query_pre_grad, key_pre_grad, value_pre_grad], axis=2).astype(bf16)
     pack_b_grad = rank_scale * dot("tcr,thce->rhce", rank_low, pre_grad)
-    normed_one_grad = scatter_product(
-        pre_grad.reshape(rows, qkv_width), attn_weight[:, :qkv_width], groups, 7
-    )[0]
     adapter_input_gradient = dot("crt,cdr->td", rank_grad_bf, a_pick)
     first_normalized_shard = block_input.astype(f32) * scale_one
     normed_local_bf = lax.dynamic_slice_in_dim(normed_bf, col_start, width_local, axis=1)
     a_rows_grad = dot("td,crt->rcd", normed_local_bf, rank_grad_bf)
+    pack_grad = jnp.concatenate(
+        [
+            pack_b_grad.transpose(1, 2, 0, 3),
+            pack_out_grad[:, None],
+        ],
+        axis=1,
+    )
+    small = jnp.concatenate(
+        [
+            a_rows_grad.reshape(compact, 3 * width_local),
+            b_out_sum,
+            pack_grad.transpose(2, 0, 1, 3).reshape(compact, heads_local * 4 * head_width),
+        ],
+        axis=1,
+    )
+    small_rows = small.astype(bf16).reshape(-1, 128)
+    rank_grads = folded(rank_grads)
+    rank_row_count = rank_grads.shape[1]
+    carried = jnp.concatenate(
+        [rank_grads, jnp.broadcast_to(small_rows, (planes,) + small_rows.shape)], axis=1
+    )
+    normed_one_grad, came = scatter_product(
+        pre_grad.reshape(rows, qkv_width), qkv_weight, groups, 7, carried, 0, planes
+    )
     scaled_one = (normed_one_grad + adapter_input_gradient) * first_norm_gain
     stat_one = jnp.sum(scaled_one * first_normalized_shard, axis=-1)
     stat_one_sum = add_small(stat_one.reshape(-1, 128), groups, 8).reshape(rows, 1)
     input_grad = middle_grad + scale_one * (
         scaled_one - first_normalized_shard * stat_one_sum / width
     )
-    rank_grads, *moe_pieces = after(normed_one_grad, rank_grads, *moe_pieces)
+    moe_pieces = after(normed_one_grad, *moe_pieces)
+    rank_grads = came[:, :rank_row_count]
     moe_part = moe_planes[0].astype(f32)
     for piece in moe_pieces:
         moe_part = moe_part + piece.astype(f32)
@@ -1566,23 +1596,7 @@
         axis=2,
     )
 
-    pack_grad = jnp.concatenate(
-        [
-            pack_b_grad.transpose(1, 2, 0, 3),
-            pack_out_grad[:, None],
-        ],
-        axis=1,
-    )
-    small = jnp.concatenate(
-        [
-            a_rows_grad.reshape(compact, 3 * width_local),
-            b_out_sum,
-            pack_grad.transpose(2, 0, 1, 3).reshape(compact, heads_local * 4 * head_width),
-        ],
-        axis=1,
-    )
-    small_all = gather_planes(small.astype(bf16), planes, 9)
-    small_all = small_all.reshape(planes * compact, small.shape[1])
+    small_all = came[:, rank_row_count:].reshape(planes * compact, small.shape[1])
     row_at = (
         adapters_all[:, :, None] * RANK + jnp.arange(RANK, dtype=jnp.int32)[None, None, :]
     ).reshape(-1)

time: 838 us -> 829 us (0.989)
  Pallas kernels: 543 us -> 531 us
  local copies, waits for them, and re-layouts: 105 us -> 115 us
    pallas_call x2 -> x1, Pallas kernels: 21.3 us -> 10.2 us  [gather_planes(): pl.pallas_call(functools.partial(planes_kernel, planes), out_shape=jax.Sh...]
    transpose x0 -> x11, local copies, waits for them, and re-layouts: none -> 9.74 us  [the longest x6 5.56 us: shards(): x.astype(bf16).T.reshape(planes, hl, set_cols)]
    unnamed x214 -> x226, local copies, waits for them, and re-layouts: 24.2 us -> 26.8 us
  transfers between devices with their start and end apart: 10 -> 12, of which waited for: 2 -> 2; matrix products, arithmetic and copies ran while one was open for 20% -> 22% of each run, Pallas kernels for 59% -> 60%
where the time goes in v5:
time: 829 us; the launch traced here: 818 us
  Pallas kernels  531 us (64%)
  local copies, waits for them, and re-layouts  115 us (14%)
  other arithmetic  53.6 us (6%)
  matrix products  53.5 us (6%)
  waiting for transfers between devices  31.9 us (4%)
  between operations  16.9 us (2%)
  starting transfers between devices  15.6 us (2%)
    pallas_call x1, Pallas kernels, spread(): pl.pallas_call(functools.partial(spread_kernel, planes, groups, in_set),...  243 us
    pallas_call x1, Pallas kernels, experts(): pl.pallas_call(functools.partial(experts_kernel, planes, groups, in_set,...  145 us
    pallas_call x2, Pallas kernels, scatter_product(): pl.pallas_call(body, out_shape=out_shape, in_specs=in_specs, out_specs=ou...  74.9 us
    dot_general x32, matrix products, dot(): return jnp.einsum(spec, left, right, preferred_element_type=f32)  53.3 us
    pallas_call x1, Pallas kernels, gather_normed(): pl.pallas_call(functools.partial(gather_kernel, chips, rows, 64), out_sha...  31 us
    unnamed x226, local copies, waits for them, and re-layouts  26.8 us
    all_to_all x1, waiting for transfers between devices, shards(): rank_sent = lax.all_to_all(rank_shard, 'gx', 0, 0, tiled=True)  20.7 us
  transfers between devices with their start and end apart: 12, of which 2 were waited for; matrix products, arithmetic and copies ran while one was open for 22% of the time, Pallas kernels for 60%

profile of v5, /device:TPU:0, one launch (start us, length us, event | category | flops | bytes accessed | tf_op | source)
XLA Modules:
  0.0 817.6 jit_solution(4024546565930248190)
XLA Ops:
  14.8 10.2 %shard_map.226 = s32[4,72,128]{2,1,0:T(8,128)} custom-call(s32[72,128]{1,0:T(8,128)} %copy-done.64), custom_call_target="tpu_custom_call" | custom-call | bytes 65536 | tf_op jit(solution)/shard_map/pallas_call | solution.py:1062
  39.3 14.5 %reshape.1235.w_ref = bf16[4,512,2048]{2,1,0:T(8,128)(2,1)} reshape(bf16[4,512,2,1024]{3,2,1,0:T(2,128)(2,1)} %param.32) | data formatting | bytes 16777216 | tf_op jit(solution)/shard_map/reshape | solution.py:1268
  54.6 31.0 %shard_map.225 = (bf16[1024,2048]{1,0:T(8,128)(2,1)S(1)}, f32[1024,128]{1,0:T(8,128)S(1)}, bf16[64,2048]{1,0:T(8,128)(2,1)S(1)}) custom-call(bf16[1088,256]{1,0:T(8,128)(2,1)S(1)} %pad_maximum_fusion.16.x_ref, f32[1,2048]{1,0:T(1,128)S(1)} %bitcast.407), custom_call_target="tpu_custom_call" | custom-call | bytes 65536 | tf_op jit(solution)/shard_map/pallas_call | solution.py:128
  107.9 3.7 slice.249.r_ref
  111.6 4.5 all-to-all-start
  116.3 6.2 fusion.174
  125.3 20.7 %all-to-all-done = bf16[4,1152,128]{1,2,0:T(8,128)(2,1)} async-done(((bf16[4,1152,128]{1,2,0:T(8,128)(2,1)}), bf16[4,1152,128]{1,2,0:T(8,128)(2,1)}, u32[]{:S(2)}, u32[]{:S(2)}) %all-to-all-start) | async-done | bytes 1179680 | tf_op jit(solution)/shard_map/all_to_all | solution.py:1300
  146.6 6.0 shard_map.227
  195.4 2.9 collective-permute-start.5
  203.7 2.9 fusion.32
  212.0 11.1 %collective-permute-done.4.rest_6_ = bf16[192,1024]{1,0:T(8,128)(2,1)} collective-permute-done((bf16[192,1024]{1,0:T(8,128)(2,1)}, bf16[192,1024]{1,0:T(8,128)(2,1)}, u32[]{:S(2)}, u32[]{:S(2)}) %collective-permute-start.4) | collective-permute-done | bytes 393248 | tf_op jit(solution)/shard_map/ppermute | solution.py:1168
  223.1 38.4 %shard_map.228 = (f32[1024,256]{1,0:T(8,128)S(1)}, bf16[4,192,1024]{2,1,0:T(8,128)(2,1)S(1)}) custom-call(bf16[1024,288]{1,0:T(8,128)(2,1)S(1)} %pad_maximum_fusion.14.l_ref, bf16[2048,288]{1,0:T(8,128)(2,1)S(1)} %pad_maximum_fusion.1.r_ref, bf16[4,512,1024]{2,1,0:T(8,128)(2,1)} %w_ref.1), custom_call_target="tpu_custom_call" | custom-call | bytes 65536 | tf_op jit(solution)/shard_map/pallas_call | solution.py:287
  268.5 242.9 %shard_map.229 = (bf16[2,1152,2048]{2,1,0:T(8,128)(2,1)}, bf16[2048,2048]{1,0:T(8,128)(2,1)}) custom-call(bf16[1024,512]{1,0:T(8,128)(2,1)S(1)} %pad_maximum_fusion.10.x_ref, s32[4,8,1024]{2,1,0:T(8,128)S(1)} %get-tuple-element.68.key_ref, bf16[4,512,2048]{2,1,0:T(8,128)(2,1)} %reshape.1235.w_ref), custom_call_target="tpu_custom_call" | custom-call | bytes 65536 | tf_op jit(solution)/shard_map/pallas_call | solution.py:573
  511.4 145.3 %shard_map.230 = (f32[1024,256]{1,0:T(8,128)}, bf16[1024,2048]{1,0:T(8,128)(2,1)}, bf16[4,1024,256]{2,1,0:T(8,128)(2,1)}, f32[128,2048]{1,0:T(8,128)}, f32[128,2...) custom-call(bf16[2,1152,2048]{2,1,0:T(8,128)(2,1)} %get-tuple-element.70.slots_ref, ...), custom_call_target="tpu_custom_call" | custom-call | bytes 65536 | tf_op jit(solution)/shard_map/pallas_call | solution.py:985
  671.1 3.2 fusion.7
  674.5 4.2 fusion.2
  679.2 2.9 fusion.6
  686.1 5.1 fusion.11
  691.2 4.6 multiply_reduce_fusion
  696.2 2.7 multiply_convert_fusion
  709.0 14.3 %shard_map.231 = f32[128,1024]{1,0:T(8,128)} custom-call(bf16[128,1024]{1,0:T(8,128)(2,1)} %fusion.126.x_ref), custom_call_target="tpu_custom_call" | custom-call | bytes 65536 | tf_op jit(solution)/shard_map/pallas_call | solution.py:380
  736.6 36.6 %shard_map.232 = (f32[1024,256]{1,0:T(8,128)S(1)}, bf16[4,1408,128]{2,1,0:T(8,128)(2,1)S(1)}) custom-call(bf16[1024,768]{1,0:T(8,128)(2,1)S(1)} %copy.200.l_ref, bf16[2048,768]{1,0:T(8,128)(2,1)} %slice.249.r_ref, bf16[4,1408,128]{2,1,0:T(8,128)(2,1)S(1)} %fusion.26.w_ref), custom_call_target="tpu_custom_call" | custom-call | bytes 65536 | tf_op jit(solution)/shard_map/pallas_call | solution.py:287
  782.3 6.4 shard_map.233
  807.1 3.2 fusion.65
  (415 shorter events, 177.2 us)
Async XLA Ops:
  7.2 115.4 %copy-start = (bf16[2,4,128,128]{3,2,1,0:T(8,128)(2,1)S(1)}, bf16[2,4,128,128]{3,2,1,0:T(8,128)(2,1)}, u32[]{:S(2)}) copy-start(bf16[2,4,128,128]{3,2,1,0:T(8,128)(2,1)} %param.30) | copy-start | bytes 786436
  7.2 100.7 %all-gather.3.cloned.1.call-start = ((), (), s32[]{:S(2)}) async-start(), calls=%async_computation.1 | async-start | bytes 5242880 | tf_op jit(solution)/shard_map/all_gather | solution.py:1208
  36.7 65.1 %copy-start.76 = (s32[64]{0:T(128)}, s32[64]{0:T(128)S(1)}, u32[]{:S(2)}) copy-start(s32[64]{0:T(128)S(1)} %broadcast_in_dim.31) | copy-start | bytes 772
  88.0 18.9 %copy-start.28 = (bf16[64,2048]{0,1:T(8,128)(2,1)}, bf16[64,2048]{0,1:T(8,128)(2,1)S(1)}, u32[]{:S(2)}) copy-start(bf16[64,2048]{0,1:T(8,128)(2,1)S(1)} %copy.177) | copy-start | bytes 786436
  90.2 32.3 %copy-start.60 = (f32[1024,16]{0,1:T(8,128)}, f32[1024,16]{0,1:T(8,128)S(1)}, u32[]{:S(2)}) copy-start(f32[1024,16]{0,1:T(8,128)S(1)} %compare_convert_fusion) | copy-start | bytes 196612
  106.9 15.7 %copy-start.48 = (f32[1024,48]{0,1:T(8,128)}, f32[1024,48]{0,1:T(8,128)S(1)}, u32[]{:S(2)}) copy-start(f32[1024,48]{0,1:T(8,128)S(1)} %fusion.117) | copy-start | bytes 589828
  111.6 34.4 %all-to-all-start = ((bf16[4,1152,128]{1,2,0:T(8,128)(2,1)}), bf16[4,1152,128]{1,2,0:T(8,128)(2,1)}, u32[]{:S(2)}, u32[]{:S(2)}) async-start(bf16[4,1152,128]{1,2,0:T(8,128)(2,1)} %pad_maximum_fusion.7), calls=%async_computation | async-start | bytes 2359296 | tf_op jit(solution)/shard_map/all_to_all | solution.py:1300
  116.1 555.0 %all-gather.5.cloned.1.call-start = ((), (), s32[]{:S(2)}) async-start(), calls=%async_computation.2 | async-start | bytes 9437184 | tf_op jit(solution)/shard_map/all_gather | solution.py:1415
  123.5 36.5 %copy-start.83 = (f32[1,256]{1,0:T(1,128)S(1)}, f32[1,256]{1,0:T(1,128)}, u32[]{:S(2)}) copy-start(f32[1,256]{1,0:T(1,128)} %get-tuple-element.179) | copy-start | bytes 3076
  123.5 36.5 %copy-start.85 = (f32[1,256]{1,0:T(1,128)S(1)}, f32[1,256]{1,0:T(1,128)}, u32[]{:S(2)}) copy-start(f32[1,256]{1,0:T(1,128)} %get-tuple-element.178) | copy-start | bytes 3076
  156.2 34.6 %collective-permute-start = (bf16[128,1024]{1,0:T(8,128)(2,1)}, bf16[128,1024]{1,0:T(8,128)(2,1)}, u32[]{:S(2)}, u32[]{:S(2)}) collective-permute-start(bf16[128,1024]{1,0:T(8,128)(2,1)} %get-tuple-element.138), channel_id=1, source_target_pairs={{0,8},{8,16},{16,24},{24,0},{1,9},{9,17},{17,25},{25,1},{2,10},{10... | collective-permute-start | bytes 786440 | tf_op jit(solution)/shard_map/ppermute | solution.py:1168
  156.2 34.6 %collective-permute-start.1 = (bf16[128,1024]{1,0:T(8,128)(2,1)}, bf16[128,1024]{1,0:T(8,128)(2,1)}, u32[]{:S(2)}, u32[]{:S(2)}) collective-permute-start(bf16[128,1024]{1,0:T(8,128)(2,1)} %get-tuple-element.137), channel_id=1, source_target_pairs={{0,16},{8,24},{16,0},{24,8},{1,17},{9,25},{17,1},{25,9},{2,18},{10... | collective-permute-start | bytes 786440 | tf_op jit(solution)/shard_map/ppermute | solution.py:1168
  158.2 32.6 %collective-permute-start.2 = (bf16[128,1024]{1,0:T(8,128)(2,1)}, bf16[128,1024]{1,0:T(8,128)(2,1)}, u32[]{:S(2)}, u32[]{:S(2)}) collective-permute-start(bf16[128,1024]{1,0:T(8,128)(2,1)} %get-tuple-element.136), channel_id=1, source_target_pairs={{0,24},{8,0},{16,8},{24,16},{1,25},{9,1},{17,9},{25,17},{2,26},{10... | collective-permute-start | bytes 786440 | tf_op jit(solution)/shard_map/ppermute | solution.py:1168
  169.6 18.5 %copy-start.41 = (bf16[2048,128]{1,0:T(8,128)(2,1)S(1)}, bf16[2048,128]{1,0:T(8,128)(2,1)}, u32[]{:S(2)}) copy-start(bf16[2048,128]{1,0:T(8,128)(2,1)} %fusion.92) | copy-start | bytes 1572868
  193.3 18.7 %collective-permute-start.3 = (bf16[192,1024]{1,0:T(8,128)(2,1)}, bf16[192,1024]{1,0:T(8,128)(2,1)}, u32[]{:S(2)}, u32[]{:S(2)}) collective-permute-start(bf16[192,1024]{1,0:T(8,128)(2,1)} %get-tuple-element.134), channel_id=1, source_target_pairs={{0,8},{8,16},{16,24},{24,0},{1,9},{9,17},{17,25},{25,1},{2,10},{10... | collective-permute-start | bytes 1179656 | tf_op jit(solution)/shard_map/ppermute | solution.py:1168
  193.9 29.2 %collective-permute-start.4 = (bf16[192,1024]{1,0:T(8,128)(2,1)}, bf16[192,1024]{1,0:T(8,128)(2,1)}, u32[]{:S(2)}, u32[]{:S(2)}) collective-permute-start(bf16[192,1024]{1,0:T(8,128)(2,1)} %get-tuple-element.133), channel_id=1, source_target_pairs={{0,16},{8,24},{16,0},{24,8},{1,17},{9,25},{17,1},{25,9},{2,18},{10... | collective-permute-start | bytes 1179656 | tf_op jit(solution)/shard_map/ppermute | solution.py:1168
  195.4 27.7 %collective-permute-start.5 = (bf16[192,1024]{1,0:T(8,128)(2,1)}, bf16[192,1024]{1,0:T(8,128)(2,1)}, u32[]{:S(2)}, u32[]{:S(2)}) collective-permute-start(bf16[192,1024]{1,0:T(8,128)(2,1)} %get-tuple-element.132), channel_id=1, source_target_pairs={{0,24},{8,0},{16,8},{24,16},{1,25},{9,1},{17,9},{25,17},{2,26},{10... | collective-permute-start | bytes 1179656 | tf_op jit(solution)/shard_map/ppermute | solution.py:1168
  206.6 54.8 %copy-start.23 = (bf16[2,128,1024]{2,1,0:T(8,128)(2,1)}, bf16[2,128,1024]{2,1,0:T(8,128)(2,1)S(1)}, u32[]{:S(2)}) copy-start(bf16[2,128,1024]{2,1,0:T(8,128)(2,1)S(1)} %fusion.32) | copy-start | bytes 1572868
  223.1 39.9 %copy-start.25 = (bf16[1024,256]{1,0:T(8,128)(2,1)S(1)}, bf16[1024,256]{1,0:T(8,128)(2,1)}, u32[]{:S(2)}) copy-start(bf16[1024,256]{1,0:T(8,128)(2,1)} %param.19) | copy-start | bytes 1572868
  262.9 248.5 %copy-start.21 = (bf16[1024,256]{1,0:T(8,128)(2,1)}, bf16[1024,256]{1,0:T(8,128)(2,1)S(1)}, u32[]{:S(2)}) copy-start(bf16[1024,256]{1,0:T(8,128)(2,1)S(1)} %fusion.85) | copy-start | bytes 1572868
  669.0 127.0 %collective-permute-start.6 = (bf16[1024,256]{1,0:T(8,128)(2,1)}, bf16[1024,256]{1,0:T(8,128)(2,1)}, u32[]{:S(2)}, u32[]{:S(2)}) collective-permute-start(bf16[1024,256]{1,0:T(8,128)(2,1)} %get-tuple-element.146), channel_id=1, source_target_pairs={{0,24},{8,0},{16,8},{24,16},{1,25},{9,1},{17,9},{25,17},{2,26},{10... | collective-permute-start | bytes 1572872 | tf_op jit(solution)/shard_map/ppermute | solution.py:1160
  669.0 127.0 %collective-permute-start.7 = (bf16[1024,256]{1,0:T(8,128)(2,1)}, bf16[1024,256]{1,0:T(8,128)(2,1)}, u32[]{:S(2)}, u32[]{:S(2)}) collective-permute-start(bf16[1024,256]{1,0:T(8,128)(2,1)} %get-tuple-element.145), channel_id=1, source_target_pairs={{0,16},{8,24},{16,0},{24,8},{1,17},{9,25},{17,1},{25,9},{2,18},{10... | collective-permute-start | bytes 1572872 | tf_op jit(solution)/shard_map/ppermute | solution.py:1160
  669.1 126.9 %collective-permute-start.8 = (bf16[1024,256]{1,0:T(8,128)(2,1)}, bf16[1024,256]{1,0:T(8,128)(2,1)}, u32[]{:S(2)}, u32[]{:S(2)}) collective-permute-start(bf16[1024,256]{1,0:T(8,128)(2,1)} %get-tuple-element.144), channel_id=1, source_target_pairs={{0,8},{8,16},{16,24},{24,0},{1,9},{9,17},{17,25},{25,1},{2,10},{10... | collective-permute-start | bytes 1572872 | tf_op jit(solution)/shard_map/ppermute | solution.py:1160
  736.6 37.7 %copy-start.101 = (s32[64]{0:T(128)S(1)}, s32[64]{0:T(128)}, u32[]{:S(2)}) copy-start(s32[64]{0:T(128)} %add.362) | copy-start | bytes 772
  (95 other events, 431.1 us)
Sparse Core Ops, SparseCore 0:
  12.2 83.4 all-gather.2
  264.2 60.7 all-gather.4
